TPU v7x, 32 devices: a whole 2x2x4 slice. The times are simulated.
32 devices in a mesh: replica: 2 (over x), shard: 16 (over z, y, core).
Axes of the slice: x: 2, y: 2, z: 4, core: 2. Of those that a mesh axis runs over, the one named last changes fastest.
Arguments:
- tokens: bfloat16 [4096, 2048], P(('replica', 'shard')), may hold values from -6 to 6
- segments: int32 [32, 128], P(('replica', 'shard')), may hold values from 0 to 7, never falling along the last dimension, each value on 1 to 64 neighbouring positions
- ln_gain: bfloat16 [2048], P('shard'), may hold values from 0.5 to 1.5
- ln_bias: bfloat16 [2048], P('shard'), may hold values from -3 to 3
- w_qkv: bfloat16 [2048, 6144], P('shard'), may hold values from -0.125 to 0.125
- b_qkv: bfloat16 [6144], P('shard'), may hold values from -3 to 3
- w_out: bfloat16 [2048, 2048], P('shard'), may hold values from -0.5 to 0.5
- w_gateup: bfloat16 [2048, 11264], P('shard'), may hold values from -0.125 to 0.125
- w_down: bfloat16 [5632, 2048], P('shard'), may hold values from -0.078125 to 0.078125
- cotangent: bfloat16 [4096, 2048], P(('replica', 'shard')), may hold values from -6 to 6
Outputs:
- block_output: bfloat16 [4096, 2048], P(('replica', 'shard'))
- tokens_grad: bfloat16 [4096, 2048], P(('replica', 'shard'))
- gain_grad: float32 [2048], P('shard')
- bias_grad: float32 [2048], P('shard')
- qkv_grad: float32 [2048, 6144], P('shard')
- qkv_bias_grad: float32 [6144], P('shard')
- out_grad: float32 [2048, 2048], P('shard')
- gateup_grad: float32 [2048, 11264], P('shard')
- down_grad: float32 [5632, 2048], P('shard')
Inputs may be any that keep to these rules, and one draw needn't show every extreme that they name: `segments`: within each sequence of 128 tokens the numbers start at 0 and never fall; each of the 8 documents holds 1 to 64 tokens, and one holds exactly 64.
All inputs are finite; a program needn't handle non-finite values.
Results may differ from a plain program's by a relative error of at most 0.0085.
Values may be sent and summed in bfloat16 or wider, within the bound.
No kernel may reach another device: no remote copies, remote signals or barrier semaphores. Data moves between devices by JAX's collectives and lax.ppermute only.
A program may use at most 512 MiB of HBM per device.

v0:
```python
import math

import jax
import jax.numpy as jnp
from jax import lax
from jax.sharding import PartitionSpec as P

HEADS = 32
HEAD_DIM = 64
ROT = 16


epsilon = 1e-05
rope_base = 10000.0


def rotary_tables(segment_row):
    length = segment_row.shape[0]
    indices = jnp.arange(length, dtype=jnp.int32)
    same_doc = segment_row[:, None] == segment_row[None, :]
    doc_start = jnp.min(jnp.where(same_doc, indices[None, :], length), axis=1)
    in_doc = (indices - doc_start).astype(jnp.float32)
    half_rot = ROT // 2
    inverse = rope_base ** (-(jnp.arange(half_rot, dtype=jnp.float32) * (2.0 / ROT)))
    angles = in_doc[:, None] * inverse[None, :]
    return (jnp.cos(angles)[:, None, :], jnp.sin(angles)[:, None, :])


def rotate(tensor, cos_table, sin_table):
    half_rot = cos_table.shape[-1]
    leading = tensor[..., :half_rot]
    trailing = tensor[..., half_rot : 2 * half_rot]
    return jnp.concatenate(
        [
            leading * cos_table - trailing * sin_table,
            trailing * cos_table + leading * sin_table,
            tensor[..., 2 * half_rot :],
        ],
        axis=-1,
    )


def unrotate(gradient, cos_table, sin_table):
    half_rot = cos_table.shape[-1]
    leading = gradient[..., :half_rot]
    trailing = gradient[..., half_rot : 2 * half_rot]
    return jnp.concatenate(
        [
            leading * cos_table + trailing * sin_table,
            trailing * cos_table - leading * sin_table,
            gradient[..., 2 * half_rot :],
        ],
        axis=-1,
    )


def per_device(
    tokens, segments, ln_gain, ln_bias, w_qkv, b_qkv, w_out, w_gateup, w_down, cotangent
):
    shards = (ln_gain, ln_bias, w_qkv, b_qkv, w_out, w_gateup, w_down)
    gathered = (
        lax.all_gather(shards[0], "shard", axis=0, tiled=True),
        lax.all_gather(shards[1], "shard", axis=0, tiled=True),
        lax.all_gather(shards[2], "shard", axis=0, tiled=True),
        lax.all_gather(shards[3], "shard", axis=0, tiled=True),
        lax.all_gather(shards[4], "shard", axis=0, tiled=True),
        lax.all_gather(shards[5], "shard", axis=0, tiled=True),
        lax.all_gather(shards[6], "shard", axis=0, tiled=True),
    )
    gain_all, bias_all, qkv_all, qkv_bias_all, out_all, gateup_all, down_all = gathered
    length, model_width = tokens.shape
    ffn_width = gateup_all.shape[1] // 2
    score_scale = 1.0 / math.sqrt(HEAD_DIM)
    segment_row = segments[0]
    cos_table, sin_table = rotary_tables(segment_row)
    tokens32 = tokens.astype(jnp.float32)
    centered = tokens32 - jnp.mean(tokens32, axis=1, keepdims=True)
    inv_std = lax.rsqrt(jnp.mean(centered * centered, axis=1, keepdims=True) + epsilon)
    normal_part = centered * inv_std
    normed = (normal_part * gain_all.astype(jnp.float32) + bias_all.astype(jnp.float32)).astype(
        jnp.bfloat16
    )
    joined_proj = jnp.dot(
        normed, qkv_all, preferred_element_type=jnp.float32
    ) + qkv_bias_all.astype(jnp.float32)
    head_shape = (length, HEADS, HEAD_DIM)
    query_heads = rotate(
        joined_proj[:, :model_width].reshape(head_shape), cos_table, sin_table
    ).astype(jnp.bfloat16)
    key_heads = rotate(
        joined_proj[:, model_width : 2 * model_width].reshape(head_shape), cos_table, sin_table
    ).astype(jnp.bfloat16)
    value_heads = joined_proj[:, 2 * model_width :].reshape(head_shape).astype(jnp.bfloat16)
    block_rows = min(length, 512)
    block_count = length // block_rows
    key_index = jnp.arange(length, dtype=jnp.int32)

    def masked_scores(block_index):
        row_start = block_index * block_rows
        scores = (
            jnp.einsum("qhd,khd->hqk", query_heads, key_heads, preferred_element_type=jnp.float32)
            * score_scale
        )
        rows_here = row_start + jnp.arange(block_rows, dtype=jnp.int32)
        allowed = (segment_row[:, None] == segment_row[None, :]) & (
            rows_here[:, None] >= key_index[None, :]
        )
        return (jnp.where(allowed[None], scores, -1e30), query_heads)

    def attend(block_index):
        scores, query_blk = masked_scores(block_index)
        row_max = jnp.max(scores, axis=2, keepdims=True)
        exp_scores = jnp.exp(scores - row_max)
        row_total = jnp.sum(exp_scores, axis=2, keepdims=True)
        attn_probs = (exp_scores / row_total).astype(jnp.bfloat16)
        context = jnp.einsum(
            "hqk,khd->qhd", attn_probs, value_heads, preferred_element_type=jnp.float32
        )
        return (context.astype(jnp.bfloat16), (row_max + jnp.log(row_total))[:, :, 0])

    contexts, log_totals = lax.map(attend, jnp.arange(block_count))
    context_all = contexts.reshape(length, model_width)
    attn_branch = jnp.dot(context_all, out_all, preferred_element_type=jnp.float32)
    gateup = jnp.dot(normed, gateup_all, preferred_element_type=jnp.float32)
    gate_part = gateup[:, :ffn_width]
    up_part = gateup[:, ffn_width:]
    sigmoid_gate = jax.nn.sigmoid(gate_part)
    hidden = (gate_part * sigmoid_gate * up_part).astype(jnp.bfloat16)
    ffn_branch = jnp.dot(hidden, down_all, preferred_element_type=jnp.float32)
    block_output = (tokens32 + attn_branch + ffn_branch).astype(jnp.bfloat16)
    regathered = (
        lax.all_gather(shards[0], "shard", axis=0, tiled=True),
        lax.all_gather(shards[1], "shard", axis=0, tiled=True),
        lax.all_gather(shards[2], "shard", axis=0, tiled=True),
        lax.all_gather(shards[3], "shard", axis=0, tiled=True),
        lax.all_gather(shards[4], "shard", axis=0, tiled=True),
        lax.all_gather(shards[5], "shard", axis=0, tiled=True),
        lax.all_gather(shards[6], "shard", axis=0, tiled=True),
    )
    gain_all = regathered[0]
    qkv_all = regathered[2]
    out_all = regathered[4]
    gateup_all = regathered[5]
    down_all = regathered[6]
    down_grad = jnp.einsum("sf,sd->fd", hidden, cotangent, preferred_element_type=jnp.float32)
    dhidden = jnp.einsum("sd,fd->sf", cotangent, down_all, preferred_element_type=jnp.float32)
    gate_grad = dhidden * up_part * sigmoid_gate * (1.0 + gate_part * (1.0 - sigmoid_gate))
    up_grad = dhidden * gate_part * sigmoid_gate
    dgateup = jnp.concatenate([gate_grad, up_grad], axis=1).astype(jnp.bfloat16)
    gateup_grad = jnp.einsum("sd,sf->df", normed, dgateup, preferred_element_type=jnp.float32)
    dnormed = jnp.einsum("sf,df->sd", dgateup, gateup_all, preferred_element_type=jnp.float32)
    out_grad = jnp.einsum("sd,se->de", context_all, cotangent, preferred_element_type=jnp.float32)
    dcontext = jnp.einsum(
        "se,de->sd", cotangent, out_all, preferred_element_type=jnp.float32
    ).astype(jnp.bfloat16)
    dcontext_heads = dcontext.reshape(head_shape)

    def back_step(carry, block_index):
        key_grad, value_grad = carry
        scores, query_blk = masked_scores(block_index)
        attn_probs = jnp.exp(scores - log_totals[block_index][:, :, None])
        prob_grad = jnp.einsum(
            "qhd,khd->hqk", dcontext_heads, value_heads, preferred_element_type=jnp.float32
        )
        score_grad = (
            attn_probs * (prob_grad - jnp.sum(prob_grad * attn_probs, axis=2, keepdims=True))
        ).astype(jnp.bfloat16)
        value_grad = value_grad + jnp.einsum(
            "hqk,qhd->khd",
            attn_probs.astype(jnp.bfloat16),
            dcontext_heads,
            preferred_element_type=jnp.float32,
        )
        key_grad = (
            key_grad
            + jnp.einsum("hqk,qhd->khd", score_grad, query_blk, preferred_element_type=jnp.float32)
            * score_scale
        )
        query_grad = (
            jnp.einsum("hqk,khd->qhd", score_grad, key_heads, preferred_element_type=jnp.float32)
            * score_scale
        )
        return ((key_grad, value_grad), query_grad)

    zeros_heads = jnp.zeros(head_shape, jnp.float32)
    (key_grads, value_grads), query_grads = lax.scan(
        back_step, (zeros_heads, zeros_heads), jnp.arange(block_count)
    )
    query_back = unrotate(query_grads.reshape(head_shape), cos_table, sin_table)
    key_back = unrotate(key_grads, cos_table, sin_table)
    dfused = jnp.concatenate(
        [
            query_back.reshape(length, model_width),
            key_back.reshape(length, model_width),
            value_grads.reshape(length, model_width),
        ],
        axis=1,
    ).astype(jnp.bfloat16)
    qkv_grad = jnp.einsum("sd,se->de", normed, dfused, preferred_element_type=jnp.float32)
    qkv_bias_grad = jnp.sum(dfused.astype(jnp.float32), axis=0)
    dnormed = dnormed + jnp.einsum("se,de->sd", dfused, qkv_all, preferred_element_type=jnp.float32)
    gain_grad = jnp.sum(dnormed * normal_part, axis=0)
    bias_grad = jnp.sum(dnormed, axis=0)
    scaled_grad = dnormed * gain_all.astype(jnp.float32)
    tokens_back = inv_std * (
        scaled_grad
        - jnp.mean(scaled_grad, axis=1, keepdims=True)
        - normal_part * jnp.mean(scaled_grad * normal_part, axis=1, keepdims=True)
    )
    tokens_grad = (cotangent.astype(jnp.float32) + tokens_back).astype(jnp.bfloat16)
    grads = (gain_grad, bias_grad, qkv_grad, qkv_bias_grad, out_grad, gateup_grad, down_grad)
    shares = (
        lax.psum_scatter(grads[0], "shard", scatter_dimension=0, tiled=True),
        lax.psum_scatter(grads[1], "shard", scatter_dimension=0, tiled=True),
        lax.psum_scatter(grads[2], "shard", scatter_dimension=0, tiled=True),
        lax.psum_scatter(grads[3], "shard", scatter_dimension=0, tiled=True),
        lax.psum_scatter(grads[4], "shard", scatter_dimension=0, tiled=True),
        lax.psum_scatter(grads[5], "shard", scatter_dimension=0, tiled=True),
        lax.psum_scatter(grads[6], "shard", scatter_dimension=0, tiled=True),
    )
    totals = (
        lax.psum(shares[0].astype(jnp.bfloat16), "replica").astype(jnp.float32),
        lax.psum(shares[1].astype(jnp.bfloat16), "replica").astype(jnp.float32),
        lax.psum(shares[2].astype(jnp.bfloat16), "replica").astype(jnp.float32),
        lax.psum(shares[3].astype(jnp.bfloat16), "replica").astype(jnp.float32),
        lax.psum(shares[4].astype(jnp.bfloat16), "replica").astype(jnp.float32),
        lax.psum(shares[5].astype(jnp.bfloat16), "replica").astype(jnp.float32),
        lax.psum(shares[6].astype(jnp.bfloat16), "replica").astype(jnp.float32),
    )
    return (
        block_output,
        tokens_grad,
        totals[0],
        totals[1],
        totals[2],
        totals[3],
        totals[4],
        totals[5],
        totals[6],
    )


def solution(mesh):
    placed = (
        P(("replica", "shard"), None),
        P(("replica", "shard"), None),
        P("shard"),
        P("shard"),
        P("shard", None),
        P("shard"),
        P("shard", None),
        P("shard", None),
        P("shard", None),
        P(("replica", "shard"), None),
    )
    return jax.shard_map(
        per_device,
        mesh=mesh,
        in_specs=placed,
        out_specs=(
            P(("replica", "shard"), None),
            P(("replica", "shard"), None),
            P("shard"),
            P("shard"),
            P("shard", None),
            P("shard"),
            P("shard", None),
            P("shard", None),
            P("shard", None),
        ),
        check_vma=False,
    )
```

profile of v0, /device:TPU:0, one launch (start us, length us, event | category | flops | bytes accessed | tf_op | source)
XLA Modules:
  0.0 2675.4 jit_solution(5653624331202639377)
XLA Ops:
  10.1 23.0 all-gather
  33.1 17.3 all-gather.1
  50.5 19.3 all-gather.2
  71.8 69.3 %all-gather.8.cloned.1.call-done = bf16[2048,6144]{1,0:T(8,128)(2,1)} async-done(((bf16[128,6144]{1,0:T(8,128)(2,1)}), bf16[2048,6144]{1,0:T(8,128)(2,1)}) %all-gather.8.cloned.1.call-update) | async-done | bytes 25165840 | tf_op jit(solution)/shard_map/all_gather | solution.py:64
  141.1 10.1 convolution_add_fusion
  151.5 1.3 copy.42
  152.8 1.0 copy.41
  153.8 1.2 slice.120
  155.4 1.0 subtract_convert_fusion.3
  156.5 1.4 fusion.37
  158.9 0.8 copy-done.4
  159.7 8.2 fusion.38
  168.1 50.3 %all-gather.10.cloned.1.call-done = bf16[2048,2048]{1,0:T(8,128)(2,1)} async-done(((bf16[128,2048]{1,0:T(8,128)(2,1)}), bf16[2048,2048]{1,0:T(8,128)(2,1)}) %all-gather.10.cloned.1.call-update) | async-done | bytes 8388624 | tf_op jit(solution)/shard_map/all_gather | solution.py:66
  218.4 7.1 convolution_convert_fusion
  225.4 2.1 copy.45
  228.3 1.9 multiply_reduce_fusion
  231.2 0.8 fusion.5
  232.7 1.1 pad_maximum_fusion.6
  233.8 1.6 convolution_convert_fusion.1
  235.5 21.9 fusion.30
  257.7 188.0 %all-gather.12.cloned.1.call-done = bf16[2048,11264]{1,0:T(8,128)(2,1)} async-done(((bf16[128,11264]{1,0:T(8,128)(2,1)}), bf16[2048,11264]{1,0:T(8,128)(2,1)}) %all-gather.12.cloned.1.call-update) | async-done | bytes 46137360 | tf_op jit(solution)/shard_map/all_gather | solution.py:67
  445.7 21.2 fusion.33
  466.8 99.0 %all-gather.14.cloned.1.call-done = bf16[5632,2048]{1,0:T(8,128)(2,1)} async-done(((bf16[352,2048]{1,0:T(8,128)(2,1)}), bf16[5632,2048]{1,0:T(8,128)(2,1)}) %all-gather.14.cloned.1.call-update) | async-done | bytes 23068688 | tf_op jit(solution)/shard_map/all_gather | solution.py:68
  565.8 14.7 multiply_convert_fusion.1
  580.5 22.7 fusion.39
  603.2 34.3 %fusion.1 = f32[2048,11264]{1,0:T(8,128)} fusion(bf16[128,5632]{1,0:T(8,128)(2,1)} %get-tuple-element.81, bf16[128,5632]{1,0:T(8,128)(2,1)} %get-tuple-element.80, bf16[128,2048]{1,0:T(8,128)(2,1)S(1)} %copy-done, f32[2048]{0:T(1024)S(1)} %bitcast.71, f32[2048]{0:T(1024)S(1)} %bitcast.61, f32[128]{0:T(128)S(1)} %copy-done.22, f32[128]{0:T(128)S(1)} %copy-done.20), kind=kOutput, calls=%fused_computation.18 | convolution fusion | flops 5912920064 | bytes 95699968 | tf_op jit(solution)/shard_map/sd,sf->df/dot_general | solution.py:150
  640.1 1.7 convert_reduce_fusion
  641.8 6.0 convolution_add_fusion.3
  647.8 100.6 %reduce-scatter.7.cloned.1.call-done = f32[128,2048]{1,0:T(8,128)} async-done(((f32[2048,2048]{1,0:T(8,128)}), f32[128,2048]{1,0:T(8,128)}) %reduce-scatter.7.cloned.1.call-update) | async-done | bytes 1048592 | tf_op jit(solution)/shard_map/reduce_scatter | solution.py:217
  748.4 2.1 convert_element_type.136
  750.4 468.8 %reduce-scatter.5.cloned.1.call-done = f32[128,6144]{1,0:T(8,128)} async-done(((f32[2048,6144]{1,0:T(8,128)}), f32[128,6144]{1,0:T(8,128)}) %reduce-scatter.5.cloned.1.call-update) | async-done | bytes 3145744 | tf_op jit(solution)/shard_map/reduce_scatter | solution.py:215
  1219.3 3.2 convert_element_type.131
  1222.5 433.2 %reduce-scatter.11.cloned.1.call-done = f32[352,2048]{1,0:T(8,128)} async-done(((f32[5632,2048]{1,0:T(8,128)}), f32[352,2048]{1,0:T(8,128)}) %reduce-scatter.11.cloned.1.call-update) | async-done | bytes 2883600 | tf_op jit(solution)/shard_map/reduce_scatter | solution.py:219
  1655.7 3.1 convert_element_type.140
  1658.8 836.9 %reduce-scatter.9.cloned.1.call-done = f32[128,11264]{1,0:T(8,128)} async-done(((f32[2048,11264]{1,0:T(8,128)}), f32[128,11264]{1,0:T(8,128)}) %reduce-scatter.9.cloned.1.call-update) | async-done | bytes 5767184 | tf_op jit(solution)/shard_map/reduce_scatter | solution.py:218
  2495.7 4.6 convert_element_type.138
  2500.3 23.0 fusion.2
  2523.3 14.9 fusion.20
  2538.2 59.0 %all-reduce.3 = (bf16[2048]{0:T(1024)(128)(2,1)S(1)}, bf16[2048]{0:T(1024)(128)(2,1)S(1)}, bf16[6144]{0:T(1024)(128)(2,1)S(1)}) all-reduce(f32[2048]{0:T(1024)S(1)} %get-tuple-element.55, f32[2048]{0:T(1024)S(1)} %get-tuple-element.58, f32[6144]{0:T(1024)S(1)} %convert_reduce_fusion), channel_id=2, replica_groups=mesh['replica'=2,'shard'=16] {'shard'}, use_global_device_ids=true, to_apply=%region_9.10.clone | all-reduce | flops 10240 | bytes 61440
  2597.4 5.3 all-reduce.4
  2604.3 2.5 fusion.19
  2606.9 11.7 fusion
  2618.5 38.3 %all-reduce.8.cloned.1.call-done = (bf16[128,6144]{1,0:T(8,128)(2,1)}, bf16[128,2048]{1,0:T(8,128)(2,1)}, bf16[128,11264]{1,0:T(8,128)(2,1)}, bf16[352,2048]{1,0:T(8,128)(2,1)}) async-done(((bf16[128,6144]{1,0:T(8,128)(2,1)}, bf16[128,2048]{1,0:T(8,128)(2,1)}, bf16[128,11264]{1,0:T(8,128)(2,1)}, bf16[352,2048]{1,0:T(8,128)(2,1)}), (bf16[128,6144]{1,0:T(8,128)(2,1)}, bf16[128,2048]{1,0:T(8,128)(2,1)}, ...) | async-done | bytes 6422544 | tf_op jit(solution)/shard_map/psum | solution.py:224
  2656.8 2.2 convert_element_type.137
  2659.0 3.4 convert_element_type.132
  2662.4 1.9 convert_element_type.141
  2664.4 0.9 copy-done.6
  2665.3 3.1 convert_element_type.139
  (114 shorter events, 12.4 us)
Async XLA Ops:
  7.2 2.9 copy-start.28
  7.2 2.9 copy-start.29
  7.2 25.9 copy-start.30
  7.2 133.9 %all-gather.8.cloned.1.call-start = ((), (), s32[]{:S(2)}) async-start(), calls=%async_computation.4 | async-start | bytes 26738688 | tf_op jit(solution)/shard_map/all_gather | solution.py:64
  7.9 61.9 %copy-start.27 = (s32[1,128]{1,0:T(1,128)S(1)}, s32[1,128]{1,0:T(1,128)}, u32[]{:S(2)}) copy-start(s32[1,128]{1,0:T(1,128)} %param.11) | copy-start | bytes 1540
  8.0 62.0 %copy-start = (bf16[128,2048]{1,0:T(8,128)(2,1)S(1)}, bf16[128,2048]{1,0:T(8,128)(2,1)}, u32[]{:S(2)}) copy-start(bf16[128,2048]{1,0:T(8,128)(2,1)} %param.10) | copy-start | bytes 1572868
  8.0 210.4 %all-gather.10.cloned.1.call-start = ((), (), s32[]{:S(2)}) async-start(), calls=%async_computation.5 | async-start | bytes 8912896 | tf_op jit(solution)/shard_map/all_gather | solution.py:66
  8.7 437.0 %all-gather.12.cloned.1.call-start = ((), (), s32[]{:S(2)}) async-start(), calls=%async_computation.6 | async-start | bytes 49020928 | tf_op jit(solution)/shard_map/all_gather | solution.py:67
  9.4 556.4 %all-gather.14.cloned.1.call-start = ((), (), s32[]{:S(2)}) async-start(), calls=%async_computation.7 | async-start | bytes 24510464 | tf_op jit(solution)/shard_map/all_gather | solution.py:68
  10.0 738.3 %reduce-scatter.7.cloned.1.call-start = ((), (), s32[]{:S(2)}) async-start(), calls=%async_computation.9 | async-start | bytes 17825792 | tf_op jit(solution)/shard_map/reduce_scatter | solution.py:217
  70.1 81.1 %copy-start.19 = (f32[128]{0:T(128)}, f32[128]{0:T(128)S(1)}, u32[]{:S(2)}) copy-start(f32[128]{0:T(128)S(1)} %broadcast_multiply_fusion.2) | copy-start | bytes 1540
  70.4 80.8 %copy-start.21 = (f32[128]{0:T(128)}, f32[128]{0:T(128)S(1)}, u32[]{:S(2)}) copy-start(f32[128]{0:T(128)S(1)} %add_rsqrt_fusion) | copy-start | bytes 1540
  155.0 2.9 copy-start.8
  156.4 1.8 copy-start.11
  156.4 1.8 copy-start.13
  156.4 1.8 copy-start.15
  156.5 1.8 copy-start.17
  156.5 1.8 copy-start.7
  157.9 0.9 copy-start.23
  158.3 0.6 copy-start.24
  158.3 1.4 copy-start.1
  158.9 0.8 copy-start.4
  167.9 1051.4 %reduce-scatter.5.cloned.1.call-start = ((), (), s32[]{:S(2)}) async-start(), calls=%async_computation.8 | async-start | bytes 53477376 | tf_op jit(solution)/shard_map/reduce_scatter | solution.py:215
  230.2 1.0 copy-start.9
  230.2 1.0 copy-start.16
  230.2 1.0 copy-start.18
  231.2 0.9 copy-start.12
  231.2 0.9 copy-start.14
  231.2 1.4 copy-start.25
  231.2 1.4 copy-start.26
  232.1 1.7 copy-start.3
  232.6 2.9 copy-start.20
  232.6 2.9 copy-start.22
  257.4 1398.2 %reduce-scatter.11.cloned.1.call-start = ((), (), s32[]{:S(2)}) async-start(), calls=%async_computation.11 | async-start | bytes 49020928 | tf_op jit(solution)/shard_map/reduce_scatter | solution.py:219
  603.2 1892.6 %reduce-scatter.9.cloned.1.call-start = ((), (), s32[]{:S(2)}) async-start(), calls=%async_computation.10 | async-start | bytes 98041856 | tf_op jit(solution)/shard_map/reduce_scatter | solution.py:218
  637.5 0.7 copy-start.31
  637.5 2.5 copy-start.2
  637.6 2019.2 %all-reduce.8.cloned.1.call-start = ((), (), s32[]{:S(2)}) async-start(), calls=%async_computation.12 | async-start | bytes 12845056 | tf_op jit(solution)/shard_map/psum | solution.py:224
  2602.7 4.2 copy-start.5
  2656.8 5.6 copy-start.10
  2662.4 2.9 copy-start.6
Sparse Core Ops, SparseCore 0:
  9.6 131.4 all-gather.7
  143.3 75.0 all-gather.9
  220.0 225.6 all-gather.11
  447.1 118.6 all-gather.13
  569.8 178.5 reduce-scatter.6
  752.4 466.7 reduce-scatter.4
  1223.5 432.1 reduce-scatter.10
  1659.9 835.8 reduce-scatter.8
  2500.4 156.3 all-reduce.7
where the time goes:
time: 2680 us
  waiting for transfers between devices  2290 us (85%)
  matrix products  202 us (8%)
  blocking collectives  124 us (5%)
  other arithmetic  35.4 us (1%)
    reduce_scatter x1, waiting for transfers between devices, per_device(): lax.psum_scatter(grads[5], 'shard', scatter_dimension=0, tiled=True)  837 us
    reduce_scatter x1, waiting for transfers between devices, per_device(): lax.psum_scatter(grads[2], 'shard', scatter_dimension=0, tiled=True)  469 us
    reduce_scatter x1, waiting for transfers between devices, per_device(): lax.psum_scatter(grads[6], 'shard', scatter_dimension=0, tiled=True)  433 us
    all_gather x1, waiting for transfers between devices, per_device(): lax.all_gather(shards[5], 'shard', axis=0, tiled=True)  188 us
    reduce_scatter x1, waiting for transfers between devices, per_device(): lax.psum_scatter(grads[4], 'shard', scatter_dimension=0, tiled=True)  101 us
    all_gather x1, waiting for transfers between devices, per_device(): lax.all_gather(shards[6], 'shard', axis=0, tiled=True)  99 us
    all_gather x1, waiting for transfers between devices, per_device(): lax.all_gather(shards[2], 'shard', axis=0, tiled=True)  69.3 us
    unnamed x1, blocking collectives  59 us
  transfers between devices with their start and end apart: 9, of which 9 were waited for; matrix products, arithmetic and copies ran while one was open for 9% of the time, Pallas kernels for 0%

commit v1 on v0

v1 whole, which is shorter than its diff:
```python
import functools
import math

import jax
import jax.numpy as jnp
from jax import lax
from jax.experimental import pallas as pl
from jax.experimental.pallas import tpu as pltpu
from jax.sharding import Mesh, PartitionSpec as P

HEADS = 32
HEAD_DIM = 64
ROT = 16
PAIR = 2 * HEAD_DIM
LANES = 128

epsilon = 1e-05
rope_base = 10000.0
score_scale = 1.0 / math.sqrt(HEAD_DIM)

bf16 = jnp.bfloat16
f32 = jnp.float32


def up_to(size, step):
    return -(-size // step) * step


def mm(a, b, dims):
    return lax.dot_general(a, b, (dims, ((), ())), preferred_element_type=f32)


def rotary_tables(segments):
    count, length = segments.shape
    indices = jnp.arange(length, dtype=jnp.int32)
    same_doc = segments[:, :, None] == segments[:, None, :]
    doc_start = jnp.min(jnp.where(same_doc, indices[None, None, :], length), axis=2)
    in_doc = (indices[None, :] - doc_start).astype(f32).reshape(count * length, 1)
    allowed = same_doc & (indices[:, None] >= indices[None, :])[None]
    half_rot = ROT // 2
    lane = jnp.arange(PAIR, dtype=jnp.int32) % HEAD_DIM
    inverse = rope_base ** (-((lane % half_rot).astype(f32) * (2.0 / ROT)))
    angles = in_doc * inverse[None, :]
    cos, sin = jnp.cos(angles), jnp.sin(angles)
    turned = (lane < ROT)[None, :]
    low = (lane < half_rot)[None, :]
    own = jnp.where(turned, cos, 1.0)
    after = jnp.where(low, -sin, 0.0)
    before = jnp.where(turned & ~low, sin, 0.0)
    return own, after, before, jnp.where(allowed, 0.0, -1e30).astype(f32)


def turn(x, own, after, before):
    half = ROT // 2
    width = x.shape[-1]
    return x * own + pltpu.roll(x, width - half, 1) * after + pltpu.roll(x, half, 1) * before


def head_mask(rows):
    return lax.broadcasted_iota(jnp.int32, (rows, PAIR), 1) < HEAD_DIM


def both_heads(x, first):
    zero = jnp.zeros_like(x)
    return jnp.concatenate([jnp.where(first, x, zero), jnp.where(first, zero, x)], axis=0)


def attend_kernel(joined_ref, bias_ref, own_ref, after_ref, before_ref, mask_ref, fused_ref, context_ref, probs_ref):
    length = joined_ref.shape[0]
    first = head_mask(length)
    own, after, before = own_ref[...], after_ref[...], before_ref[...]
    joined = joined_ref[...] + bias_ref[...]
    q = turn(joined[:, :PAIR], own, after, before).astype(bf16)
    k = turn(joined[:, PAIR : 2 * PAIR], own, after, before).astype(bf16)
    v = joined[:, 2 * PAIR :].astype(bf16)
    mask = mask_ref[0]
    scores = mm(both_heads(q, first), k, ((1,), (1,))) * score_scale
    scores = scores + jnp.concatenate([mask, mask], axis=0)
    top = jnp.max(scores, axis=1, keepdims=True)
    exps = jnp.exp(scores - top)
    probs = exps / jnp.sum(exps, axis=1, keepdims=True)
    low = probs.astype(bf16)
    side = jnp.concatenate([low[:length], low[length:]], axis=1)
    context = mm(side, both_heads(v, first), ((1,), (0,)))
    fused_ref[:, :PAIR] = q
    fused_ref[:, PAIR : 2 * PAIR] = k
    fused_ref[:, 2 * PAIR :] = v
    context_ref[...] = context.astype(bf16)
    probs_ref[0] = probs


def attend_back_kernel(fused_ref, probs_ref, dcontext_ref, own_ref, after_ref, before_ref, dfused_ref, sums_ref):
    length = fused_ref.shape[0]
    first = head_mask(length)
    own, after, before = own_ref[...], after_ref[...], before_ref[...]
    q = fused_ref[:, :PAIR]
    k = fused_ref[:, PAIR : 2 * PAIR]
    v = fused_ref[:, 2 * PAIR :]
    probs = probs_ref[0]
    dc = both_heads(dcontext_ref[...], first)
    dprobs = mm(dc, v, ((1,), (1,)))
    dscores = (probs * (dprobs - jnp.sum(dprobs * probs, axis=1, keepdims=True))).astype(bf16)
    dv = mm(probs.astype(bf16), dc, ((0,), (0,)))
    side = jnp.concatenate([dscores[:length], dscores[length:]], axis=1)
    dq = mm(side, both_heads(k, first), ((1,), (0,))) * score_scale
    dk = mm(dscores, both_heads(q, first), ((0,), (0,))) * score_scale
    out = jnp.concatenate(
        [turn(dq, own, -after, -before).astype(bf16), turn(dk, own, -after, -before).astype(bf16), dv.astype(bf16)],
        axis=1,
    )
    dfused_ref[...] = out

    @pl.when(pl.program_id(0) == 0)
    def _():
        sums_ref[...] = jnp.zeros_like(sums_ref)

    sums_ref[...] += jnp.sum(out.astype(f32), axis=0, keepdims=True)


def attend(joined, bias, tables, count):
    own, after, before, mask = tables
    tokens, width = joined.shape
    length = tokens // count
    row = lambda w: pl.BlockSpec((length, w), lambda i: (i, 0))
    return pl.pallas_call(
        attend_kernel,
        grid=(count,),
        in_specs=[
            row(width),
            pl.BlockSpec((1, width), lambda i: (0, 0)),
            row(PAIR),
            row(PAIR),
            row(PAIR),
            pl.BlockSpec((1, length, length), lambda i: (i, 0, 0)),
        ],
        out_specs=[row(width), row(PAIR), pl.BlockSpec((1, 2 * length, length), lambda i: (i, 0, 0))],
        out_shape=[
            jax.ShapeDtypeStruct((tokens, width), bf16),
            jax.ShapeDtypeStruct((tokens, PAIR), bf16),
            jax.ShapeDtypeStruct((count, 2 * length, length), f32),
        ],
        compiler_params=pltpu.CompilerParams(vmem_limit_bytes=32 << 20),
        cost_estimate=pl.CostEstimate(flops=tokens * length * PAIR * 8, bytes_accessed=tokens * 6000, transcendentals=tokens * length * 2),
    )(joined, bias, own, after, before, mask)


def attend_back(fused, probs, dcontext, tables, count):
    own, after, before, _ = tables
    tokens, width = fused.shape
    length = tokens // count
    row = lambda w: pl.BlockSpec((length, w), lambda i: (i, 0))
    return pl.pallas_call(
        attend_back_kernel,
        grid=(count,),
        in_specs=[
            row(width),
            pl.BlockSpec((1, 2 * length, length), lambda i: (i, 0, 0)),
            row(PAIR),
            row(PAIR),
            row(PAIR),
            row(PAIR),
        ],
        out_specs=[row(width), pl.BlockSpec((1, width), lambda i: (0, 0))],
        out_shape=[jax.ShapeDtypeStruct((tokens, width), bf16), jax.ShapeDtypeStruct((1, width), f32)],
        compiler_params=pltpu.CompilerParams(vmem_limit_bytes=32 << 20),
        cost_estimate=pl.CostEstimate(flops=tokens * length * PAIR * 16, bytes_accessed=tokens * 6000, transcendentals=0),
    )(fused, probs, dcontext, own, after, before)


def per_device(
    groups, tp, outer, tokens, segments, ln_gain, ln_bias, w_qkv, b_qkv, w_out, w_gateup, w_down, cotangent
):
    length, width = tokens.shape
    shards = tp * outer
    rows = w_qkv.shape[0]
    ffn = w_gateup.shape[1] // 2
    own_ffn = ffn // tp
    wide = up_to(own_ffn, LANES)
    own_qkv = 3 * PAIR

    small = jnp.concatenate([ln_gain, ln_bias, b_qkv, segments[0].astype(bf16)])
    small_rows = up_to(-(-small.shape[0] // width), 16)
    small_rows_of = jnp.pad(small, (0, small_rows * width - small.shape[0])).reshape(small_rows, width)
    packed = jnp.concatenate([tokens, small_rows_of], axis=0)
    gathered = lax.all_gather(packed, "tp", axis=0, tiled=False)
    vectors = gathered[:, length:, :].reshape(tp, -1)[:, : small.shape[0]]
    seg_all = vectors[:, small.shape[0] - length :].astype(jnp.int32)
    vectors = vectors[:, : small.shape[0] - length]
    if outer > 1:
        vectors = lax.all_gather(vectors, "outer", axis=1, tiled=False)
    vectors = vectors.reshape(shards, -1)
    gain_all = vectors[:, :rows].reshape(width).astype(f32)
    bias_all = vectors[:, rows : 2 * rows].reshape(width).astype(f32)
    qkv_bias = vectors[:, 2 * rows :].reshape(3, tp, PAIR).astype(f32)
    me = lax.axis_index("tp")
    my_bias = lax.dynamic_index_in_dim(qkv_bias, me, 1, keepdims=False).reshape(1, own_qkv)
    tokens_all = gathered[:, :length, :].reshape(tp * length, width)
    cotangent_all = lax.all_gather(cotangent, "tp", axis=0, tiled=True)

    qkv_cols = w_qkv.reshape(rows, 3, tp, PAIR).transpose(2, 0, 1, 3).reshape(tp, rows, own_qkv)
    ffn_cols = jnp.pad(
        w_gateup.reshape(rows, 2, tp, own_ffn).transpose(2, 0, 1, 3), ((0, 0), (0, 0), (0, 0), (0, wide - own_ffn))
    ).reshape(tp, rows, 2 * wide)
    columns = lax.all_to_all(jnp.concatenate([qkv_cols, ffn_cols], axis=2), "tp", 0, 0, tiled=True)
    if outer > 1:
        columns = lax.all_gather(columns, "outer", axis=1, tiled=False)
        w_out = lax.all_gather(w_out, "outer", axis=0, tiled=True)
        w_down = lax.all_gather(w_down, "outer", axis=0, tiled=True)
    columns = columns.reshape(width, own_qkv + 2 * wide)
    w_rows = jnp.concatenate([w_out, w_down, jnp.zeros((wide - own_ffn, width), bf16)], axis=0)

    tokens32 = tokens_all.astype(f32)
    centered = tokens32 - jnp.mean(tokens32, axis=1, keepdims=True)
    inv_std = lax.rsqrt(jnp.mean(centered * centered, axis=1, keepdims=True) + epsilon)
    normal_part = centered * inv_std
    normed = (normal_part * gain_all + bias_all).astype(bf16)
    tables = rotary_tables(seg_all)
    joined = mm(normed, columns[:, :own_qkv], ((1,), (0,)))
    fused, context, probs = attend(joined, my_bias, tables, tp)
    gateup = mm(normed, columns[:, own_qkv:], ((1,), (0,)))
    gate, up = gateup[:, :wide], gateup[:, wide:]
    s = jax.nn.sigmoid(gate)
    hidden = (gate * s * up).astype(bf16)
    inner = jnp.concatenate([context, hidden], axis=1)
    branch = mm(inner, w_rows, ((1,), (0,))).astype(bf16)
    branch = lax.psum_scatter(branch, "tp", scatter_dimension=0, tiled=True)
    block_output = (tokens.astype(f32) + branch.astype(f32)).astype(bf16)

    dinner = mm(cotangent_all, w_rows, ((1,), (1,)))
    dcontext = dinner[:, :PAIR].astype(bf16)
    dhidden = dinner[:, PAIR:]
    dgate = (dhidden * up * s * (1.0 + gate * (1.0 - s))).astype(bf16)
    dup = (dhidden * gate * s).astype(bf16)
    dfused, bias_sums = attend_back(fused, probs, dcontext, tables, tp)
    dcolumns = jnp.concatenate([dfused, dgate, dup], axis=1)
    dnormed = mm(dcolumns, columns, ((1,), (1,)))
    rows_grad = mm(inner, cotangent_all, ((0,), (0,)))[: PAIR + own_ffn]
    columns_grad = mm(normed, dcolumns, ((0,), (0,)))
    gain_sum = jnp.sum(dnormed * normal_part, axis=0)
    bias_sum = jnp.sum(dnormed, axis=0)
    dnormed_own = lax.psum_scatter(dnormed.astype(bf16), "tp", scatter_dimension=0, tiled=True).astype(f32)
    t32 = tokens.astype(f32)
    c = t32 - jnp.mean(t32, axis=1, keepdims=True)
    inv = lax.rsqrt(jnp.mean(c * c, axis=1, keepdims=True) + epsilon)
    xhat = c * inv
    e = dnormed_own * gain_all
    tokens_back = inv * (e - jnp.mean(e, axis=1, keepdims=True) - xhat * jnp.mean(e * xhat, axis=1, keepdims=True))
    tokens_grad = (cotangent.astype(f32) + tokens_back).astype(bf16)

    extra = jnp.concatenate(
        [gain_sum[:, None], bias_sum[:, None], jnp.zeros((width, LANES - 2), f32)], axis=1
    )
    grads = jnp.concatenate([columns_grad, extra], axis=1)
    if outer > 1:
        grads = grads.reshape(tp, outer, rows, -1)
        grads = lax.psum_scatter(grads, "outer", scatter_dimension=1, tiled=True)
        rows_out = lax.psum_scatter(rows_grad[:PAIR], "outer", scatter_dimension=0, tiled=True)
        rows_down = lax.psum_scatter(rows_grad[PAIR:], "outer", scatter_dimension=0, tiled=True)
        bias_sums = lax.psum(bias_sums, "outer")
    else:
        rows_out, rows_down = rows_grad[:PAIR], rows_grad[PAIR:]
    grads = grads.reshape(tp, rows, -1).astype(bf16)
    grads = lax.all_to_all(grads, "tp", 0, 0, tiled=True)
    rows_out = lax.psum(rows_out.astype(bf16), "replica").astype(f32)
    rows_down = lax.psum(rows_down.astype(bf16), "replica").astype(f32)
    grads = lax.psum(grads, "replica").astype(f32)
    qkv_grad = grads[:, :, :own_qkv].reshape(tp, rows, 3, PAIR).transpose(1, 2, 0, 3).reshape(rows, -1)
    gateup_grad = (
        grads[:, :, own_qkv : own_qkv + 2 * wide]
        .reshape(tp, rows, 2, wide)[..., :own_ffn]
        .transpose(1, 2, 0, 3)
        .reshape(rows, -1)
    )
    own_sums = jnp.sum(grads[:, :, own_qkv + 2 * wide :], axis=0)
    bias_all_sums = lax.all_gather(bias_sums.reshape(3, PAIR), "tp", axis=1, tiled=False)
    bias_all_sums = lax.psum(bias_all_sums, "replica").reshape(-1)
    place = me * outer + lax.axis_index("outer")
    qkv_bias_grad = lax.dynamic_slice_in_dim(bias_all_sums, place * (3 * rows), 3 * rows, 0)
    return (
        block_output,
        tokens_grad,
        own_sums[:, 0],
        own_sums[:, 1],
        qkv_grad,
        qkv_bias_grad,
        rows_out,
        gateup_grad,
        rows_down,
    )


def solution(mesh):
    groups, shards = mesh.shape["replica"], mesh.shape["shard"]
    tp = math.gcd(shards, HEADS // 2)
    outer = shards // tp
    inner_mesh = Mesh(mesh.devices.reshape(groups, tp, outer), ("replica", "tp", "outer"))
    everywhere = P(("replica", "tp", "outer"), None)
    vector = P(("tp", "outer"))
    matrix = P(("tp", "outer"), None)
    return jax.shard_map(
        functools.partial(per_device, groups, tp, outer),
        mesh=inner_mesh,
        in_specs=(everywhere, everywhere, vector, vector, matrix, vector, matrix, matrix, matrix, everywhere),
        out_specs=(everywhere, everywhere, vector, vector, matrix, vector, matrix, matrix, matrix),
        check_vma=False,
    )
```

time: 2680 us -> 845 us (0.32)
  waiting for transfers between devices: 2290 us -> 538 us
  matrix products: 202 us -> 71.5 us
  local copies, waits for them, and re-layouts: 9.72 us -> 87.2 us
  blocking collectives: 124 us -> 48.3 us
    reduce_scatter x4 -> x2, waiting for transfers between devices: 1840 us -> 56.3 us  [the longest x1 56.3 us: per_device(): branch = lax.psum_scatter(branch, 'tp', scatter_dimension=0, tiled=True)]
    all_gather x4 -> x2, waiting for transfers between devices: 407 us -> 70 us  [the longest x1 70 us: per_device(): gathered = lax.all_gather(packed, 'tp', axis=0, tiled=False)]
    all_to_all x0 -> x2, waiting for transfers between devices: none -> 237 us  [the longest x1 126 us: per_device(): lax.all_to_all(jnp.concatenate([qkv_cols, ffn_cols], axis=2), 'tp', 0, 0,...]
    psum x1, waiting for transfers between devices: 38.3 us -> 174 us  [per_device(): grads = lax.psum(grads, 'replica').astype(f32)]
    dot_general x18 -> x7, matrix products: 202 us -> 71.5 us  [mm(): return lax.dot_general(a, b, (dims, ((), ())), preferred_element_type=f32)]
    unnamed x1 -> x0, blocking collectives: 59 us -> none
    unnamed x69 -> x43, local copies, waits for them, and re-layouts: 3.44 us -> 31.6 us
    all_gather x3 -> x1, blocking collectives: 59.6 us -> 39.8 us  [per_device(): lax.all_gather(bias_sums.reshape(3, PAIR), 'tp', axis=1, tiled=False)]
  transfers between devices with their start and end apart: 9 -> 7, of which waited for: 9 -> 5; matrix products, arithmetic and copies ran while one was open for 9% -> 12% of each run, Pallas kernels for 0% -> 0%
where the time goes in v1:
time: 845 us; the launch traced here: 834 us
  waiting for transfers between devices  538 us (64%)
  local copies, waits for them, and re-layouts  87.2 us (10%)
  matrix products  71.5 us (8%)
  blocking collectives  48.3 us (6%)
  other arithmetic  43.1 us (5%)
  Pallas kernels  18.4 us (2%)
  between operations  14.7 us (2%)
  starting transfers between devices  12.6 us (1%)
    psum x1, waiting for transfers between devices, per_device(): grads = lax.psum(grads, 'replica').astype(f32)  174 us
    all_to_all x1, waiting for transfers between devices, per_device(): lax.all_to_all(jnp.concatenate([qkv_cols, ffn_cols], axis=2), 'tp', 0, 0,...  126 us
    all_to_all x1, waiting for transfers between devices, per_device(): grads = lax.all_to_all(grads, 'tp', 0, 0, tiled=True)  111 us
    dot_general x7, matrix products, mm(): return lax.dot_general(a, b, (dims, ((), ())), preferred_element_type=f32)  71.5 us
    all_gather x1, waiting for transfers between devices, per_device(): gathered = lax.all_gather(packed, 'tp', axis=0, tiled=False)  70 us
    reduce_scatter x1, waiting for transfers between devices, per_device(): branch = lax.psum_scatter(branch, 'tp', scatter_dimension=0, tiled=True)  56.3 us
    all_gather x1, blocking collectives, per_device(): lax.all_gather(bias_sums.reshape(3, PAIR), 'tp', axis=1, tiled=False)  39.8 us
    unnamed x43, local copies, waits for them, and re-layouts  31.6 us
  transfers between devices with their start and end apart: 7, of which 5 were waited for; matrix products, arithmetic and copies ran while one was open for 12% of the time, Pallas kernels for 0%

profile of v1, /device:TPU:0, one launch (start us, length us, event | category | flops | bytes accessed | tf_op | source)
XLA Modules:
  0.0 834.0 jit_solution(6217276339827509919)
XLA Ops:
  9.4 1.9 pad_maximum_fusion.7
  11.3 4.5 copy.74
  15.8 2.1 copy.93
  18.0 2.6 copy.72
  20.5 1.6 copy.73
  22.5 2.5 pad_maximum_fusion
  25.1 7.4 all-to-all-start
  32.7 126.0 %all-to-all-done = bf16[16,128,1152]{1,2,0:T(8,128)(2,1)} async-done(((bf16[16,128,1152]{1,2,0:T(8,128)(2,1)}), bf16[16,128,1152]{1,2,0:T(8,128)(2,1)}, u32[]{:S(2)}, u32[]{:S(2)}) %all-to-all-start) | async-done | bytes 4718624 | tf_op jit(solution)/shard_map/all_to_all | solution.py:204
  158.7 6.6 copy.76
  165.3 7.4 convolution_bitcast_fusion
  172.7 2.1 copy-done.7
  175.7 70.0 %all-gather.6.cloned.1.call-done = bf16[2304,2048]{1,0:T(8,128)(2,1)} async-done(((bf16[144,2048]{1,0:T(8,128)(2,1)}), bf16[2304,2048]{1,0:T(8,128)(2,1)}) %all-gather.6.cloned.1.call-update) | async-done | bytes 9437200 | tf_op jit(solution)/shard_map/all_gather | solution.py:185
  245.6 4.7 convert_reduce_fusion
  250.3 1.7 slice.94
  252.6 2.7 multiply_reduce_fusion.1
  255.4 3.7 add_convert_fusion
  259.2 4.6 fusion.5.joined_ref
  263.8 8.7 %fusion.2 = f32[2048,768]{1,0:T(8,128)} fusion(bf16[2048,2048]{1,0:T(8,128)(2,1)S(1)} %add_convert_fusion, bf16[2048,1152]{1,0:T(8,128)(2,1)S(1)} %bitcast.88), kind=kOutput, calls=%fused_computation.12 | convolution fusion | flops 6442450944 | bytes 17825792 | tf_op jit(solution)/shard_map/dot_general | solution.py:30
  273.5 5.8 multiply_convert_fusion.1
  279.2 3.8 fusion.7
  283.1 9.3 %shard_map.169 = (bf16[2048,384]{1,0:T(8,128)(2,1)S(1)}, bf16[2048,128]{1,0:T(8,128)(2,1)S(1)}, f32[16,256,128]{2,1,0:T(8,128)S(1)}) custom-call(f32[2048,384]{1,0:T(8,128)S(1)} %fusion.5.joined_ref, f32[1,384]{1,0:T(1,128)S(1)} %dynamic-slice_bitcast_fusion.bias_ref, f32[2048,128]{1,0:T(8,128)S(1)} %get-tuple-element.75.own_ref, ...), custom_call_target="tpu_custom_call" | custom-call | flops 268435456 | bytes 12288000 | tf_op jit(solution)/shard_map/pallas_call | solution.py:125
  292.5 9.0 %shard_map.170 = (bf16[2048,384]{1,0:T(8,128)(2,1)S(1)}, f32[1,384]{1,0:T(1,128)S(1)}) custom-call(bf16[2048,384]{1,0:T(8,128)(2,1)S(1)} %get-tuple-element.15.fused_ref, f32[16,256,128]{2,1,0:T(8,128)S(1)} %get-tuple-element.16.probs_ref, bf16[2048,128]{1,0:T(8,128)(2,1)S(1)} %copy-done, f32[2048,128]{1,0:T(8,128)S(1)} %get-tuple-element.75.own_ref, ...), custom_call_target="tpu_custom_call" | custom-call | flops 536870912 | bytes 12288000 | tf_op jit(solution)/shard_map/pallas_call | solution.py:152
  301.5 16.6 %fusion.47 = (bf16[2048]{0:T(1024)(128)(2,1)S(1)}, bf16[2048]{0:T(1024)(128)(2,1)S(1)}, bf16[2048,2048]{1,0:T(8,128)(2,1)}) fusion(f32[2048]{0:T(1024)S(1)} %rsqrt_bitcast_fusion, f32[2048]{0:T(1024)S(1)} %get-tuple-element.76, bf16[16,144,2048]{2,1,0:T(8,128)(2,1)} %bitcast.71, bf16[2048,1152]{1,0:T(8,128)(2,1)} %bitcast.84, ...), kind=kOutput, calls=%fused_computation.101 | convolution fusion | flops 9707188224 | bytes 26238976 | tf_op jit(solution)/shard_map/dot_general | solution.py:30
  319.3 10.2 %convolution_convert_fusion = bf16[2048,2048]{1,0:T(8,128)(2,1)} fusion(bf16[2048,384]{1,0:T(8,128)(2,1)} %get-tuple-element.67, bf16[2048,128]{1,0:T(8,128)(2,1)S(1)} %copy-done.2, bf16[352,2048]{1,0:T(8,128)(2,1)} %param.18, bf16[128,2048]{1,0:T(8,128)(2,1)S(1)} %copy-done.15, bf16[512]{0:T(512)(128)(2,1)S(1)} %pad.15.clone), kind=kOutput, calls=%fused_computation.6 | convolution fusion | flops 4309647360 | bytes 12452864 | tf_op jit(solution)/shard_map/dot_general | solution.py:30
  329.6 12.7 %copy.91 = bf16[2048,2048]{1,0:T(8,128)(2,1)} copy(bf16[2048,2048]{0,1:T(8,128)(2,1)} %bitcast.74) | data formatting | bytes 16777216 | tf_op jit(solution)/shard_map/dot_general | solution.py:30
  342.9 15.8 %convolution_convert_fusion.1 = bf16[16,128,1152]{2,1,0:T(8,128)(2,1)} fusion(bf16[16,128,2048]{2,1,0:T(8,128)(2,1)} %bitcast.81, bf16[2048,384]{1,0:T(8,128)(2,1)} %get-tuple-element.66, bf16[2048,384]{1,0:T(8,128)(2,1)} %copy-done.10, bf16[2048,384]{1,0:T(8,128)(2,1)S(1)} %get-tuple-element.17), kind=kOutput, calls=%fused_computation.7 | convolution fusion | flops 9680191488 | bytes 17825792 | tf_op jit(solution)/shard_map/dot_general | solution.py:30
  358.8 9.1 %concatenate.35 = bf16[16,128,1280]{2,1,0:T(8,128)(2,1)} concatenate(bf16[16,128,1152]{2,1,0:T(8,128)(2,1)} %convolution_convert_fusion.1, bf16[16,128,1]{2,1,0:T(8,128)(2,1)S(1)} %copy.81, bf16[16,128,1]{2,1,0:T(8,128)(2,1)S(1)} %copy.82, bf16[16,128,126]{2,1,0:T(8,128)(2,1)S(1)} %broadcast_in_dim.83), dimensions={2} | concatenate | bytes 10485760 | tf_op jit(solution)/shard_map/concatenate | solution.py:253
  367.9 4.7 all-to-all-start.1
  372.7 8.3 convolution_convert_fusion.2
  381.0 1.3 slice.112
  383.1 110.9 %all-to-all-done.1 = bf16[16,128,1280]{2,1,0:T(8,128)(2,1)} async-done(((bf16[16,128,1280]{2,1,0:T(8,128)(2,1)}), bf16[16,128,1280]{2,1,0:T(8,128)(2,1)}, u32[]{:S(2)}, u32[]{:S(2)}) %all-to-all-start.1) | async-done | bytes 5242912 | tf_op jit(solution)/shard_map/all_to_all | solution.py:263
  494.6 39.8 %all_gather.15 = f32[3,16,128]{2,0,1:T(4,128)S(1)} all-gather(f32[3,1,128]{2,0,1:T(4,128)S(1)} %bitcast.93), channel_id=1, replica_groups=mesh['replica'=2,'shard'=16] {'shard'}, dimensions={1}, use_global_device_ids=true | all-gather | bytes 26112 | tf_op jit(solution)/shard_map/all_gather | solution.py:275
  534.4 8.5 %psum.29 = f32[6144]{0:T(1024)S(1)} all-reduce(f32[6144]{0:T(1024)S(1)} %bitcast.92), channel_id=1, replica_groups=mesh['replica'=2,'shard'=16] {'replica'}, use_global_device_ids=true, to_apply=%region_13.14 | all-reduce | flops 6144 | bytes 49152 | tf_op jit(solution)/shard_map/psum | solution.py:276
  543.6 1.4 fusion.25
  545.0 56.3 %reduce-scatter.3.cloned.1.call-done = bf16[128,2048]{1,0:T(8,128)(2,1)} async-done(((bf16[2048,2048]{1,0:T(8,128)(2,1)}), bf16[128,2048]{1,0:T(8,128)(2,1)}) %reduce-scatter.3.cloned.1.call-update) | async-done | bytes 524304 | tf_op jit(solution)/shard_map/reduce_scatter | solution.py:226
  601.3 2.8 fusion.17
  604.1 174.3 %all-reduce.5.cloned.1.call-done = (bf16[16,128,1280]{2,1,0:T(8,128)(2,1)}, bf16[128,2048]{1,0:T(8,128)(2,1)}, bf16[352,2048]{1,0:T(8,128)(2,1)}) async-done(((bf16[16,128,1280]{2,1,0:T(8,128)(2,1)}, bf16[128,2048]{1,0:T(8,128)(2,1)}, bf16[352,2048]{1,0:T(8,128)(2,1)}), (bf16[16,128,1280]{2,1,0:T(8,128)(2,1)}, bf16[128,2048]{1,0:T(8,128)(2,1)}, bf16[352,2048]{1,0:T(8,128)(2,1)})) %all-reduce.5.cloned.1.call-update) | async-done | bytes 7208976 | tf_op jit(solution)/shard_map/psum | solution.py:266
  778.4 5.3 slice.110
  784.1 5.1 convert_element_type.143
  789.2 8.3 reshape.219
  797.5 10.1 %copy.92 = f32[16,128,2,352]{1,3,0,2:T(8,128)} copy(f32[16,128,2,352]{3,2,1,0:T(2,128)} %bitcast.75) | data formatting | bytes 11534336
  807.6 6.2 copy.88
  813.8 2.4 copy.83
  816.2 2.1 copy.84
  818.3 2.4 copy.87
  820.6 1.3 slice_reduce_fusion
  822.7 3.3 convert_element_type.145
  826.0 1.1 convert_element_type.144
  (84 shorter events, 10.4 us)
Async XLA Ops:
  7.2 158.1 %all-gather.4.cloned.1.call-start = ((), (), s32[]{:S(2)}) async-start(), calls=%async_computation.5 | async-start | bytes 8912896 | tf_op jit(solution)/shard_map/all_gather | solution.py:198
  7.9 237.7 %all-gather.6.cloned.1.call-start = ((), (), s32[]{:S(2)}) async-start(), calls=%async_computation.7 | async-start | bytes 10027008 | tf_op jit(solution)/shard_map/all_gather | solution.py:185
  25.1 133.6 %all-to-all-start = ((bf16[16,128,1152]{1,2,0:T(8,128)(2,1)}), bf16[16,128,1152]{1,2,0:T(8,128)(2,1)}, u32[]{:S(2)}, u32[]{:S(2)}) async-start(bf16[16,128,1152]{1,2,0:T(8,128)(2,1)} %pad_maximum_fusion), calls=%async_computation | async-start | bytes 9437184 | tf_op jit(solution)/shard_map/all_to_all | solution.py:204
  32.5 511.1 %reduce-scatter.5.cloned.1.call-start = ((), (), s32[]{:S(2)}) async-start(), calls=%async_computation.6 | async-start | bytes 8912896 | tf_op jit(solution)/shard_map/reduce_scatter | solution.py:241
  32.7 132.6 %copy-start.13 = (bf16[352,2048]{1,0:T(8,128)(2,1)S(1)}, bf16[352,2048]{1,0:T(8,128)(2,1)}, u32[]{:S(2)}) copy-start(bf16[352,2048]{1,0:T(8,128)(2,1)} %param.18) | copy-start | bytes 4325380
  32.7 132.6 %copy-start.14 = (bf16[128,2048]{1,0:T(8,128)(2,1)S(1)}, bf16[128,2048]{1,0:T(8,128)(2,1)}, u32[]{:S(2)}) copy-start(bf16[128,2048]{1,0:T(8,128)(2,1)} %param.16) | copy-start | bytes 1572868
  172.7 2.1 copy-start.7
  245.6 7.0 copy-start.3
  252.6 6.5 slice-start
  255.4 3.8 slice-start.1
  259.1 4.6 copy-start.5
  279.2 22.3 %copy-start.10 = (bf16[2048,384]{1,0:T(8,128)(2,1)}, bf16[2048,384]{1,0:T(8,128)(2,1)S(1)}, u32[]{:S(2)}) copy-start(bf16[2048,384]{1,0:T(8,128)(2,1)S(1)} %get-tuple-element.65) | copy-start | bytes 4718596
  283.1 9.4 %copy-start = (bf16[2048,128]{1,0:T(8,128)(2,1)S(1)}, bf16[2048,128]{1,0:T(8,128)(2,1)}, u32[]{:S(2)}) copy-start(bf16[2048,128]{1,0:T(8,128)(2,1)} %slice.140.dcontext_ref) | copy-start | bytes 1572868
  292.4 9.1 %copy-start.1 = (bf16[2048,128]{1,0:T(8,128)(2,1)}, bf16[2048,128]{1,0:T(8,128)(2,1)S(1)}, u32[]{:S(2)}) copy-start(bf16[2048,128]{1,0:T(8,128)(2,1)S(1)} %get-tuple-element.14) | copy-start | bytes 1572868
  292.4 9.1 %copy-start.11 = (bf16[2048,384]{1,0:T(8,128)(2,1)S(1)}, bf16[2048,384]{1,0:T(8,128)(2,1)}, u32[]{:S(2)}) copy-start(bf16[2048,384]{1,0:T(8,128)(2,1)} %get-tuple-element.66) | copy-start | bytes 4718596
  318.1 1.0 copy-start.2
  318.1 1.2 copy-start.15
  318.1 283.2 %reduce-scatter.3.cloned.1.call-start = ((), (), s32[]{:S(2)}) async-start(), calls=%async_computation.4 | async-start | bytes 8912896 | tf_op jit(solution)/shard_map/reduce_scatter | solution.py:226
  367.9 4.8 copy-start.9
  367.9 126.2 %all-to-all-start.1 = ((bf16[16,128,1280]{2,1,0:T(8,128)(2,1)}), bf16[16,128,1280]{2,1,0:T(8,128)(2,1)}, u32[]{:S(2)}, u32[]{:S(2)}) async-start(bf16[16,128,1280]{2,1,0:T(8,128)(2,1)} %concatenate.35), calls=%async_computation.3 | async-start | bytes 10485760 | tf_op jit(solution)/shard_map/all_to_all | solution.py:263
  372.6 405.8 %all-reduce.5.cloned.1.call-start = ((), (), s32[]{:S(2)}) async-start(), calls=%async_computation.8 | async-start | bytes 14417920 | tf_op jit(solution)/shard_map/psum | solution.py:266
  382.3 111.8 %copy-start.6 = (bf16[128,2048]{1,0:T(8,128)(2,1)S(1)}, bf16[128,2048]{1,0:T(8,128)(2,1)}, u32[]{:S(2)}) copy-start(bf16[128,2048]{1,0:T(8,128)(2,1)} %param.10) | copy-start | bytes 1572868
  494.0 107.3 %copy-start.8 = (bf16[128,2048]{1,0:T(8,128)(2,1)S(1)}, bf16[128,2048]{1,0:T(8,128)(2,1)}, u32[]{:S(2)}) copy-start(bf16[128,2048]{1,0:T(8,128)(2,1)} %param.19) | copy-start | bytes 1572868
  778.4 5.3 copy-start.4
  820.6 5.3 copy-start.12
Sparse Core Ops, SparseCore 0:
  10.2 143.6 all-gather.3
  156.7 88.8 all-gather.5
  318.3 173.5 reduce-scatter.4
  495.8 105.4 reduce-scatter.2
  604.9 173.4 all-reduce.4

commit v2 on v1

v2 whole, which is shorter than its diff:
```python
import functools
import math

import jax
import jax.numpy as jnp
from jax import lax
from jax.experimental import pallas as pl
from jax.experimental.pallas import tpu as pltpu
from jax.sharding import Mesh, PartitionSpec as P

HEADS = 32
HEAD_DIM = 64
ROT = 16
PAIR = 2 * HEAD_DIM
TP = ("z", "y", "c")
LANES = 128
SEQUENCES = 8
CHUNK = 512

epsilon = 1e-05
rope_base = 10000.0
score_scale = 1.0 / math.sqrt(HEAD_DIM)

bf16 = jnp.bfloat16
f32 = jnp.float32


def up_to(size, step):
    return -(-size // step) * step


def mm(a, b, dims):
    return lax.dot_general(a, b, (dims, ((), ())), preferred_element_type=f32)


def rotary_tables(segments):
    count, length = segments.shape
    indices = jnp.arange(length, dtype=jnp.int32)
    same_doc = segments[:, :, None] == segments[:, None, :]
    doc_start = jnp.min(jnp.where(same_doc, indices[None, None, :], length), axis=2)
    in_doc = (indices[None, :] - doc_start).astype(f32).reshape(count * length, 1)
    allowed = same_doc & (indices[:, None] >= indices[None, :])[None]
    half_rot = ROT // 2
    lane = jnp.arange(PAIR, dtype=jnp.int32) % HEAD_DIM
    inverse = rope_base ** (-((lane % half_rot).astype(f32) * (2.0 / ROT)))
    angles = in_doc * inverse[None, :]
    cos, sin = jnp.cos(angles), jnp.sin(angles)
    turned = (lane < ROT)[None, :]
    low = (lane < half_rot)[None, :]
    own = jnp.where(turned, cos, 1.0)
    after = jnp.where(low, -sin, 0.0)
    before = jnp.where(turned & ~low, sin, 0.0)
    return own, after, before, jnp.where(allowed, 0.0, -1e30).astype(f32)


def turn(x, own, after, before):
    half = ROT // 2
    width = x.shape[-1]
    return x * own + pltpu.roll(x, width - half, 1) * after + pltpu.roll(x, half, 1) * before


def head_mask(rows):
    return lax.broadcasted_iota(jnp.int32, (rows, PAIR), 1) < HEAD_DIM


def both_heads(x, first):
    zero = jnp.zeros_like(x)
    return jnp.concatenate([jnp.where(first, x, zero), jnp.where(first, zero, x)], axis=0)


def attend_kernel(joined_ref, bias_ref, own_ref, after_ref, before_ref, mask_ref, fused_ref, context_ref, probs_ref):
    length = mask_ref.shape[1]
    first = head_mask(length)
    for n in range(mask_ref.shape[0]):
        rows = pl.ds(n * length, length)
        own, after, before = own_ref[rows, :], after_ref[rows, :], before_ref[rows, :]
        joined = joined_ref[rows, :] + bias_ref[...]
        q = turn(joined[:, :PAIR], own, after, before).astype(bf16)
        k = turn(joined[:, PAIR : 2 * PAIR], own, after, before).astype(bf16)
        v = joined[:, 2 * PAIR :].astype(bf16)
        mask = mask_ref[n]
        scores = mm(both_heads(q, first), k, ((1,), (1,))) * score_scale
        scores = scores + jnp.concatenate([mask, mask], axis=0)
        top = jnp.max(scores, axis=1, keepdims=True)
        exps = jnp.exp(scores - top)
        probs = exps / jnp.sum(exps, axis=1, keepdims=True)
        low = probs.astype(bf16)
        side = jnp.concatenate([low[:length], low[length:]], axis=1)
        context = mm(side, both_heads(v, first), ((1,), (0,)))
        fused_ref[rows, :PAIR] = q
        fused_ref[rows, PAIR : 2 * PAIR] = k
        fused_ref[rows, 2 * PAIR :] = v
        context_ref[rows, :] = context.astype(bf16)
        probs_ref[n] = probs


def attend_back_kernel(fused_ref, probs_ref, dcontext_ref, own_ref, after_ref, before_ref, dfused_ref, sums_ref):
    length = probs_ref.shape[2]
    first = head_mask(length)
    total = jnp.zeros(sums_ref.shape, f32)
    for n in range(probs_ref.shape[0]):
        rows = pl.ds(n * length, length)
        own, after, before = own_ref[rows, :], after_ref[rows, :], before_ref[rows, :]
        q = fused_ref[rows, :PAIR]
        k = fused_ref[rows, PAIR : 2 * PAIR]
        v = fused_ref[rows, 2 * PAIR :]
        probs = probs_ref[n]
        dc = both_heads(dcontext_ref[rows, :], first)
        dprobs = mm(dc, v, ((1,), (1,)))
        dscores = (probs * (dprobs - jnp.sum(dprobs * probs, axis=1, keepdims=True))).astype(bf16)
        dv = mm(probs.astype(bf16), dc, ((0,), (0,)))
        side = jnp.concatenate([dscores[:length], dscores[length:]], axis=1)
        dq = mm(side, both_heads(k, first), ((1,), (0,))) * score_scale
        dk = mm(dscores, both_heads(q, first), ((0,), (0,))) * score_scale
        out = jnp.concatenate(
            [turn(dq, own, -after, -before).astype(bf16), turn(dk, own, -after, -before).astype(bf16), dv.astype(bf16)],
            axis=1,
        )
        dfused_ref[rows, :] = out
        total = total + jnp.sum(out.astype(f32), axis=0, keepdims=True)

    @pl.when(pl.program_id(0) == 0)
    def _():
        sums_ref[...] = jnp.zeros_like(sums_ref)

    sums_ref[...] += total


def attend(joined, bias, tables, count):
    own, after, before, mask = tables
    tokens, width = joined.shape
    length = tokens // count
    many = math.gcd(count, SEQUENCES)
    row = lambda w: pl.BlockSpec((many * length, w), lambda i: (i, 0))
    return pl.pallas_call(
        attend_kernel,
        name="attend",
        grid=(count // many,),
        in_specs=[
            row(width),
            pl.BlockSpec((1, width), lambda i: (0, 0)),
            row(PAIR),
            row(PAIR),
            row(PAIR),
            pl.BlockSpec((many, length, length), lambda i: (i, 0, 0)),
        ],
        out_specs=[row(width), row(PAIR), pl.BlockSpec((many, 2 * length, length), lambda i: (i, 0, 0))],
        out_shape=[
            jax.ShapeDtypeStruct((tokens, width), bf16),
            jax.ShapeDtypeStruct((tokens, PAIR), bf16),
            jax.ShapeDtypeStruct((count, 2 * length, length), f32),
        ],
        compiler_params=pltpu.CompilerParams(vmem_limit_bytes=32 << 20),
        cost_estimate=pl.CostEstimate(flops=tokens * length * PAIR * 8, bytes_accessed=tokens * 6000, transcendentals=tokens * length * 2),
    )(joined, bias, own, after, before, mask)


def attend_back(fused, probs, dcontext, tables, count, *others):
    own, after, before, _ = tables
    tokens, width = fused.shape
    length = tokens // count
    many = math.gcd(count, SEQUENCES)
    row = lambda w: pl.BlockSpec((many * length, w), lambda i: (i, 0))
    return pl.pallas_call(
        ignoring(attend_back_kernel, 6, len(others)),
        name="attend_back",
        grid=(count // many,),
        in_specs=[
            row(width),
            pl.BlockSpec((many, 2 * length, length), lambda i: (i, 0, 0)),
            row(PAIR),
            row(PAIR),
            row(PAIR),
            row(PAIR),
            *anywhere(others),
        ],
        out_specs=[row(width), pl.BlockSpec((1, width), lambda i: (0, 0))],
        out_shape=[jax.ShapeDtypeStruct((tokens, width), bf16), jax.ShapeDtypeStruct((1, width), f32)],
        compiler_params=pltpu.CompilerParams(vmem_limit_bytes=32 << 20),
        cost_estimate=pl.CostEstimate(flops=tokens * length * PAIR * 16, bytes_accessed=tokens * 6000, transcendentals=0),
    )(fused, probs, dcontext, own, after, before, *others)


def shifted(x, axis, size, step):
    return lax.ppermute(x, axis, [(i, (i + step) % size) for i in range(size)])


def limits(mib):
    return pltpu.CompilerParams(vmem_limit_bytes=mib << 20)


def cost(flops, moved):
    return pl.CostEstimate(flops=1, bytes_accessed=1, transcendentals=0)


def whole_block(array):
    return pl.BlockSpec(array.shape, lambda *_: (0,) * array.ndim)


def pack_kernel(part_ref, own_ref, out_ref, *, sections, tp, size, wide):
    own = own_ref[...]
    rows = own.shape[0]
    for t in range(tp):
        pieces = []
        for section in range(sections):
            at = (section * tp + t) * size
            pieces.append(own[:, at : at + size])
            if wide > size:
                pieces.append(jnp.zeros((rows, wide - size), own.dtype))
        out_ref[t] = jnp.concatenate(pieces, axis=1) if len(pieces) > 1 else pieces[0]


def pack(weight, part, groups, sections, tp, size, wide):
    rows, width = weight.shape
    half = rows // groups
    step = min(half, 16)
    return pl.pallas_call(
        functools.partial(pack_kernel, sections=sections, tp=tp, size=size, wide=wide),
        name="pack",
        grid_spec=pltpu.PrefetchScalarGridSpec(
            num_scalar_prefetch=1,
            grid=(half // step,),
            in_specs=[pl.BlockSpec((step, width), lambda i, part: (part[0] * (half // step) + i, 0))],
            out_specs=pl.BlockSpec((tp, step, sections * wide), lambda i, part: (0, i, 0)),
        ),
        out_shape=jax.ShapeDtypeStruct((tp, half, sections * wide), weight.dtype),
        compiler_params=limits(32),
        cost_estimate=cost(0, 4 * half * width),
    )(part, weight)


def nothing(*refs):
    del refs


def anywhere(arrays):
    return [pl.BlockSpec(memory_space=pl.ANY) for _ in arrays]


def after(x, *others):
    return pl.pallas_call(
        nothing,
        name="after",
        in_specs=anywhere((x, *others)),
        out_specs=pl.BlockSpec(memory_space=pl.ANY),
        out_shape=jax.ShapeDtypeStruct(x.shape, x.dtype),
        input_output_aliases={0: 0},
    )(x, *others)


def ignoring(kernel, at, count):
    return lambda *refs: kernel(*refs[:at], *refs[at + count :])


def in_three(x):
    parts = []
    for _ in range(3):
        low = lax.reduce_precision(x, 8, 7)
        parts.append(low.astype(bf16))
        x = x - low
    return parts


def as_column(row):
    n = row.shape[1]
    square = lax.broadcasted_iota(jnp.int32, (n, n), 0) == lax.broadcasted_iota(jnp.int32, (n, n), 1)
    return jnp.sum(jnp.where(square, row, 0.0), axis=1, keepdims=True)


def normal_of(a_ref, b_ref, stats_ref):
    parts = []
    for k, ref in enumerate((a_ref, b_ref)):
        mean, inv_std = as_column(stats_ref[k, 0:1, :]), as_column(stats_ref[k, 1:2, :])
        parts.append((ref[0].astype(f32) - mean) * inv_std)
    return jnp.concatenate(parts, axis=0)


def unpack_kernel(part_ref, own_ref, other_ref, out_ref, *, sections, tp, size, wide):
    got = jnp.where(pl.program_id(0) == 0, own_ref[...], other_ref[...])
    for section in range(sections):
        pieces = [got[t, :, section * wide : section * wide + size] for t in range(tp)]
        out_ref[:, section * tp * size : (section + 1) * tp * size] = jnp.concatenate(pieces, axis=1).astype(f32)


def unpack(own, other, part, sections, size, wide):
    tp, half, width = own.shape
    step = min(half, 16)
    count = half // step
    return pl.pallas_call(
        functools.partial(unpack_kernel, sections=sections, tp=tp, size=size, wide=wide),
        name="unpack",
        grid_spec=pltpu.PrefetchScalarGridSpec(
            num_scalar_prefetch=1,
            grid=(2, count),
            in_specs=[
                pl.BlockSpec((tp, step, width), lambda i, j, part: (0, jnp.where(i == 0, j, count - 1), 0)),
                pl.BlockSpec((tp, step, width), lambda i, j, part: (0, jnp.where(i == 0, 0, j), 0)),
            ],
            out_specs=pl.BlockSpec(
                (step, sections * tp * size), lambda i, j, part: (lax.rem(part[0] + i, 2) * count + j, 0)
            ),
        ),
        out_shape=jax.ShapeDtypeStruct((2 * half, sections * tp * size), f32),
        compiler_params=limits(48),
        cost_estimate=cost(0, 12 * half * width * tp),
    )(part, own, other)


def gate_kernel(
    a_ref, b_ref, stats_ref, gain_ref, bias_ref, gu_ref, qkv_ref, normed_ref, gate_ref, up_ref, hidden_ref, joined_ref
):
    normed = (normal_of(a_ref, b_ref, stats_ref) * gain_ref[...] + bias_ref[...]).astype(bf16)
    normed_ref[...] = normed
    wide = gate_ref.shape[1]
    gateup = mm(normed, gu_ref[...], ((1,), (0,)))
    gate, up = gateup[:, :wide], gateup[:, wide:]
    gate_ref[...] = gate
    up_ref[...] = up
    hidden_ref[...] = (gate * jax.nn.sigmoid(gate) * up).astype(bf16)
    joined_ref[...] = mm(normed, qkv_ref[...], ((1,), (0,)))


def gate_forward(gathered, stats, gain, bias, gu, qkv):
    count, padded, width = gathered.shape
    length, wide = LANES, gu.shape[1] // 2
    tokens = count * length
    block = lambda k: pl.BlockSpec((1, length, width), lambda i: (2 * i + k, 0, 0))
    row = lambda w: pl.BlockSpec((2 * length, w), lambda i: (i, 0))
    return pl.pallas_call(
        gate_kernel,
        name="gate_fwd",
        grid=(count // 2,),
        in_specs=[
            block(0),
            block(1),
            pl.BlockSpec((2, 8, length), lambda i: (i, 0, 0)),
            whole_block(gain),
            whole_block(bias),
            whole_block(gu),
            whole_block(qkv),
        ],
        out_specs=[row(width), row(wide), row(wide), row(wide), row(3 * PAIR)],
        out_shape=[
            jax.ShapeDtypeStruct((tokens, width), bf16),
            jax.ShapeDtypeStruct((tokens, wide), f32),
            jax.ShapeDtypeStruct((tokens, wide), f32),
            jax.ShapeDtypeStruct((tokens, wide), bf16),
            jax.ShapeDtypeStruct((tokens, 3 * PAIR), f32),
        ],
        compiler_params=limits(56),
        cost_estimate=cost(2 * tokens * width * (2 * wide + 3 * PAIR), tokens * (4 * width + 10 * wide + 12 * PAIR)),
    )(gathered, gathered, stats, gain, bias, gu, qkv)


def branch_kernel(far, order_ref, ac_ref, bc_ref, ah_ref, bh_ref, w_ref, *refs):
    context = jnp.concatenate([ac_ref[...], bc_ref[...]], axis=0)
    hidden = jnp.concatenate([ah_ref[...], bh_ref[...]], axis=0)
    total = mm(context, w_ref[:PAIR, :], ((1,), (0,))) + mm(hidden, w_ref[PAIR:, :], ((1,), (0,)))
    if far:
        refs[0][...] = total.astype(bf16)
        return
    got_ref, sent_ref, keep_ref = refs
    keep_ref[...] = total + got_ref[...].astype(f32)

    @pl.when(pl.program_id(0) < pl.num_programs(0) // 2)
    def _():
        sent_ref[...] = keep_ref[...].astype(bf16)


def branches(order, context, hidden, w, got=None):
    tokens, wide = hidden.shape
    width = w.shape[1]
    count = order.shape[0]
    step = 2 * LANES
    row = lambda x, k: pl.BlockSpec((LANES, x.shape[1]), lambda i, order: (order[2 * i + k], 0))
    plain = pl.BlockSpec((step, width), lambda i, order: (i, 0))
    if got is None:
        out_specs = [plain]
        out_shape = [jax.ShapeDtypeStruct((count * LANES, width), bf16)]
        more = []
    else:
        sent = count // 4
        out_specs = [
            pl.BlockSpec((step, width), lambda i, order: (jnp.minimum(i, sent - 1), 0)),
            pl.BlockSpec((step, width), lambda i, order: (jnp.maximum(i - sent, 0), 0)),
        ]
        out_shape = [jax.ShapeDtypeStruct((count * LANES // 2, width), kind) for kind in (bf16, f32)]
        more = [got]
    return pl.pallas_call(
        functools.partial(branch_kernel, got is None),
        name="branch_far" if got is None else "branch_near",
        grid_spec=pltpu.PrefetchScalarGridSpec(
            num_scalar_prefetch=1,
            grid=(count // 2,),
            in_specs=[
                row(context, 0),
                row(context, 1),
                row(hidden, 0),
                row(hidden, 1),
                whole_block(w),
                *[plain for _ in more],
            ],
            out_specs=out_specs,
        ),
        out_shape=out_shape,
        compiler_params=limits(48),
        cost_estimate=cost(2 * tokens * width * (PAIR + wide), 2 * tokens * (width + PAIR + wide)),
    )(order, context, context, hidden, hidden, w, *more)


def gate_back_kernel(cotangent_ref, gate_ref, up_ref, w_ref, dgateup_ref, dcontext_ref):
    dinner = mm(cotangent_ref[...], w_ref[...], ((1,), (1,)))
    dcontext_ref[...] = dinner[:, :PAIR].astype(bf16)
    dhidden = dinner[:, PAIR:]
    gate, up = gate_ref[...], up_ref[...]
    s = jax.nn.sigmoid(gate)
    wide = gate.shape[1]
    dgateup_ref[:, :wide] = (dhidden * up * s * (1.0 + gate * (1.0 - s))).astype(bf16)
    dgateup_ref[:, wide:] = (dhidden * gate * s).astype(bf16)


def gate_backward(cotangent, gate, up, w, *others):
    tokens, wide = gate.shape
    width = w.shape[1]
    row = lambda w: pl.BlockSpec((2 * LANES, w), lambda i: (i, 0))
    return pl.pallas_call(
        ignoring(gate_back_kernel, 4, len(others)),
        name="gate_back",
        grid=(tokens // (2 * LANES),),
        in_specs=[row(width), row(wide), row(wide), whole_block(w), *anywhere(others)],
        out_specs=[row(2 * wide), row(PAIR)],
        out_shape=[jax.ShapeDtypeStruct((tokens, 2 * wide), bf16), jax.ShapeDtypeStruct((tokens, PAIR), bf16)],
        compiler_params=limits(48),
        cost_estimate=cost(2 * tokens * width * (PAIR + wide), tokens * (2 * width + 12 * wide)),
    )(cotangent, gate, up, w, *others)


def grads_kernel(part_ref, normed_ref, d_ref, mine_ref, theirs_ref):
    grads = mm(normed_ref[...], d_ref[...], ((0,), (0,)))
    count, half, _ = mine_ref.shape
    first = part_ref[0] == 0
    for t in range(count):
        low = grads[2 * t * half : (2 * t + 1) * half]
        high = grads[(2 * t + 1) * half : (2 * t + 2) * half]
        mine_ref[t] = jnp.where(first, low, high)
        theirs_ref[t] = jnp.where(first, high, low).astype(bf16)


def split_grads(part, normed, d, half, *others):
    tokens, width = normed.shape
    step = 4 * LANES
    out = d.shape[1]
    blocks = step // (2 * half)
    piece = lambda: pl.BlockSpec((blocks, half, out), lambda i, part: (i, 0, 0))
    return pl.pallas_call(
        ignoring(grads_kernel, 3, len(others)),
        name="grads",
        grid_spec=pltpu.PrefetchScalarGridSpec(
            num_scalar_prefetch=1,
            grid=(width // step,),
            in_specs=[pl.BlockSpec((tokens, step), lambda i, part: (0, i)), whole_block(d)]
            + anywhere(others),
            out_specs=[piece(), piece()],
        ),
        out_shape=[
            jax.ShapeDtypeStruct((width // (2 * half), half, out), f32),
            jax.ShapeDtypeStruct((width // (2 * half), half, out), bf16),
        ],
        compiler_params=limits(56),
        cost_estimate=cost(2 * tokens * width * d.shape[1], 2 * tokens * (width + d.shape[1]) + 3 * width * out),
    )(part, normed, d, *others)


def rows_kernel(context_ref, hidden_ref, cotangent_ref, out_ref):
    cotangent = cotangent_ref[...]
    out_ref[:PAIR, :] = mm(context_ref[...], cotangent, ((0,), (0,))).astype(out_ref.dtype)
    hidden = mm(hidden_ref[...], cotangent, ((0,), (0,)))
    out_ref[PAIR:, :] = hidden[: out_ref.shape[0] - PAIR].astype(out_ref.dtype)


def rows_grads(context, hidden, cotangent, own, kind, *others):
    tokens, width = cotangent.shape
    step = 4 * LANES
    return pl.pallas_call(
        ignoring(rows_kernel, 3, len(others)),
        name="rows",
        grid=(width // step,),
        in_specs=[
            whole_block(context),
            whole_block(hidden),
            pl.BlockSpec((tokens, step), lambda i: (0, i)),
            *anywhere(others),
        ],
        out_specs=pl.BlockSpec((own, step), lambda i: (0, i)),
        out_shape=jax.ShapeDtypeStruct((own, width), kind),
        compiler_params=limits(56),
        cost_estimate=cost(2 * tokens * width * own, tokens * width * 2),
    )(context, hidden, cotangent, *others)


def dnormed_kernel(order_ref, a_ref, b_ref, as_ref, bs_ref, ag_ref, bg_ref, aq_ref, bq_ref, gu_ref, qkv_ref, *refs):
    *far_refs, out_ref, sums_ref = refs if len(refs) == 2 else (*refs[:-2], refs[-1], refs[-2])
    step = pl.program_id(0)
    gateup = jnp.concatenate([ag_ref[...], bg_ref[...]], axis=0)
    fused = jnp.concatenate([aq_ref[...], bq_ref[...]], axis=0)

    @pl.when(step == 0)
    def _():
        sums_ref[...] = jnp.zeros_like(sums_ref)

    means = [as_column(ref[0, 0:1, :]) for ref in (as_ref, bs_ref)]
    stds = [as_column(ref[0, 1:2, :]) for ref in (as_ref, bs_ref)]
    width = gu_ref.shape[0]
    for at in range(0, width, CHUNK):
        cols = pl.ds(at, CHUNK)
        dnormed = mm(gateup, gu_ref[cols, :], ((1,), (1,))) + mm(fused, qkv_ref[cols, :], ((1,), (1,)))
        out_ref[:, cols] = dnormed.astype(out_ref.dtype)
        normal = jnp.concatenate(
            [(ref[0, :, cols].astype(f32) - mean) * std for ref, mean, std in zip((a_ref, b_ref), means, stds)], axis=0
        )
        sums_ref[0:1, cols] += jnp.sum(dnormed * normal, axis=0, keepdims=True)
        sums_ref[1:2, cols] += jnp.sum(dnormed, axis=0, keepdims=True)
    for i, far_ref in enumerate(far_refs):

        @pl.when(step == i)
        def _():
            far_ref[...] = out_ref[...]


def dnormed_share(order, *others, gathered, stats, dgateup, dfused, gu, qkv, far):
    width = gathered.shape[2]
    count = order.shape[0]
    step = 2 * LANES
    block = lambda k: pl.BlockSpec((1, LANES, width), lambda i, order: (order[2 * i + k], 0, 0))
    stat = lambda k: pl.BlockSpec((1, 8, LANES), lambda i, order: (order[2 * i + k], 0, 0))
    row = lambda x, k: pl.BlockSpec((LANES, x.shape[1]), lambda i, order: (order[2 * i + k], 0))
    if far:
        outs = [pl.BlockSpec((step, width), lambda i, order: (0, 0)) for _ in range(count // 2)]
        shapes = [jax.ShapeDtypeStruct((step, width), bf16) for _ in range(count // 2)]
    else:
        outs = [pl.BlockSpec((step, width), lambda i, order: (i, 0))]
        shapes = [jax.ShapeDtypeStruct((count * LANES, width), f32)]
    return pl.pallas_call(
        ignoring(dnormed_kernel, 11, len(others)),
        name="dn_far" if far else "dn_near",
        grid_spec=pltpu.PrefetchScalarGridSpec(
            num_scalar_prefetch=1,
            grid=(count // 2,),
            in_specs=[
                block(0),
                block(1),
                stat(0),
                stat(1),
                row(dgateup, 0),
                row(dgateup, 1),
                row(dfused, 0),
                row(dfused, 1),
                whole_block(gu),
                whole_block(qkv),
                *anywhere(others),
            ],
            out_specs=[*outs, pl.BlockSpec((8, width), lambda i, order: (0, 0))],
            scratch_shapes=[pltpu.VMEM((step, width), bf16)] if far else [],
        ),
        out_shape=[*shapes, jax.ShapeDtypeStruct((8, width), f32)],
        compiler_params=limits(60),
        cost_estimate=cost(
            2 * count * LANES * width * (dgateup.shape[1] + dfused.shape[1]), count * LANES * width * 8
        ),
    )(order, gathered, gathered, stats, stats, dgateup, dgateup, dfused, dfused, gu, qkv, *others)


def combine_kernel(near_ref, *refs):
    got_refs, sent_refs, keep_ref = refs[: len(refs) - 1 - (len(refs) - 1) // 3], refs[-1 - (len(refs) - 1) // 3 : -1], refs[-1]
    for i, got_ref in enumerate(got_refs):

        @pl.when(pl.program_id(0) == i)
        def _():
            total = near_ref[...] + got_ref[...].astype(f32)
            if i < len(sent_refs):
                sent_refs[i][...] = total.astype(bf16)
            else:
                keep_ref[...] = total


def combine(near, got, *others):
    rows, width = near.shape
    step = rows // len(got)
    sent = len(got) // 2
    fixed = pl.BlockSpec((step, width), lambda i: (0, 0))
    return pl.pallas_call(
        ignoring(combine_kernel, 1 + len(got), len(others)),
        name="combine",
        grid=(len(got),),
        in_specs=[pl.BlockSpec((step, width), lambda i: (i, 0)), *[fixed for _ in got], *anywhere(others)],
        out_specs=[fixed for _ in range(sent)] + [pl.BlockSpec((step, width), lambda i: (jnp.maximum(i - sent, 0), 0))],
        out_shape=[jax.ShapeDtypeStruct((step, width), bf16) for _ in range(sent)]
        + [jax.ShapeDtypeStruct((rows // 2, width), f32)],
        compiler_params=limits(48),
        cost_estimate=cost(0, rows * width * 9),
    )(near, *got, *others)


def add_kernel(keep_ref, got_ref, out_ref):
    out_ref[...] = (keep_ref[...] + got_ref[...].astype(f32)).astype(bf16)


def add_up(keep, got, *others):
    rows, width = keep.shape
    row = pl.BlockSpec((LANES, width), lambda i: (i, 0))
    return pl.pallas_call(
        ignoring(add_kernel, 2, len(others)),
        name="add_up",
        grid=(rows // LANES,),
        in_specs=[row, row, *anywhere(others)],
        out_specs=row,
        out_shape=jax.ShapeDtypeStruct((rows, width), bf16),
        compiler_params=limits(16),
        cost_estimate=cost(0, rows * width * 8),
    )(keep, got, *others)


def per_device(
    groups, outer, zs, ys, cs, tokens, segments, ln_gain, ln_bias, w_qkv, b_qkv, w_out, w_gateup, w_down, cotangent
):
    length, width = tokens.shape
    tp = zs * ys * cs
    shards = tp * outer
    z, y, c = (lax.axis_index(axis) for axis in TP)
    me = (z * ys + y) * cs + c

    own_ffn = w_gateup.shape[1] // 2 // tp
    wide = up_to(own_ffn, LANES)
    own_qkv = 3 * PAIR
    rows = w_qkv.shape[0]
    half = rows // groups
    part = lax.axis_index("replica")
    parts = part.astype(jnp.int32).reshape(1)
    steps = sorted(range(zs), key=lambda k: -min(k, zs - k))
    order = [
        jnp.stack(
            [
                (lax.rem(z + zs - k, zs) * ys + lax.rem(y + ys - j, ys)) * cs + lax.rem(c + cs - i, cs)
                for j in reversed(range(ys))
                for k in steps
            ]
        ).astype(jnp.int32)
        for i in range(cs)
    ]

    plain_order = [
        jnp.stack(
            [(k * ys + lax.rem(y + ys - j, ys)) * cs + lax.rem(c + cs - i, cs) for j in reversed(range(ys)) for k in range(zs)]
        ).astype(jnp.int32)
        for i in range(cs)
    ]

    tokens32 = tokens.astype(f32)
    mean = jnp.mean(tokens32, axis=1)
    centered = tokens32 - mean[:, None]
    inv_std = lax.rsqrt(jnp.mean(centered * centered, axis=1) + epsilon)
    small = jnp.concatenate(
        [ln_gain, ln_bias, b_qkv, segments[0].astype(bf16), *in_three(mean), *in_three(inv_std)]
    )
    of_params = 2 * rows + b_qkv.shape[0]
    small_rows = up_to(-(-small.shape[0] // width), 16)
    small_rows_of = jnp.pad(small, (0, small_rows * width - small.shape[0])).reshape(small_rows, width)
    packed = jnp.concatenate([tokens, small_rows_of], axis=0)
    gathered = lax.all_gather(packed, TP, axis=0, tiled=False)

    cotangent_all = lax.all_gather(cotangent, TP, axis=0, tiled=True)

    def other(own):
        return shifted(own, "replica", groups, 1)

    def to_columns(own):
        own = lax.all_to_all(own, TP, 0, 0, tiled=True)
        whole = jnp.zeros((tp, groups, half, own.shape[-1]), bf16)
        whole = lax.dynamic_update_slice(whole, own[:, None], (0, part, 0, 0))
        whole = lax.dynamic_update_slice(whole, other(own)[:, None], (0, 1 - part, 0, 0))
        whole = whole.reshape(tp, rows, own.shape[-1])
        if outer > 1:
            whole = lax.all_gather(whole, "outer", axis=1, tiled=False)
        return whole.reshape(width, own.shape[-1])

    gu_cols = to_columns(pack(w_gateup, parts, groups, 2, tp, own_ffn, wide))
    qkv_cols = to_columns(pack(w_qkv, parts, groups, 3, tp, PAIR, PAIR))
    if outer > 1:
        w_out = lax.all_gather(w_out, "outer", axis=0, tiled=True)
        w_down = lax.all_gather(w_down, "outer", axis=0, tiled=True)
    w_rows = jnp.concatenate([w_out, w_down, jnp.zeros((wide - own_ffn, width), bf16)], axis=0)

    vectors = gathered[:, length:, :].reshape(tp, -1)[:, : small.shape[0]]
    of_tokens = vectors[:, of_params:].reshape(tp, 7, length)
    seg_all = of_tokens[:, 0].astype(jnp.int32)
    of_tokens = of_tokens[:, 1:].astype(f32).reshape(tp, 2, 3, length)
    stats = jnp.pad(of_tokens[:, :, 0] + of_tokens[:, :, 1] + of_tokens[:, :, 2], ((0, 0), (0, 6), (0, 0)))
    vectors = vectors[:, :of_params]
    if outer > 1:
        vectors = lax.all_gather(vectors, "outer", axis=1, tiled=False)
    vectors = vectors.reshape(shards, -1)
    gain_all = vectors[:, :rows].reshape(1, width).astype(f32)
    bias_all = vectors[:, rows : 2 * rows].reshape(1, width).astype(f32)
    qkv_bias = vectors[:, 2 * rows :].reshape(3, tp, PAIR).astype(f32)
    my_bias = lax.dynamic_index_in_dim(qkv_bias, me, 1, keepdims=False).reshape(1, own_qkv)
    tables = rotary_tables(seg_all)

    normed, gate, up, hidden, joined = gate_forward(gathered, stats, gain_all, bias_all, gu_cols, qkv_cols)
    fused, context, probs = attend(joined, my_bias, tables, tp)
    branch_far = branches(plain_order[1], context, hidden, w_rows)[0]
    branch_sent, branch_keep = branches(plain_order[0], context, hidden, w_rows, shifted(branch_far, "c", cs, 1))
    branch_got = shifted(branch_sent, "y", ys, 1)

    dgateup, dcontext = gate_backward(cotangent_all, gate, up, w_rows, branch_sent)

    def grads_of(d, *others):
        if outer == 1:
            return split_grads(parts, normed, d, half, *others)
        mine, theirs = of_replicas(mm(normed, d, ((0,), (0,))))
        return mine, theirs.astype(bf16)

    def of_replicas(grads):
        if outer > 1:
            grads = lax.psum_scatter(grads.reshape(tp, outer, rows, -1), "outer", scatter_dimension=1, tiled=True)
        grads = grads.reshape(tp, groups, half, -1)
        mine = lax.dynamic_index_in_dim(grads, part, 1, keepdims=False)
        return mine, lax.dynamic_index_in_dim(grads, 1 - part, 1, keepdims=False)

    gu_mine, gu_theirs = grads_of(dgateup)
    gu_got = other(gu_theirs)
    dfused, bias_sums = attend_back(fused, probs, dcontext, tables, tp, gu_theirs)
    share = functools.partial(dnormed_share, gathered=gathered, stats=stats, dgateup=dgateup, dfused=dfused, gu=gu_cols, qkv=qkv_cols)
    branch = add_up(branch_keep, branch_got, dfused)
    branch_own = lax.psum_scatter(branch, "z", scatter_dimension=0, tiled=True)
    block_output = (tokens32 + branch_own.astype(f32)).astype(bf16)
    *far_shares, far_sums = share(order[1], branch, far=True)
    got = [shifted(far_share, "c", cs, 1) for far_share in far_shares]
    near_share, near_sums = share(order[0], *far_shares, far=False)
    gain_sum, bias_sum = near_sums[0] + far_sums[0], near_sums[1] + far_sums[1]

    per_row = own_qkv // half
    tiled_sums = jnp.broadcast_to(bias_sums.reshape(1, half, per_row), (width // half, half, per_row)).reshape(width, per_row)
    extra = jnp.concatenate(
        [gain_sum[:, None], bias_sum[:, None], tiled_sums, jnp.zeros((width, LANES - 2 - per_row), f32)], axis=1
    )
    mine, theirs = of_replicas(extra)
    extra = jnp.concatenate([mine[..., :2], theirs[..., :2], mine[..., 2 : 2 + per_row]], axis=2)
    extra = jnp.pad(extra, ((0, 0), (0, 0), (own_ffn, 2 * wide - own_ffn - 4 - per_row)))
    gu_total = (gu_mine + after(gu_got, near_share).astype(f32) + extra).astype(bf16)
    gu_own = lax.all_to_all(gu_total, TP, 0, 0, tiled=True)
    *sent, keep = combine(near_share, got, gu_total)
    qkv_mine, qkv_theirs = grads_of(dfused, *sent)
    qkv_got = other(qkv_theirs)
    rows_part = rows_grads(context, hidden, cotangent_all, PAIR + own_ffn, bf16 if outer == 1 else f32, qkv_theirs)
    if outer > 1:
        rows_out = lax.psum_scatter(rows_part[:PAIR], "outer", scatter_dimension=0, tiled=True)
        rows_down = lax.psum_scatter(rows_part[PAIR:], "outer", scatter_dimension=0, tiled=True)
        rows_part = jnp.concatenate([rows_out, rows_down], axis=0).astype(bf16)
    rows_got = other(rows_part)
    dnormed_own = 0.0
    leaving = []
    for i, pair in enumerate(sent):
        pair = shifted(after(pair, *leaving, rows_part) if leaving else pair, "y", ys, 1)
        at = 2 * i * length
        for j, k in enumerate(steps[2 * i : 2 * i + 2]):
            rows_at = slice(j * length, (j + 1) * length)
            term = keep[at : at + 2 * length][rows_at] + pair[rows_at].astype(f32)
            if k:
                leaving.append(term.astype(bf16))
                term = shifted(leaving[-1], "z", zs, zs - k).astype(f32)
            dnormed_own = dnormed_own + term
    inv = inv_std[:, None]
    xhat = centered * inv
    e = dnormed_own * gain_all
    tokens_back = inv * (e - jnp.mean(e, axis=1, keepdims=True) - xhat * jnp.mean(e * xhat, axis=1, keepdims=True))
    tokens_grad = (cotangent.astype(f32) + tokens_back).astype(bf16)
    qkv_total = (qkv_mine + qkv_got.astype(f32)).astype(bf16)
    qkv_total = after(qkv_total, gu_own, branch_own)
    qkv_own = lax.all_to_all(qkv_total, TP, 0, 0, tiled=True)
    gu_other = other(gu_own)
    gateup_grad = unpack(gu_own, gu_other, parts, 2, own_ffn, wide)
    qkv_grad = unpack(qkv_own, other(qkv_own), parts, 3, PAIR, PAIR)
    rows_grad = rows_part.astype(f32) + rows_got.astype(f32)
    sums_of = lambda x: jnp.sum(x[:, :, own_ffn : own_ffn + 4].astype(f32), axis=0)
    mine, theirs = sums_of(gu_own), sums_of(gu_other)
    here, there = mine[:, :2] + theirs[:, 2:], theirs[:, :2] + mine[:, 2:]
    first = part == 0
    own_sums = jnp.concatenate([jnp.where(first, here, there), jnp.where(first, there, here)], axis=0)
    bias_of = lambda x: x[:, :, own_ffn + 4 : own_ffn + 4 + per_row].reshape(tp, 3, PAIR).astype(f32)
    bias_grads = bias_of(gu_own) + bias_of(gu_other)
    bias_grads = bias_grads.transpose(1, 0, 2).reshape(-1)
    place = me * outer + lax.axis_index("outer")
    qkv_bias_grad = lax.dynamic_slice_in_dim(bias_grads, place * (3 * rows), 3 * rows, 0)
    return (
        block_output,
        tokens_grad,
        own_sums[:, 0],
        own_sums[:, 1],
        qkv_grad,
        qkv_bias_grad,
        rows_grad[: PAIR // outer],
        gateup_grad,
        rows_grad[PAIR // outer :],
    )


def solution(mesh):
    groups, shards = mesh.shape["replica"], mesh.shape["shard"]
    tp = math.gcd(shards, HEADS // 2)
    outer = shards // tp
    ys = cs = 2
    zs = tp // (ys * cs)
    inner_mesh = Mesh(mesh.devices.reshape(groups, zs, ys, cs, outer), ("replica", *TP, "outer"))
    everywhere = P(("replica", *TP, "outer"), None)
    vector = P((*TP, "outer"))
    matrix = P((*TP, "outer"), None)
    return jax.shard_map(
        functools.partial(per_device, groups, outer, zs, ys, cs),
        mesh=inner_mesh,
        in_specs=(everywhere, everywhere, vector, vector, matrix, vector, matrix, matrix, matrix, everywhere),
        out_specs=(everywhere, everywhere, vector, vector, matrix, vector, matrix, matrix, matrix),
        check_vma=False,
    )
```

time: 845 us -> 443 us (0.52); the launches traced: 834 us -> 441 us
  waiting for transfers between devices: 538 us -> 182 us
  Pallas kernels: 18.4 us -> 128 us
  matrix products: 71.5 us -> 0 us
  local copies, waits for them, and re-layouts: 87.2 us -> 36.5 us
  blocking collectives: 48.3 us -> 0 us
  starting transfers between devices: 12.6 us -> 45.2 us
  other arithmetic: 43.1 us -> 34.4 us
    psum x1 -> x0, waiting for transfers between devices: 174 us -> none  [per_device(): grads = lax.psum(grads, 'replica').astype(f32)]
    all_to_all x2 -> x4, waiting for transfers between devices: 237 us -> 95 us  [the longest x2 79.2 us: to_columns(): own = lax.all_to_all(own, TP, 0, 0, tiled=True)]
    pallas_call x2 -> x20, Pallas kernels: 18.4 us -> 128 us  [the longest x2 25.7 us: dnormed_share(): pl.pallas_call(ignoring(dnormed_kernel, 11, len(others)), name='dn_far' i...]
    dot_general x7 -> x0, matrix products: 71.5 us -> none  [mm(): return lax.dot_general(a, b, (dims, ((), ())), preferred_element_type=f32)]
    ppermute x0 -> x18, waiting for transfers between devices: none -> 69.6 us  [shifted(): return lax.ppermute(x, axis, [(i, (i + step) % size) for i in range(size)])]
    reduce_scatter x2 -> x1, waiting for transfers between devices: 56.3 us -> 0.01 us  [per_device(): branch_own = lax.psum_scatter(branch, 'z', scatter_dimension=0, tiled=True)]
    all_gather x2, waiting for transfers between devices: 70 us -> 17.1 us  [the longest x1 17.1 us: per_device(): cotangent_all = lax.all_gather(cotangent, TP, axis=0, tiled=True)]
    all_gather x1 -> x0, blocking collectives: 39.8 us -> none  [per_device(): lax.all_gather(bias_sums.reshape(3, PAIR), 'tp', axis=1, tiled=False)]
  transfers between devices with their start and end apart: 7 -> 25, of which waited for: 5 -> 12; matrix products, arithmetic and copies ran while one was open for 12% -> 11% of each run, Pallas kernels for 0% -> 28%
where the time goes in v2:
time: 443 us; the launch traced here: 441 us
  waiting for transfers between devices  182 us (41%)
  Pallas kernels  128 us (29%)
  starting transfers between devices  45.2 us (10%)
  local copies, waits for them, and re-layouts  36.5 us (8%)
  other arithmetic  34.4 us (8%)
  between operations  14.4 us (3%)
    all_to_all x2, waiting for transfers between devices, to_columns(): own = lax.all_to_all(own, TP, 0, 0, tiled=True)  79.2 us
    ppermute x18, waiting for transfers between devices, shifted(): return lax.ppermute(x, axis, [(i, (i + step) % size) for i in range(size)])  69.6 us
    pallas_call x2, Pallas kernels, dnormed_share(): pl.pallas_call(ignoring(dnormed_kernel, 11, len(others)), name='dn_far' i...  25.7 us
    pallas_call x2, Pallas kernels, split_grads(): pl.pallas_call(ignoring(grads_kernel, 3, len(others)), name='grads', grid...  19.9 us
    ppermute x18, starting transfers between devices, shifted(): return lax.ppermute(x, axis, [(i, (i + step) % size) for i in range(size)])  19.1 us
    unnamed x69, local copies, waits for them, and re-layouts  17.7 us
    pallas_call x1, Pallas kernels, gate_forward(): pl.pallas_call(gate_kernel, name='gate_fwd', grid=(count // 2,), in_specs...  17.5 us
    all_gather x1, waiting for transfers between devices, per_device(): cotangent_all = lax.all_gather(cotangent, TP, axis=0, tiled=True)  17.1 us
  transfers between devices with their start and end apart: 25, of which 12 were waited for; matrix products, arithmetic and copies ran while one was open for 11% of the time, Pallas kernels for 28%

profile of v2, /device:TPU:0, one launch (start us, length us, event | category | flops | bytes accessed | tf_op | source)
XLA Modules:
  0.0 440.9 jit_solution(14657178633068382509)
XLA Ops:
  14.6 1.9 pad_maximum_fusion
  17.3 2.0 pack.2
  19.3 7.5 %all-to-all-start = ((bf16[16,64,768]{2,1,0:T(8,128)(2,1)}), bf16[16,64,768]{2,1,0:T(8,128)(2,1)S(1)}, u32[]{:S(2)}, u32[]{:S(2)}) async-start(bf16[16,64,768]{2,1,0:T(8,128)(2,1)} %pack.2), calls=%async_computation | async-start | bytes 3145728 | tf_op jit(solution)/shard_map/all_to_all | solution.py:677
  28.4 49.3 %all-to-all-done = bf16[16,64,768]{2,1,0:T(8,128)(2,1)S(1)} async-done(((bf16[16,64,768]{2,1,0:T(8,128)(2,1)}), bf16[16,64,768]{2,1,0:T(8,128)(2,1)S(1)}, u32[]{:S(2)}, u32[]{:S(2)}) %all-to-all-start) | async-done | bytes 1572896 | tf_op jit(solution)/shard_map/all_to_all | solution.py:677
  77.7 9.3 %all-to-all-start.1 = ((bf16[16,64,384]{2,1,0:T(8,128)(2,1)}), bf16[16,64,384]{2,1,0:T(8,128)(2,1)S(1)}, u32[]{:S(2)}, u32[]{:S(2)}) async-start(bf16[16,64,384]{2,1,0:T(8,128)(2,1)} %pack.3), calls=%async_computation.1 | async-start | bytes 1572864 | tf_op jit(solution)/shard_map/all_to_all | solution.py:677
  88.5 29.9 %all-to-all-done.1 = bf16[16,64,384]{2,1,0:T(8,128)(2,1)S(1)} async-done(((bf16[16,64,384]{2,1,0:T(8,128)(2,1)}), bf16[16,64,384]{2,1,0:T(8,128)(2,1)S(1)}, u32[]{:S(2)}, u32[]{:S(2)}) %all-to-all-start.1) | async-done | bytes 786464 | tf_op jit(solution)/shard_map/all_to_all | solution.py:677
  119.9 3.2 maximum_maximum_fusion.w_ref.refs_3_
  123.5 17.2 %collective-permute-done.1 = bf16[16,64,384]{2,1,0:T(8,128)(2,1)} collective-permute-done((bf16[16,64,384]{2,1,0:T(8,128)(2,1)S(1)}, bf16[16,64,384]{2,1,0:T(8,128)(2,1)}, u32[]{:S(2)}, u32[]{:S(2)}) %collective-permute-start.1) | collective-permute-done | bytes 786464 | tf_op jit(solution)/shard_map/ppermute | solution.py:185
  142.0 2.2 broadcast_in_dim.91
  145.5 2.7 bitcast_dynamic-update-slice_fusion
  151.4 17.5 %gate_fwd.1 = (bf16[2048,2048]{1,0:T(8,128)(2,1)}, f32[2048,384]{1,0:T(8,128)}, f32[2048,384]{1,0:T(8,128)}, bf16[2048,384]{1,0:T(8,128)(2,1)}, f32[2048,384]{1,0:T(8,128)}) custom-call(bf16[16,144,2048]{2,1,0:T(8,128)(2,1)} %bitcast.82, bf16[16,144,2048]{2,1,0:T(8,128)(2,1)} %bitcast.83, f32[16,8,128]{2,1,0:T(8,128)} %pad.13.stats_ref.refs_3_.refs_4_, ...), custom_call_target="tpu_custom_call" | custom-call | flops 1 | bytes 1 | tf_op jit(solution)/shard_map/gate_fwd/pallas_call | solution.py:329
  170.0 3.8 fusion
  173.9 3.3 attend.1
  177.3 5.5 %branch_far.1 = bf16[1024,2048]{1,0:T(8,128)(2,1)} custom-call(s32[8]{0:T(128)S(1)} %stack.125.order_ref, bf16[2048,128]{1,0:T(8,128)(2,1)S(1)} %get-tuple-element.38.ac_ref.bc_ref.refs_0_, bf16[2048,128]{1,0:T(8,128)(2,1)S(1)} %get-tuple-element.38.ac_ref.bc_ref.refs_0_, bf16[2048,384]{1,0:T(8,128)(2,1)S(1)} %copy-done.1, bf16[2048,384]{1,0:T(8,128)(2,1)S(1)} %copy-done.1, ...), custom_call_target="tpu_custom_call" | custom-call | flops 1 | bytes 1 | tf_op jit(solution)/shard_map/branch_far/pallas_call | solution.py:389
  182.9 7.4 %collective-permute-done.2.refs_0_ = bf16[1024,2048]{1,0:T(8,128)(2,1)} collective-permute-done((bf16[1024,2048]{1,0:T(8,128)(2,1)}, bf16[1024,2048]{1,0:T(8,128)(2,1)}, u32[]{:S(2)}, u32[]{:S(2)}) %collective-permute-start.2) | collective-permute-done | bytes 4194336 | tf_op jit(solution)/shard_map/ppermute | solution.py:185
  190.3 8.9 %branch_near.1 = (bf16[512,2048]{1,0:T(8,128)(2,1)}, f32[512,2048]{1,0:T(8,128)}) custom-call(s32[8]{0:T(128)S(1)} %stack.116.order_ref, bf16[2048,128]{1,0:T(8,128)(2,1)S(1)} %get-tuple-element.38.ac_ref.bc_ref.refs_0_, bf16[2048,128]{1,0:T(8,128)(2,1)S(1)} %get-tuple-element.38.ac_ref.bc_ref.refs_0_, bf16[2048,384]{1,0:T(8,128)(2,1)S(1)} %copy-done.1, ...), custom_call_target="tpu_custom_call" | custom-call | flops 1 | bytes 1 | tf_op jit(solution)/shard_map/branch_near/pallas_call | solution.py:389
  200.4 17.1 %all-gather.4.cloned.1.call-done.refs_0_.refs_2_ = bf16[2048,2048]{1,0:T(8,128)(2,1)} async-done(((bf16[128,2048]{1,0:T(8,128)(2,1)}), bf16[2048,2048]{1,0:T(8,128)(2,1)}) %all-gather.4.cloned.1.call-update) | async-done | bytes 8388624 | tf_op jit(solution)/shard_map/all_gather | solution.py:671
  217.5 1.6 copy-done.3
  219.1 11.4 %gate_back.1 = (bf16[2048,768]{1,0:T(8,128)(2,1)}, bf16[2048,128]{1,0:T(8,128)(2,1)S(1)}) custom-call(bf16[2048,2048]{1,0:T(8,128)(2,1)} %all-gather.4.cloned.1.call-done.refs_0_.refs_2_, f32[2048,384]{1,0:T(8,128)} %get-tuple-element.44.refs_1_, f32[2048,384]{1,0:T(8,128)} %get-tuple-element.45.refs_2_, bf16[512,2048]{1,0:T(8,128)(2,1)S(1)} %copy-done.3, ...), custom_call_target="tpu_custom_call" | custom-call | flops 1 | bytes 1 | tf_op jit(solution)/shard_map/gate_back/pallas_call | solution.py:426
  230.5 11.2 %grads.2 = (f32[16,64,768]{2,1,0:T(8,128)}, bf16[16,64,768]{2,1,0:T(8,128)(2,1)}) custom-call(s32[1]{0:T(128)} %bitcast.14.part_ref.refs_0_, bf16[2048,2048]{1,0:T(8,128)(2,1)} %get-tuple-element.47.refs_1_, bf16[2048,768]{1,0:T(8,128)(2,1)} %get-tuple-element.48.refs_2_.refs_5_.refs_6_), custom_call_target="tpu_custom_call" | custom-call | flops 1 | bytes 1 | tf_op jit(solution)/shard_map/grads/pallas_call | solution.py:455
  251.3 5.4 %attend_back.1 = (bf16[2048,384]{1,0:T(8,128)(2,1)S(1)}, f32[1,384]{1,0:T(1,128)S(1)}) custom-call(bf16[2048,384]{1,0:T(8,128)(2,1)S(1)} %copy-done.19, f32[16,256,128]{2,1,0:T(8,128)S(1)} %copy-done.15, bf16[2048,128]{1,0:T(8,128)(2,1)S(1)} %get-tuple-element.46.refs_2_, f32[2048,128]{1,0:T(8,128)S(1)} %copy-done.9, f32[2048,128]{1,0:T(8,128)S(1)} %copy-done.7, ...), custom_call_target="tpu_custom_call" | custom-call | flops 536870912 | bytes 12288000 | tf_op jit(solution)/shard_map/attend_back/pallas_call | solution.py:164
  256.9 2.5 copy-done.11
  259.4 2.5 add_up.1.refs_11_
  263.2 13.2 %dn_far.1 = (bf16[256,2048]{1,0:T(8,128)(2,1)}, bf16[256,2048]{1,0:T(8,128)(2,1)}, bf16[256,2048]{1,0:T(8,128)(2,1)}, bf16[256,2048]{1,0:T(8,128)(2,1)}, f32[8,2048]{1,0:T(8,128)}) custom-call(s32[8]{0:T(128)} %stack.143.refs_0_, bf16[16,144,2048]{2,1,0:T(8,128)(2,1)} %bitcast.84, bf16[16,144,2048]{2,1,0:T(8,128)(2,1)} %bitcast.85, ...), custom_call_target="tpu_custom_call" | custom-call | flops 1 | bytes 1 | tf_op jit(solution)/shard_map/dn_far/pallas_call | solution.py:543
  277.6 12.5 %dn_near.1 = (f32[1024,2048]{1,0:T(8,128)}, f32[8,2048]{1,0:T(8,128)}) custom-call(s32[8]{0:T(128)} %stack.134.refs_0_, bf16[16,144,2048]{2,1,0:T(8,128)(2,1)} %bitcast.86, bf16[16,144,2048]{2,1,0:T(8,128)(2,1)} %bitcast.87, f32[16,8,128]{2,1,0:T(8,128)} %pad.13.stats_ref.refs_3_.refs_4_, f32[16,8,128]{2,1,0:T(8,128)} %pad.13.stats_ref.refs_3_.refs_4_, ...), custom_call_target="tpu_custom_call" | custom-call | flops 1 | bytes 1 | tf_op jit(solution)/shard_map/dn_near/pallas_call | solution.py:543
  292.7 4.3 add_convert_fusion.refs_5_
  297.0 4.4 %all-to-all-start.2 = ((bf16[16,64,768]{2,1,0:T(8,128)(2,1)}), bf16[16,64,768]{2,1,0:T(8,128)(2,1)}, u32[]{:S(2)}, u32[]{:S(2)}) async-start(bf16[16,64,768]{2,1,0:T(8,128)(2,1)} %add_convert_fusion.refs_5_), calls=%async_computation.3 | async-start | bytes 3145728 | tf_op jit(solution)/shard_map/all_to_all | solution.py:750
  301.5 6.0 %combine.1 = (bf16[256,2048]{1,0:T(8,128)(2,1)S(1)}, bf16[256,2048]{1,0:T(8,128)(2,1)S(1)}, f32[512,2048]{1,0:T(8,128)}) custom-call(f32[1024,2048]{1,0:T(8,128)} %get-tuple-element.55.refs_1_.refs_0_, bf16[256,2048]{1,0:T(8,128)(2,1)S(1)} %collective-permute-done.4.refs_1_, bf16[256,2048]{1,0:T(8,128)(2,1)S(1)} %collective-permute-done.5.refs_2_, ...), custom_call_target="tpu_custom_call" | custom-call | flops 1 | bytes 1 | tf_op jit(solution)/shard_map/combine/pallas_call | solution.py:591
  308.5 1.8 collective-permute-start.9
  310.3 8.7 %grads.3 = (f32[16,64,384]{2,1,0:T(8,128)}, bf16[16,64,384]{2,1,0:T(8,128)(2,1)}) custom-call(s32[1]{0:T(128)} %bitcast.14.part_ref.refs_0_, bf16[2048,2048]{1,0:T(8,128)(2,1)} %get-tuple-element.47.refs_1_, bf16[2048,384]{1,0:T(8,128)(2,1)} %copy-done, bf16[256,2048]{1,0:T(8,128)(2,1)} %copy-done.20, bf16[256,2048]{1,0:T(8,128)(2,1)} %copy-done.10), custom_call_target="tpu_custom_call" | custom-call | flops 1 | bytes 1 | tf_op jit(solution)/shard_map/grads/pallas_call | solution.py:455
  319.4 9.0 %rows.1.refs_3_ = bf16[480,2048]{1,0:T(8,128)(2,1)} custom-call(bf16[2048,128]{1,0:T(8,128)(2,1)} %copy-done.5, bf16[2048,384]{1,0:T(8,128)(2,1)} %get-tuple-element.39.ah_ref.bh_ref.refs_1_, bf16[2048,2048]{1,0:T(8,128)(2,1)} %all-gather.4.cloned.1.call-done.refs_0_.refs_2_, bf16[16,64,384]{2,1,0:T(8,128)(2,1)} %get-tuple-element.63.refs_3_), custom_call_target="tpu_custom_call" | custom-call | flops 1 | bytes 1 | tf_op jit(solution)/shard_map/rows/pallas_call | solution.py:484
  329.7 14.0 %collective-permute-done.9 = bf16[256,2048]{1,0:T(8,128)(2,1)S(1)} collective-permute-done((bf16[256,2048]{1,0:T(8,128)(2,1)S(1)}, bf16[256,2048]{1,0:T(8,128)(2,1)S(1)}, u32[]{:S(2)}, u32[]{:S(2)}) %collective-permute-start.9) | collective-permute-done | bytes 1048608 | tf_op jit(solution)/shard_map/ppermute | solution.py:185
  345.0 2.2 collective-permute-start.12
  348.3 2.3 collective-permute-start.10
  353.7 16.9 %collective-permute-done.12 = bf16[256,2048]{1,0:T(8,128)(2,1)} collective-permute-done((bf16[256,2048]{1,0:T(8,128)(2,1)}, bf16[256,2048]{1,0:T(8,128)(2,1)}, u32[]{:S(2)}, u32[]{:S(2)}) %collective-permute-start.12) | collective-permute-done | bytes 1048608 | tf_op jit(solution)/shard_map/ppermute | solution.py:185
  370.6 2.3 add_convert_fusion.2
  374.4 4.8 %all-to-all-start.3 = ((bf16[16,64,384]{2,1,0:T(8,128)(2,1)}), bf16[16,64,384]{2,1,0:T(8,128)(2,1)S(1)}, u32[]{:S(2)}, u32[]{:S(2)}) async-start(bf16[16,64,384]{2,1,0:T(8,128)(2,1)} %after.5), calls=%async_computation.4 | async-start | bytes 1572864 | tf_op jit(solution)/shard_map/all_to_all | solution.py:779
  379.3 2.6 collective-permute-done.17
  381.8 2.9 convert_add_fusion
  384.7 1.9 slice.189
  387.7 2.3 collective-permute-done.13
  389.9 2.5 fusion.29
  394.0 15.8 %all-to-all-done.3.own_ref = bf16[16,64,384]{2,1,0:T(8,128)(2,1)S(1)} async-done(((bf16[16,64,384]{2,1,0:T(8,128)(2,1)}), bf16[16,64,384]{2,1,0:T(8,128)(2,1)S(1)}, u32[]{:S(2)}, u32[]{:S(2)}) %all-to-all-start.3) | async-done | bytes 786464 | tf_op jit(solution)/shard_map/all_to_all | solution.py:779
  410.6 3.7 collective-permute-done.14.other_ref
  414.3 1.9 convert_add_fusion.2
  416.3 6.1 %unpack.3 = f32[128,11264]{1,0:T(8,128)} custom-call(s32[1]{0:T(128)} %bitcast.14.part_ref.refs_0_, bf16[16,64,768]{2,1,0:T(8,128)(2,1)} %all-to-all-done.2.refs_1_.own_ref, bf16[16,64,768]{2,1,0:T(8,128)(2,1)S(1)} %collective-permute-done.14.other_ref), custom_call_target="tpu_custom_call" | custom-call | flops 1 | bytes 1 | tf_op jit(solution)/shard_map/unpack/pallas_call | solution.py:289
  425.3 5.6 %collective-permute-done.16.other_ref = bf16[16,64,384]{2,1,0:T(8,128)(2,1)S(1)} collective-permute-done((bf16[16,64,384]{2,1,0:T(8,128)(2,1)S(1)}, bf16[16,64,384]{2,1,0:T(8,128)(2,1)S(1)}, u32[]{:S(2)}, u32[]{:S(2)}) %collective-permute-start.16) | collective-permute-done | bytes 786464 | tf_op jit(solution)/shard_map/ppermute | solution.py:185
  430.9 3.4 unpack.2
  (178 shorter events, 52.3 us)
Async XLA Ops:
  7.2 10.1 %copy-start.13 = (bf16[128,11264]{1,0:T(8,128)(2,1)S(1)}, bf16[128,11264]{1,0:T(8,128)(2,1)}, u32[]{:S(2)}) copy-start(bf16[128,11264]{1,0:T(8,128)(2,1)} %own_ref.2) | copy-start | bytes 8650756
  7.2 141.0 %all-gather.6.cloned.1.call-start = ((), (), s32[]{:S(2)}) async-start(), calls=%async_computation.7 | async-start | bytes 10027008 | tf_op jit(solution)/shard_map/all_gather | solution.py:669
  16.5 201.0 %all-gather.4.cloned.1.call-start = ((), (), s32[]{:S(2)}) async-start(), calls=%async_computation.5 | async-start | bytes 8912896 | tf_op jit(solution)/shard_map/all_gather | solution.py:671
  19.3 7.5 %copy-start.16 = (bf16[128,6144]{1,0:T(8,128)(2,1)S(1)}, bf16[128,6144]{1,0:T(8,128)(2,1)}, u32[]{:S(2)}) copy-start(bf16[128,6144]{1,0:T(8,128)(2,1)} %own_ref.3) | copy-start | bytes 4718596
  19.3 58.3 %all-to-all-start = ((bf16[16,64,768]{2,1,0:T(8,128)(2,1)}), bf16[16,64,768]{2,1,0:T(8,128)(2,1)S(1)}, u32[]{:S(2)}, u32[]{:S(2)}) async-start(bf16[16,64,768]{2,1,0:T(8,128)(2,1)} %pack.2), calls=%async_computation | async-start | bytes 3145728 | tf_op jit(solution)/shard_map/all_to_all | solution.py:677
  77.7 40.7 %all-to-all-start.1 = ((bf16[16,64,384]{2,1,0:T(8,128)(2,1)}), bf16[16,64,384]{2,1,0:T(8,128)(2,1)S(1)}, u32[]{:S(2)}, u32[]{:S(2)}) async-start(bf16[16,64,384]{2,1,0:T(8,128)(2,1)} %pack.3), calls=%async_computation.1 | async-start | bytes 1572864 | tf_op jit(solution)/shard_map/all_to_all | solution.py:677
  86.9 287.5 %reduce-scatter.2.cloned.1.call-start = ((), (), s32[]{:S(2)}) async-start(), calls=%async_computation.6 | async-start | bytes 2621440 | tf_op jit(solution)/shard_map/reduce_scatter | solution.py:734
  87.0 58.5 %collective-permute-start = (bf16[16,64,768]{2,1,0:T(8,128)(2,1)S(1)}, bf16[16,64,768]{2,1,0:T(8,128)(2,1)}, u32[]{:S(2)}, u32[]{:S(2)}) collective-permute-start(bf16[16,64,768]{2,1,0:T(8,128)(2,1)S(1)} %all-to-all-done), channel_id=1, source_target_pairs={{0,16},{16,0},{1,17},{17,1},{2,18},{18,2},{3,19},{19,3},{4,20},{20... | collective-permute-start | bytes 4718600 | tf_op jit(solution)/shard_map/ppermute | solution.py:185
  118.3 22.4 %collective-permute-start.1 = (bf16[16,64,384]{2,1,0:T(8,128)(2,1)S(1)}, bf16[16,64,384]{2,1,0:T(8,128)(2,1)}, u32[]{:S(2)}, u32[]{:S(2)}) collective-permute-start(bf16[16,64,384]{2,1,0:T(8,128)(2,1)S(1)} %all-to-all-done.1), channel_id=1, source_target_pairs={{0,16},{16,0},{1,17},{17,1},{2,18},{18,2},{3,19},{19,3},{4,20},{20... | collective-permute-start | bytes 2359304 | tf_op jit(solution)/shard_map/ppermute | solution.py:185
  142.0 3.4 copy-start.21
  169.7 4.2 copy-start.12
  173.9 3.4 copy-start.6
  173.9 3.4 copy-start.8
  173.9 3.4 copy-start.1
  173.9 3.4 copy-start.2
  177.3 5.5 %copy-start.14 = (f32[16,256,128]{2,1,0:T(8,128)}, f32[16,256,128]{2,1,0:T(8,128)S(1)}, u32[]{:S(2)}) copy-start(f32[16,256,128]{2,1,0:T(8,128)S(1)} %get-tuple-element.43.refs_1_) | copy-start | bytes 6291460
  177.3 5.5 %copy-start.18 = (bf16[2048,384]{1,0:T(8,128)(2,1)}, bf16[2048,384]{1,0:T(8,128)(2,1)S(1)}, u32[]{:S(2)}) copy-start(bf16[2048,384]{1,0:T(8,128)(2,1)S(1)} %get-tuple-element.42.refs_0_) | copy-start | bytes 4718596
  177.3 13.0 %copy-start.5 = (bf16[2048,128]{1,0:T(8,128)(2,1)}, bf16[2048,128]{1,0:T(8,128)(2,1)S(1)}, u32[]{:S(2)}) copy-start(bf16[2048,128]{1,0:T(8,128)(2,1)S(1)} %get-tuple-element.38.ac_ref.bc_ref.refs_0_) | copy-start | bytes 1572868
  182.8 7.5 %collective-permute-start.2 = (bf16[1024,2048]{1,0:T(8,128)(2,1)}, bf16[1024,2048]{1,0:T(8,128)(2,1)}, u32[]{:S(2)}, u32[]{:S(2)}) collective-permute-start(bf16[1024,2048]{1,0:T(8,128)(2,1)} %branch_far.1), channel_id=1, source_target_pairs={{0,1},{1,0},{2,3},{3,2},{4,5},{5,4},{6,7},{7,6},{8,9},{9,8},{10,11... | collective-permute-start | bytes 12582920 | tf_op jit(solution)/shard_map/ppermute | solution.py:185
  199.2 57.7 %collective-permute-start.3 = (bf16[512,2048]{1,0:T(8,128)(2,1)}, bf16[512,2048]{1,0:T(8,128)(2,1)}, u32[]{:S(2)}, u32[]{:S(2)}) collective-permute-start(bf16[512,2048]{1,0:T(8,128)(2,1)} %get-tuple-element.41.refs_4_), channel_id=1, source_target_pairs={{0,2},{2,0},{1,3},{3,1},{4,6},{6,4},{5,7},{7,5},{8,10},{10,8},{9,1... | collective-permute-start | bytes 6291464 | tf_op jit(solution)/shard_map/ppermute | solution.py:185
  217.5 1.6 copy-start.3
  241.7 51.0 %collective-permute-start.8 = (bf16[16,64,768]{2,1,0:T(8,128)(2,1)}, bf16[16,64,768]{2,1,0:T(8,128)(2,1)}, u32[]{:S(2)}, u32[]{:S(2)}) collective-permute-start(bf16[16,64,768]{2,1,0:T(8,128)(2,1)} %get-tuple-element.49.refs_6_), channel_id=1, source_target_pairs={{0,16},{16,0},{1,17},{17,1},{2,18},{18,2},{3,19},{19,3},{4,20},{20... | collective-permute-start | bytes 4718600 | tf_op jit(solution)/shard_map/ppermute | solution.py:185
  246.9 1.6 copy-start.15
  256.7 5.2 %copy-start = (bf16[2048,384]{1,0:T(8,128)(2,1)}, bf16[2048,384]{1,0:T(8,128)(2,1)S(1)}, u32[]{:S(2)}) copy-start(bf16[2048,384]{1,0:T(8,128)(2,1)S(1)} %get-tuple-element.50.refs_2_.refs_7_.refs_8_) | copy-start | bytes 4718596
  256.9 2.5 copy-start.11
  276.5 25.0 %collective-permute-start.4 = (bf16[256,2048]{1,0:T(8,128)(2,1)}, bf16[256,2048]{1,0:T(8,128)(2,1)S(1)}, u32[]{:S(2)}, u32[]{:S(2)}) collective-permute-start(bf16[256,2048]{1,0:T(8,128)(2,1)} %get-tuple-element.51.refs_11_), channel_id=1, source_target_pairs={{0,1},{1,0},{2,3},{3,2},{4,5},{5,4},{6,7},{7,6},{8,9},{9,8},{10,11... | collective-permute-start | bytes 3145736 | tf_op jit(solution)/shard_map/ppermute | solution.py:185
  276.6 24.9 %collective-permute-start.5 = (bf16[256,2048]{1,0:T(8,128)(2,1)}, bf16[256,2048]{1,0:T(8,128)(2,1)S(1)}, u32[]{:S(2)}, u32[]{:S(2)}) collective-permute-start(bf16[256,2048]{1,0:T(8,128)(2,1)} %get-tuple-element.52.refs_12_), channel_id=1, source_target_pairs={{0,1},{1,0},{2,3},{3,2},{4,5},{5,4},{6,7},{7,6},{8,9},{9,8},{10,11... | collective-permute-start | bytes 3145736 | tf_op jit(solution)/shard_map/ppermute | solution.py:185
  277.1 24.4 %collective-permute-start.6 = (bf16[256,2048]{1,0:T(8,128)(2,1)}, bf16[256,2048]{1,0:T(8,128)(2,1)S(1)}, u32[]{:S(2)}, u32[]{:S(2)}) collective-permute-start(bf16[256,2048]{1,0:T(8,128)(2,1)} %get-tuple-element.53.refs_13_), channel_id=1, source_target_pairs={{0,1},{1,0},{2,3},{3,2},{4,5},{5,4},{6,7},{7,6},{8,9},{9,8},{10,11... | collective-permute-start | bytes 3145736 | tf_op jit(solution)/shard_map/ppermute | solution.py:185
  277.2 24.3 %collective-permute-start.7 = (bf16[256,2048]{1,0:T(8,128)(2,1)}, bf16[256,2048]{1,0:T(8,128)(2,1)}, u32[]{:S(2)}, u32[]{:S(2)}) collective-permute-start(bf16[256,2048]{1,0:T(8,128)(2,1)} %get-tuple-element.54.refs_14_), channel_id=1, source_target_pairs={{0,1},{1,0},{2,3},{3,2},{4,5},{5,4},{6,7},{7,6},{8,9},{9,8},{10,11... | collective-permute-start | bytes 3145736 | tf_op jit(solution)/shard_map/ppermute | solution.py:185
  297.0 55.1 %all-to-all-start.2 = ((bf16[16,64,768]{2,1,0:T(8,128)(2,1)}), bf16[16,64,768]{2,1,0:T(8,128)(2,1)}, u32[]{:S(2)}, u32[]{:S(2)}) async-start(bf16[16,64,768]{2,1,0:T(8,128)(2,1)} %add_convert_fusion.refs_5_), calls=%async_computation.3 | async-start | bytes 3145728 | tf_op jit(solution)/shard_map/all_to_all | solution.py:750
  308.5 1.8 copy-start.20
  308.5 35.2 %collective-permute-start.9 = (bf16[256,2048]{1,0:T(8,128)(2,1)S(1)}, bf16[256,2048]{1,0:T(8,128)(2,1)S(1)}, u32[]{:S(2)}, u32[]{:S(2)}) collective-permute-start(bf16[256,2048]{1,0:T(8,128)(2,1)S(1)} %get-tuple-element.61.refs_3_), channel_id=1, source_target_pairs={{0,2},{2,0},{1,3},{3,1},{4,6},{6,4},{5,7},{7,5},{8,10},{10,8},{9,1... | collective-permute-start | bytes 3145736 | tf_op jit(solution)/shard_map/ppermute | solution.py:185
  319.0 24.8 %copy-start.23 = (f32[512,2048]{1,0:T(8,128)S(1)}, f32[512,2048]{1,0:T(8,128)}, u32[]{:S(2)}) copy-start(f32[512,2048]{1,0:T(8,128)} %get-tuple-element.60) | copy-start | bytes 12582916
  319.0 28.2 %collective-permute-start.15 = (bf16[16,64,384]{2,1,0:T(8,128)(2,1)}, bf16[16,64,384]{2,1,0:T(8,128)(2,1)S(1)}, u32[]{:S(2)}, u32[]{:S(2)}) collective-permute-start(bf16[16,64,384]{2,1,0:T(8,128)(2,1)} %get-tuple-element.63.refs_3_), channel_id=1, source_target_pairs={{0,16},{16,0},{1,17},{17,1},{2,18},{18,2},{3,19},{19,3},{4,20},{20... | collective-permute-start | bytes 2359304 | tf_op jit(solution)/shard_map/ppermute | solution.py:185
  328.4 53.4 %collective-permute-start.17 = (bf16[480,2048]{1,0:T(8,128)(2,1)}, bf16[480,2048]{1,0:T(8,128)(2,1)}, u32[]{:S(2)}, u32[]{:S(2)}) collective-permute-start(bf16[480,2048]{1,0:T(8,128)(2,1)} %rows.1.refs_3_), channel_id=1, source_target_pairs={{0,16},{16,0},{1,17},{17,1},{2,18},{18,2},{3,19},{19,3},{4,20},{20... | collective-permute-start | bytes 5898248 | tf_op jit(solution)/shard_map/ppermute | solution.py:185
  345.0 2.2 copy-start.28
  345.0 3.3 copy-start.27
  345.0 5.6 %copy-start.26 = (bf16[128,2048]{1,0:T(8,128)(2,1)S(1)}, bf16[128,2048]{1,0:T(8,128)(2,1)}, u32[]{:S(2)}) copy-start(bf16[128,2048]{1,0:T(8,128)(2,1)} %get-tuple-element.72.refs_2_) | copy-start | bytes 1572868
  345.0 25.6 %collective-permute-start.12 = (bf16[256,2048]{1,0:T(8,128)(2,1)}, bf16[256,2048]{1,0:T(8,128)(2,1)}, u32[]{:S(2)}, u32[]{:S(2)}) collective-permute-start(bf16[256,2048]{1,0:T(8,128)(2,1)} %after.4), channel_id=1, source_target_pairs={{0,2},{2,0},{1,3},{3,1},{4,6},{6,4},{5,7},{7,5},{8,10},{10,8},{9,1... | collective-permute-start | bytes 3145736 | tf_op jit(solution)/shard_map/ppermute | solution.py:185
  348.3 39.4 %collective-permute-start.10 = (bf16[128,2048]{1,0:T(8,128)(2,1)S(1)}, bf16[128,2048]{1,0:T(8,128)(2,1)}, u32[]{:S(2)}, u32[]{:S(2)}) collective-permute-start(bf16[128,2048]{1,0:T(8,128)(2,1)S(1)} %copy-done.27), channel_id=1, source_target_pairs={{0,8},{4,12},{8,0},{12,4},{1,9},{5,13},{9,1},{13,5},{2,10},{6,14},... | collective-permute-start | bytes 1572872 | tf_op jit(solution)/shard_map/ppermute | solution.py:185
  350.6 37.1 %collective-permute-start.11 = (bf16[128,2048]{1,0:T(8,128)(2,1)S(1)}, bf16[128,2048]{1,0:T(8,128)(2,1)}, u32[]{:S(2)}, u32[]{:S(2)}) collective-permute-start(bf16[128,2048]{1,0:T(8,128)(2,1)S(1)} %copy-done.26), channel_id=1, source_target_pairs={{0,12},{4,0},{8,4},{12,8},{1,13},{5,1},{9,5},{13,9},{2,14},{6,2},{... | collective-permute-start | bytes 1572872 | tf_op jit(solution)/shard_map/ppermute | solution.py:185
  352.2 62.1 %collective-permute-start.14 = (bf16[16,64,768]{2,1,0:T(8,128)(2,1)}, bf16[16,64,768]{2,1,0:T(8,128)(2,1)S(1)}, u32[]{:S(2)}, u32[]{:S(2)}) collective-permute-start(bf16[16,64,768]{2,1,0:T(8,128)(2,1)} %all-to-all-done.2.refs_1_.own_ref), channel_id=1, source_target_pairs={{0,16},{16,0},{1,17},{17,1},{2,18},{18,2},{3,19},{19,3},{4,20},{20... | collective-permute-start | bytes 4718600 | tf_op jit(solution)/shard_map/ppermute | solution.py:185
  372.9 17.1 %collective-permute-start.13 = (bf16[128,2048]{1,0:T(8,128)(2,1)}, bf16[128,2048]{1,0:T(8,128)(2,1)}, u32[]{:S(2)}, u32[]{:S(2)}) collective-permute-start(bf16[128,2048]{1,0:T(8,128)(2,1)} %add_convert_fusion.2), channel_id=1, source_target_pairs={{0,4},{4,8},{8,12},{12,0},{1,5},{5,9},{9,13},{13,1},{2,6},{6,10},{... | collective-permute-start | bytes 1572872 | tf_op jit(solution)/shard_map/ppermute | solution.py:185
  374.4 35.4 %all-to-all-start.3 = ((bf16[16,64,384]{2,1,0:T(8,128)(2,1)}), bf16[16,64,384]{2,1,0:T(8,128)(2,1)S(1)}, u32[]{:S(2)}, u32[]{:S(2)}) async-start(bf16[16,64,384]{2,1,0:T(8,128)(2,1)} %after.5), calls=%async_computation.4 | async-start | bytes 1572864 | tf_op jit(solution)/shard_map/all_to_all | solution.py:779
  386.6 3.3 copy-start.22
  389.9 2.5 copy-start.24
  389.9 2.5 copy-start.25
  409.8 21.1 %collective-permute-start.16 = (bf16[16,64,384]{2,1,0:T(8,128)(2,1)S(1)}, bf16[16,64,384]{2,1,0:T(8,128)(2,1)S(1)}, u32[]{:S(2)}, u32[]{:S(2)}) collective-permute-start(bf16[16,64,384]{2,1,0:T(8,128)(2,1)S(1)} %all-to-all-done.3.own_ref), channel_id=1, source_target_pairs={{0,16},{16,0},{1,17},{17,1},{2,18},{18,2},{3,19},{19,3},{4,20},{20... | collective-permute-start | bytes 2359304 | tf_op jit(solution)/shard_map/ppermute | solution.py:185
  (6 other events, 7.6 us)
Sparse Core Ops, SparseCore 0:
  16.7 124.6 all-gather.5
  143.5 73.9 all-gather.3
  263.4 41.2 reduce-scatter.1

commit v3 on v2

--- a/solution.py
+++ b/solution.py
@@ -252,29 +252,6 @@
     return lambda *refs: kernel(*refs[:at], *refs[at + count :])
 
 
-def in_three(x):
-    parts = []
-    for _ in range(3):
-        low = lax.reduce_precision(x, 8, 7)
-        parts.append(low.astype(bf16))
-        x = x - low
-    return parts
-
-
-def as_column(row):
-    n = row.shape[1]
-    square = lax.broadcasted_iota(jnp.int32, (n, n), 0) == lax.broadcasted_iota(jnp.int32, (n, n), 1)
-    return jnp.sum(jnp.where(square, row, 0.0), axis=1, keepdims=True)
-
-
-def normal_of(a_ref, b_ref, stats_ref):
-    parts = []
-    for k, ref in enumerate((a_ref, b_ref)):
-        mean, inv_std = as_column(stats_ref[k, 0:1, :]), as_column(stats_ref[k, 1:2, :])
-        parts.append((ref[0].astype(f32) - mean) * inv_std)
-    return jnp.concatenate(parts, axis=0)
-
-
 def unpack_kernel(part_ref, own_ref, other_ref, out_ref, *, sections, tp, size, wide):
     got = jnp.where(pl.program_id(0) == 0, own_ref[...], other_ref[...])
     for section in range(sections):
@@ -307,9 +284,15 @@
 
 
 def gate_kernel(
-    a_ref, b_ref, stats_ref, gain_ref, bias_ref, gu_ref, qkv_ref, normed_ref, gate_ref, up_ref, hidden_ref, joined_ref
+    a_ref, b_ref, gain_ref, bias_ref, gu_ref, qkv_ref, stats_ref, normed_ref, gate_ref, up_ref, hidden_ref, joined_ref
 ):
-    normed = (normal_of(a_ref, b_ref, stats_ref) * gain_ref[...] + bias_ref[...]).astype(bf16)
+    x = jnp.concatenate([a_ref[0], b_ref[0]], axis=0).astype(f32)
+    mean = jnp.mean(x, axis=1, keepdims=True)
+    centered = x - mean
+    inv_std = lax.rsqrt(jnp.mean(centered * centered, axis=1, keepdims=True) + epsilon)
+    lane = lax.broadcasted_iota(jnp.int32, stats_ref.shape, 1)
+    stats_ref[...] = jnp.where(lane == 0, mean, inv_std)
+    normed = (centered * inv_std * gain_ref[...] + bias_ref[...]).astype(bf16)
     normed_ref[...] = normed
     wide = gate_ref.shape[1]
     gateup = mm(normed, gu_ref[...], ((1,), (0,)))
@@ -320,7 +303,7 @@
     joined_ref[...] = mm(normed, qkv_ref[...], ((1,), (0,)))
 
 
-def gate_forward(gathered, stats, gain, bias, gu, qkv):
+def gate_forward(gathered, gain, bias, gu, qkv):
     count, padded, width = gathered.shape
     length, wide = LANES, gu.shape[1] // 2
     tokens = count * length
@@ -333,14 +316,14 @@
         in_specs=[
             block(0),
             block(1),
-            pl.BlockSpec((2, 8, length), lambda i: (i, 0, 0)),
             whole_block(gain),
             whole_block(bias),
             whole_block(gu),
             whole_block(qkv),
         ],
-        out_specs=[row(width), row(wide), row(wide), row(wide), row(3 * PAIR)],
+        out_specs=[row(LANES), row(width), row(wide), row(wide), row(wide), row(3 * PAIR)],
         out_shape=[
+            jax.ShapeDtypeStruct((tokens, LANES), f32),
             jax.ShapeDtypeStruct((tokens, width), bf16),
             jax.ShapeDtypeStruct((tokens, wide), f32),
             jax.ShapeDtypeStruct((tokens, wide), f32),
@@ -349,7 +332,7 @@
         ],
         compiler_params=limits(56),
         cost_estimate=cost(2 * tokens * width * (2 * wide + 3 * PAIR), tokens * (4 * width + 10 * wide + 12 * PAIR)),
-    )(gathered, gathered, stats, gain, bias, gu, qkv)
+    )(gathered, gathered, gain, bias, gu, qkv)
 
 
 def branch_kernel(far, order_ref, ac_ref, bc_ref, ah_ref, bh_ref, w_ref, *refs):
@@ -508,8 +491,8 @@
     def _():
         sums_ref[...] = jnp.zeros_like(sums_ref)
 
-    means = [as_column(ref[0, 0:1, :]) for ref in (as_ref, bs_ref)]
-    stds = [as_column(ref[0, 1:2, :]) for ref in (as_ref, bs_ref)]
+    means = [ref[:, 0:1] for ref in (as_ref, bs_ref)]
+    stds = [ref[:, 1:2] for ref in (as_ref, bs_ref)]
     width = gu_ref.shape[0]
     for at in range(0, width, CHUNK):
         cols = pl.ds(at, CHUNK)
@@ -532,7 +515,6 @@
     count = order.shape[0]
     step = 2 * LANES
     block = lambda k: pl.BlockSpec((1, LANES, width), lambda i, order: (order[2 * i + k], 0, 0))
-    stat = lambda k: pl.BlockSpec((1, 8, LANES), lambda i, order: (order[2 * i + k], 0, 0))
     row = lambda x, k: pl.BlockSpec((LANES, x.shape[1]), lambda i, order: (order[2 * i + k], 0))
     if far:
         outs = [pl.BlockSpec((step, width), lambda i, order: (0, 0)) for _ in range(count // 2)]
@@ -549,8 +531,8 @@
             in_specs=[
                 block(0),
                 block(1),
-                stat(0),
-                stat(1),
+                row(stats, 0),
+                row(stats, 1),
                 row(dgateup, 0),
                 row(dgateup, 1),
                 row(dfused, 0),
@@ -655,13 +637,7 @@
         for i in range(cs)
     ]
 
-    tokens32 = tokens.astype(f32)
-    mean = jnp.mean(tokens32, axis=1)
-    centered = tokens32 - mean[:, None]
-    inv_std = lax.rsqrt(jnp.mean(centered * centered, axis=1) + epsilon)
-    small = jnp.concatenate(
-        [ln_gain, ln_bias, b_qkv, segments[0].astype(bf16), *in_three(mean), *in_three(inv_std)]
-    )
+    small = jnp.concatenate([ln_gain, ln_bias, b_qkv, segments[0].astype(bf16)])
     of_params = 2 * rows + b_qkv.shape[0]
     small_rows = up_to(-(-small.shape[0] // width), 16)
     small_rows_of = jnp.pad(small, (0, small_rows * width - small.shape[0])).reshape(small_rows, width)
@@ -691,10 +667,7 @@
     w_rows = jnp.concatenate([w_out, w_down, jnp.zeros((wide - own_ffn, width), bf16)], axis=0)
 
     vectors = gathered[:, length:, :].reshape(tp, -1)[:, : small.shape[0]]
-    of_tokens = vectors[:, of_params:].reshape(tp, 7, length)
-    seg_all = of_tokens[:, 0].astype(jnp.int32)
-    of_tokens = of_tokens[:, 1:].astype(f32).reshape(tp, 2, 3, length)
-    stats = jnp.pad(of_tokens[:, :, 0] + of_tokens[:, :, 1] + of_tokens[:, :, 2], ((0, 0), (0, 6), (0, 0)))
+    seg_all = vectors[:, of_params:].astype(jnp.int32)
     vectors = vectors[:, :of_params]
     if outer > 1:
         vectors = lax.all_gather(vectors, "outer", axis=1, tiled=False)
@@ -705,7 +678,7 @@
     my_bias = lax.dynamic_index_in_dim(qkv_bias, me, 1, keepdims=False).reshape(1, own_qkv)
     tables = rotary_tables(seg_all)
 
-    normed, gate, up, hidden, joined = gate_forward(gathered, stats, gain_all, bias_all, gu_cols, qkv_cols)
+    stats, normed, gate, up, hidden, joined = gate_forward(gathered, gain_all, bias_all, gu_cols, qkv_cols)
     fused, context, probs = attend(joined, my_bias, tables, tp)
     branch_far = branches(plain_order[1], context, hidden, w_rows)[0]
     branch_sent, branch_keep = branches(plain_order[0], context, hidden, w_rows, shifted(branch_far, "c", cs, 1))
@@ -732,6 +705,7 @@
     share = functools.partial(dnormed_share, gathered=gathered, stats=stats, dgateup=dgateup, dfused=dfused, gu=gu_cols, qkv=qkv_cols)
     branch = add_up(branch_keep, branch_got, dfused)
     branch_own = lax.psum_scatter(branch, "z", scatter_dimension=0, tiled=True)
+    tokens32 = tokens.astype(f32)
     block_output = (tokens32 + branch_own.astype(f32)).astype(bf16)
     *far_shares, far_sums = share(order[1], branch, far=True)
     got = [shifted(far_share, "c", cs, 1) for far_share in far_shares]
@@ -746,10 +720,10 @@
     mine, theirs = of_replicas(extra)
     extra = jnp.concatenate([mine[..., :2], theirs[..., :2], mine[..., 2 : 2 + per_row]], axis=2)
     extra = jnp.pad(extra, ((0, 0), (0, 0), (own_ffn, 2 * wide - own_ffn - 4 - per_row)))
-    gu_total = (gu_mine + after(gu_got, near_share).astype(f32) + extra).astype(bf16)
+    *sent, keep = combine(near_share, got)
+    gu_total = (gu_mine + after(gu_got, *sent).astype(f32) + extra).astype(bf16)
     gu_own = lax.all_to_all(gu_total, TP, 0, 0, tiled=True)
-    *sent, keep = combine(near_share, got, gu_total)
-    qkv_mine, qkv_theirs = grads_of(dfused, *sent)
+    qkv_mine, qkv_theirs = grads_of(dfused, gu_total)
     qkv_got = other(qkv_theirs)
     rows_part = rows_grads(context, hidden, cotangent_all, PAIR + own_ffn, bf16 if outer == 1 else f32, qkv_theirs)
     if outer > 1:
@@ -769,7 +743,8 @@
                 leaving.append(term.astype(bf16))
                 term = shifted(leaving[-1], "z", zs, zs - k).astype(f32)
             dnormed_own = dnormed_own + term
-    inv = inv_std[:, None]
+    centered = tokens32 - jnp.mean(tokens32, axis=1, keepdims=True)
+    inv = lax.rsqrt(jnp.mean(centered * centered, axis=1, keepdims=True) + epsilon)
     xhat = centered * inv
     e = dnormed_own * gain_all
     tokens_back = inv * (e - jnp.mean(e, axis=1, keepdims=True) - xhat * jnp.mean(e * xhat, axis=1, keepdims=True))

time: 443 us -> 437 us (0.986)
  waiting for transfers between devices: 182 us -> 169 us
  starting transfers between devices: 45.2 us -> 52 us
  Pallas kernels: 128 us -> 134 us
    all_to_all x1, waiting for transfers between devices: 15.8 us -> 0.85 us  [per_device(): qkv_own = lax.all_to_all(qkv_total, TP, 0, 0, tiled=True)]
    ppermute x18, waiting for transfers between devices: 69.6 us -> 76.4 us  [shifted(): return lax.ppermute(x, axis, [(i, (i + step) % size) for i in range(size)])]
    all_to_all x1, starting transfers between devices: 4.84 us -> 10.4 us  [per_device(): qkv_own = lax.all_to_all(qkv_total, TP, 0, 0, tiled=True)]
    unnamed x69 -> x71, local copies, waits for them, and re-layouts: 17.7 us -> 14.1 us
  transfers between devices with their start and end apart: 25 -> 25, of which waited for: 12 -> 13; matrix products, arithmetic and copies ran while one was open for 11% -> 11% of each run, Pallas kernels for 28% -> 30%
where the time goes in v3:
time: 437 us; the launch traced here: 435 us
  waiting for transfers between devices  169 us (39%)
  Pallas kernels  134 us (31%)
  starting transfers between devices  52 us (12%)
  other arithmetic  33.2 us (8%)
  local copies, waits for them, and re-layouts  33.1 us (8%)
  between operations  14.4 us (3%)
    all_to_all x2, waiting for transfers between devices, to_columns(): own = lax.all_to_all(own, TP, 0, 0, tiled=True)  77.5 us
    ppermute x18, waiting for transfers between devices, shifted(): return lax.ppermute(x, axis, [(i, (i + step) % size) for i in range(size)])  76.4 us
    pallas_call x2, Pallas kernels, dnormed_share(): pl.pallas_call(ignoring(dnormed_kernel, 11, len(others)), name='dn_far' i...  25.7 us
    pallas_call x1, Pallas kernels, gate_forward(): pl.pallas_call(gate_kernel, name='gate_fwd', grid=(count // 2,), in_specs...  21.1 us
    ppermute x18, starting transfers between devices, shifted(): return lax.ppermute(x, axis, [(i, (i + step) % size) for i in range(size)])  20.5 us
    pallas_call x2, Pallas kernels, split_grads(): pl.pallas_call(ignoring(grads_kernel, 3, len(others)), name='grads', grid...  20 us
    all_to_all x2, starting transfers between devices, to_columns(): own = lax.all_to_all(own, TP, 0, 0, tiled=True)  16.1 us
    pallas_call x2, Pallas kernels, branches(): pl.pallas_call(functools.partial(branch_kernel, got is None), name='branc...  14.3 us
  transfers between devices with their start and end apart: 25, of which 13 were waited for; matrix products, arithmetic and copies ran while one was open for 11% of the time, Pallas kernels for 30%

profile of v3, /device:TPU:0, one launch (start us, length us, event | category | flops | bytes accessed | tf_op | source)
XLA Modules:
  0.0 435.1 jit_solution(15056230109997389348)
XLA Ops:
  8.6 1.9 pad_maximum_fusion
  11.3 1.8 copy-done.14
  13.1 2.0 pack.2
  15.1 7.6 %all-to-all-start = ((bf16[16,64,768]{2,1,0:T(8,128)(2,1)}), bf16[16,64,768]{2,1,0:T(8,128)(2,1)}, u32[]{:S(2)}, u32[]{:S(2)}) async-start(bf16[16,64,768]{2,1,0:T(8,128)(2,1)} %pack.2), calls=%async_computation | async-start | bytes 3145728 | tf_op jit(solution)/shard_map/all_to_all | solution.py:653
  24.2 48.9 %all-to-all-done = bf16[16,64,768]{2,1,0:T(8,128)(2,1)} async-done(((bf16[16,64,768]{2,1,0:T(8,128)(2,1)}), bf16[16,64,768]{2,1,0:T(8,128)(2,1)}, u32[]{:S(2)}, u32[]{:S(2)}) %all-to-all-start) | async-done | bytes 1572896 | tf_op jit(solution)/shard_map/all_to_all | solution.py:653
  73.2 8.5 %all-to-all-start.1 = ((bf16[16,64,384]{2,1,0:T(8,128)(2,1)}), bf16[16,64,384]{2,1,0:T(8,128)(2,1)S(1)}, u32[]{:S(2)}, u32[]{:S(2)}) async-start(bf16[16,64,384]{2,1,0:T(8,128)(2,1)} %pack.3), calls=%async_computation.1 | async-start | bytes 1572864 | tf_op jit(solution)/shard_map/all_to_all | solution.py:653
  82.3 1.7 collective-permute-start
  84.5 28.6 %all-to-all-done.1 = bf16[16,64,384]{2,1,0:T(8,128)(2,1)S(1)} async-done(((bf16[16,64,384]{2,1,0:T(8,128)(2,1)}), bf16[16,64,384]{2,1,0:T(8,128)(2,1)S(1)}, u32[]{:S(2)}, u32[]{:S(2)}) %all-to-all-start.1) | async-done | bytes 786464 | tf_op jit(solution)/shard_map/all_to_all | solution.py:653
  113.1 1.7 collective-permute-start.1
  119.7 16.4 %collective-permute-done.1 = bf16[16,64,384]{2,1,0:T(8,128)(2,1)} collective-permute-done((bf16[16,64,384]{2,1,0:T(8,128)(2,1)S(1)}, bf16[16,64,384]{2,1,0:T(8,128)(2,1)}, u32[]{:S(2)}, u32[]{:S(2)}) %collective-permute-start.1) | collective-permute-done | bytes 786464 | tf_op jit(solution)/shard_map/ppermute | solution.py:185
  136.2 2.2 bitcast_dynamic-update-slice_fusion.2
  141.9 2.1 slice.143
  145.3 21.1 %gate_fwd.1 = (f32[2048,128]{1,0:T(8,128)}, bf16[2048,2048]{1,0:T(8,128)(2,1)}, f32[2048,384]{1,0:T(8,128)}, f32[2048,384]{1,0:T(8,128)}, bf16[2048,384]{1,0:T(8,128)(2,1)}, /*index=5*/f32[2048,384]{1,0:T(8,128)}) custom-call(bf16[16,144,2048]{2,1,0:T(8,128)(2,1)} %bitcast.77, bf16[16,144,2048]{2,1,0:T(8,128)(2,1)} %bitcast.78, f32[1,2048]{1,0:T(1,128)} %bitcast.90, ...), custom_call_target="tpu_custom_call" | custom-call | flops 1 | bytes 1 | tf_op jit(solution)/shard_map/gate_fwd/pallas_call | solution.py:312
  167.4 3.8 fusion
  171.3 3.3 attend.1
  174.7 5.5 %branch_far.1 = bf16[1024,2048]{1,0:T(8,128)(2,1)} custom-call(s32[8]{0:T(128)S(1)} %stack.125.order_ref, bf16[2048,128]{1,0:T(8,128)(2,1)S(1)} %get-tuple-element.39.ac_ref.bc_ref.refs_0_, bf16[2048,128]{1,0:T(8,128)(2,1)S(1)} %get-tuple-element.39.ac_ref.bc_ref.refs_0_, bf16[2048,384]{1,0:T(8,128)(2,1)S(1)} %copy-done.1, bf16[2048,384]{1,0:T(8,128)(2,1)S(1)} %copy-done.1, ...), custom_call_target="tpu_custom_call" | custom-call | flops 1 | bytes 1 | tf_op jit(solution)/shard_map/branch_far/pallas_call | solution.py:372
  180.3 7.4 %collective-permute-done.2.refs_0_ = bf16[1024,2048]{1,0:T(8,128)(2,1)} collective-permute-done((bf16[1024,2048]{1,0:T(8,128)(2,1)}, bf16[1024,2048]{1,0:T(8,128)(2,1)}, u32[]{:S(2)}, u32[]{:S(2)}) %collective-permute-start.2) | collective-permute-done | bytes 4194336 | tf_op jit(solution)/shard_map/ppermute | solution.py:185
  187.7 8.9 %branch_near.1 = (bf16[512,2048]{1,0:T(8,128)(2,1)}, f32[512,2048]{1,0:T(8,128)}) custom-call(s32[8]{0:T(128)S(1)} %stack.116.order_ref, bf16[2048,128]{1,0:T(8,128)(2,1)S(1)} %get-tuple-element.39.ac_ref.bc_ref.refs_0_, bf16[2048,128]{1,0:T(8,128)(2,1)S(1)} %get-tuple-element.39.ac_ref.bc_ref.refs_0_, bf16[2048,384]{1,0:T(8,128)(2,1)S(1)} %copy-done.1, ...), custom_call_target="tpu_custom_call" | custom-call | flops 1 | bytes 1 | tf_op jit(solution)/shard_map/branch_near/pallas_call | solution.py:372
  196.6 1.7 collective-permute-start.3
  198.3 13.2 %all-gather.4.cloned.1.call-done.refs_0_.refs_2_ = bf16[2048,2048]{1,0:T(8,128)(2,1)} async-done(((bf16[128,2048]{1,0:T(8,128)(2,1)}), bf16[2048,2048]{1,0:T(8,128)(2,1)}) %all-gather.4.cloned.1.call-update) | async-done | bytes 8388624 | tf_op jit(solution)/shard_map/all_gather | solution.py:647
  213.1 11.4 %gate_back.1 = (bf16[2048,768]{1,0:T(8,128)(2,1)}, bf16[2048,128]{1,0:T(8,128)(2,1)S(1)}) custom-call(bf16[2048,2048]{1,0:T(8,128)(2,1)} %all-gather.4.cloned.1.call-done.refs_0_.refs_2_, f32[2048,384]{1,0:T(8,128)} %get-tuple-element.45.refs_1_, f32[2048,384]{1,0:T(8,128)} %get-tuple-element.46.refs_2_, bf16[512,2048]{1,0:T(8,128)(2,1)S(1)} %copy-done.3, ...), custom_call_target="tpu_custom_call" | custom-call | flops 1 | bytes 1 | tf_op jit(solution)/shard_map/gate_back/pallas_call | solution.py:409
  224.6 11.3 %grads.2 = (f32[16,64,768]{2,1,0:T(8,128)}, bf16[16,64,768]{2,1,0:T(8,128)(2,1)}) custom-call(s32[1]{0:T(128)} %bitcast.12.part_ref.refs_0_, bf16[2048,2048]{1,0:T(8,128)(2,1)} %get-tuple-element.48.refs_1_, bf16[2048,768]{1,0:T(8,128)(2,1)} %get-tuple-element.49.refs_2_.refs_5_.refs_6_), custom_call_target="tpu_custom_call" | custom-call | flops 1 | bytes 1 | tf_op jit(solution)/shard_map/grads/pallas_call | solution.py:438
  244.8 5.4 %attend_back.1 = (bf16[2048,384]{1,0:T(8,128)(2,1)S(1)}, f32[1,384]{1,0:T(1,128)S(1)}) custom-call(bf16[2048,384]{1,0:T(8,128)(2,1)S(1)} %copy-done.20, f32[16,256,128]{2,1,0:T(8,128)S(1)} %copy-done.16, bf16[2048,128]{1,0:T(8,128)(2,1)S(1)} %get-tuple-element.47.refs_2_, f32[2048,128]{1,0:T(8,128)S(1)} %copy-done.10, f32[2048,128]{1,0:T(8,128)S(1)} %copy-done.8, ...), custom_call_target="tpu_custom_call" | custom-call | flops 536870912 | bytes 12288000 | tf_op jit(solution)/shard_map/attend_back/pallas_call | solution.py:164
  250.2 4.3 add_up.1.refs_11_
  254.5 13.2 %dn_far.1 = (bf16[256,2048]{1,0:T(8,128)(2,1)}, bf16[256,2048]{1,0:T(8,128)(2,1)}, bf16[256,2048]{1,0:T(8,128)(2,1)}, bf16[256,2048]{1,0:T(8,128)(2,1)}, f32[8,2048]{1,0:T(8,128)}) custom-call(s32[8]{0:T(128)} %stack.143.refs_0_, bf16[16,144,2048]{2,1,0:T(8,128)(2,1)} %bitcast.79, bf16[16,144,2048]{2,1,0:T(8,128)(2,1)} %bitcast.80, ...), custom_call_target="tpu_custom_call" | custom-call | flops 1 | bytes 1 | tf_op jit(solution)/shard_map/dn_far/pallas_call | solution.py:525
  269.7 12.5 %dn_near.1 = (f32[1024,2048]{1,0:T(8,128)}, f32[8,2048]{1,0:T(8,128)}) custom-call(s32[8]{0:T(128)} %stack.134.refs_0_, bf16[16,144,2048]{2,1,0:T(8,128)(2,1)} %bitcast.81, bf16[16,144,2048]{2,1,0:T(8,128)(2,1)} %bitcast.82, f32[2048,128]{1,0:T(8,128)} %get-tuple-element.52.refs_3_.refs_4_, f32[2048,128]{1,0:T(8,128)} %get-tuple-element.52.refs_3_.refs_4_, ...), custom_call_target="tpu_custom_call" | custom-call | flops 1 | bytes 1 | tf_op jit(solution)/shard_map/dn_near/pallas_call | solution.py:525
  284.9 6.4 %combine.1 = (bf16[256,2048]{1,0:T(8,128)(2,1)}, bf16[256,2048]{1,0:T(8,128)(2,1)S(1)}, f32[512,2048]{1,0:T(8,128)}) custom-call(f32[1024,2048]{1,0:T(8,128)} %get-tuple-element.57.refs_0_, bf16[256,2048]{1,0:T(8,128)(2,1)S(1)} %collective-permute-done.4.refs_1_, bf16[256,2048]{1,0:T(8,128)(2,1)S(1)} %collective-permute-done.5.refs_2_, ...), custom_call_target="tpu_custom_call" | custom-call | flops 1 | bytes 1 | tf_op jit(solution)/shard_map/combine/pallas_call | solution.py:573
  292.9 1.9 copy-done.24
  294.9 3.4 add_convert_fusion.refs_3_
  298.3 4.8 %all-to-all-start.2 = ((bf16[16,64,768]{2,1,0:T(8,128)(2,1)}), bf16[16,64,768]{2,1,0:T(8,128)(2,1)}, u32[]{:S(2)}, u32[]{:S(2)}) async-start(bf16[16,64,768]{2,1,0:T(8,128)(2,1)} %add_convert_fusion.refs_3_), calls=%async_computation.3 | async-start | bytes 3145728 | tf_op jit(solution)/shard_map/all_to_all | solution.py:725
  303.1 8.7 %grads.3 = (f32[16,64,384]{2,1,0:T(8,128)}, bf16[16,64,384]{2,1,0:T(8,128)(2,1)}) custom-call(s32[1]{0:T(128)} %bitcast.12.part_ref.refs_0_, bf16[2048,2048]{1,0:T(8,128)(2,1)} %get-tuple-element.48.refs_1_, bf16[2048,384]{1,0:T(8,128)(2,1)} %copy-done, bf16[16,64,768]{2,1,0:T(8,128)(2,1)} %add_convert_fusion.refs_3_), custom_call_target="tpu_custom_call" | custom-call | flops 1 | bytes 1 | tf_op jit(solution)/shard_map/grads/pallas_call | solution.py:438
  311.8 1.9 collective-permute-start.15
  313.8 8.8 %rows.1.refs_3_ = bf16[480,2048]{1,0:T(8,128)(2,1)} custom-call(bf16[2048,128]{1,0:T(8,128)(2,1)} %copy-done.4, bf16[2048,384]{1,0:T(8,128)(2,1)} %get-tuple-element.40.ah_ref.bh_ref.refs_1_, bf16[2048,2048]{1,0:T(8,128)(2,1)} %all-gather.4.cloned.1.call-done.refs_0_.refs_2_, bf16[16,64,384]{2,1,0:T(8,128)(2,1)} %get-tuple-element.65.refs_3_), custom_call_target="tpu_custom_call" | custom-call | flops 1 | bytes 1 | tf_op jit(solution)/shard_map/rows/pallas_call | solution.py:467
  323.8 2.5 add_convert_fusion.3
  327.8 4.6 %collective-permute-done.15 = bf16[16,64,384]{2,1,0:T(8,128)(2,1)S(1)} collective-permute-done((bf16[16,64,384]{2,1,0:T(8,128)(2,1)}, bf16[16,64,384]{2,1,0:T(8,128)(2,1)S(1)}, u32[]{:S(2)}, u32[]{:S(2)}) %collective-permute-start.15) | collective-permute-done | bytes 786464 | tf_op jit(solution)/shard_map/ppermute | solution.py:185
  333.5 3.7 collective-permute-start.10
  337.1 19.9 %collective-permute-done.12 = bf16[256,2048]{1,0:T(8,128)(2,1)} collective-permute-done((bf16[256,2048]{1,0:T(8,128)(2,1)}, bf16[256,2048]{1,0:T(8,128)(2,1)}, u32[]{:S(2)}, u32[]{:S(2)}) %collective-permute-start.12) | collective-permute-done | bytes 1048608 | tf_op jit(solution)/shard_map/ppermute | solution.py:185
  357.0 2.3 add_convert_fusion.2
  359.2 2.4 collective-permute-start.13
  363.2 10.4 %all-to-all-start.3 = ((bf16[16,64,384]{2,1,0:T(8,128)(2,1)}), bf16[16,64,384]{2,1,0:T(8,128)(2,1)S(1)}, u32[]{:S(2)}, u32[]{:S(2)}) async-start(bf16[16,64,384]{2,1,0:T(8,128)(2,1)} %after.5), calls=%async_computation.4 | async-start | bytes 1572864 | tf_op jit(solution)/shard_map/all_to_all | solution.py:754
  374.6 2.9 convert_add_fusion
  377.5 1.9 slice.164
  380.4 19.1 %collective-permute-done.9 = bf16[128,2048]{1,0:T(8,128)(2,1)} collective-permute-done((bf16[128,2048]{1,0:T(8,128)(2,1)S(1)}, bf16[128,2048]{1,0:T(8,128)(2,1)}, u32[]{:S(2)}, u32[]{:S(2)}) %collective-permute-start.9) | collective-permute-done | bytes 524320 | tf_op jit(solution)/shard_map/ppermute | solution.py:185
  399.5 2.5 fusion.31
  407.8 1.9 convert_add_fusion.2
  409.8 6.1 %unpack.3 = f32[128,11264]{1,0:T(8,128)} custom-call(s32[1]{0:T(128)} %bitcast.12.part_ref.refs_0_, bf16[16,64,768]{2,1,0:T(8,128)(2,1)} %all-to-all-done.2.refs_1_.own_ref, bf16[16,64,768]{2,1,0:T(8,128)(2,1)S(1)} %collective-permute-done.14.other_ref), custom_call_target="tpu_custom_call" | custom-call | flops 1 | bytes 1 | tf_op jit(solution)/shard_map/unpack/pallas_call | solution.py:266
  418.9 6.2 %collective-permute-done.16.other_ref = bf16[16,64,384]{2,1,0:T(8,128)(2,1)S(1)} collective-permute-done((bf16[16,64,384]{2,1,0:T(8,128)(2,1)S(1)}, bf16[16,64,384]{2,1,0:T(8,128)(2,1)S(1)}, u32[]{:S(2)}, u32[]{:S(2)}) %collective-permute-start.16) | collective-permute-done | bytes 786464 | tf_op jit(solution)/shard_map/ppermute | solution.py:185
  425.1 3.4 unpack.2
  (170 shorter events, 48.6 us)
Async XLA Ops:
  7.2 134.7 %all-gather.6.cloned.1.call-start = ((), (), s32[]{:S(2)}) async-start(), calls=%async_computation.7 | async-start | bytes 10027008 | tf_op jit(solution)/shard_map/all_gather | solution.py:645
  10.6 201.0 %all-gather.4.cloned.1.call-start = ((), (), s32[]{:S(2)}) async-start(), calls=%async_computation.5 | async-start | bytes 8912896 | tf_op jit(solution)/shard_map/all_gather | solution.py:647
  15.1 7.6 %copy-start.17 = (bf16[128,6144]{1,0:T(8,128)(2,1)S(1)}, bf16[128,6144]{1,0:T(8,128)(2,1)}, u32[]{:S(2)}) copy-start(bf16[128,6144]{1,0:T(8,128)(2,1)} %own_ref.3) | copy-start | bytes 4718596
  15.1 58.0 %all-to-all-start = ((bf16[16,64,768]{2,1,0:T(8,128)(2,1)}), bf16[16,64,768]{2,1,0:T(8,128)(2,1)}, u32[]{:S(2)}, u32[]{:S(2)}) async-start(bf16[16,64,768]{2,1,0:T(8,128)(2,1)} %pack.2), calls=%async_computation | async-start | bytes 3145728 | tf_op jit(solution)/shard_map/all_to_all | solution.py:653
  22.7 92.8 %copy-start.29 = (bf16[352,2048]{1,0:T(8,128)(2,1)S(1)}, bf16[352,2048]{1,0:T(8,128)(2,1)}, u32[]{:S(2)}) copy-start(bf16[352,2048]{1,0:T(8,128)(2,1)} %param.18) | copy-start | bytes 4325380
  22.7 92.8 %copy-start.30 = (bf16[128,2048]{1,0:T(8,128)(2,1)S(1)}, bf16[128,2048]{1,0:T(8,128)(2,1)}, u32[]{:S(2)}) copy-start(bf16[128,2048]{1,0:T(8,128)(2,1)} %param.16) | copy-start | bytes 1572868
  73.2 40.0 %all-to-all-start.1 = ((bf16[16,64,384]{2,1,0:T(8,128)(2,1)}), bf16[16,64,384]{2,1,0:T(8,128)(2,1)S(1)}, u32[]{:S(2)}, u32[]{:S(2)}) async-start(bf16[16,64,384]{2,1,0:T(8,128)(2,1)} %pack.3), calls=%async_computation.1 | async-start | bytes 1572864 | tf_op jit(solution)/shard_map/all_to_all | solution.py:653
  81.7 281.5 %reduce-scatter.2.cloned.1.call-start = ((), (), s32[]{:S(2)}) async-start(), calls=%async_computation.6 | async-start | bytes 2621440 | tf_op jit(solution)/shard_map/reduce_scatter | solution.py:707
  82.3 58.0 %collective-permute-start = (bf16[16,64,768]{2,1,0:T(8,128)(2,1)}, bf16[16,64,768]{2,1,0:T(8,128)(2,1)}, u32[]{:S(2)}, u32[]{:S(2)}) collective-permute-start(bf16[16,64,768]{2,1,0:T(8,128)(2,1)} %all-to-all-done), channel_id=1, source_target_pairs={{0,16},{16,0},{1,17},{17,1},{2,18},{18,2},{3,19},{19,3},{4,20},{20... | collective-permute-start | bytes 4718600 | tf_op jit(solution)/shard_map/ppermute | solution.py:185
  113.1 23.0 %collective-permute-start.1 = (bf16[16,64,384]{2,1,0:T(8,128)(2,1)S(1)}, bf16[16,64,384]{2,1,0:T(8,128)(2,1)}, u32[]{:S(2)}, u32[]{:S(2)}) collective-permute-start(bf16[16,64,384]{2,1,0:T(8,128)(2,1)S(1)} %all-to-all-done.1), channel_id=1, source_target_pairs={{0,16},{16,0},{1,17},{17,1},{2,18},{18,2},{3,19},{19,3},{4,20},{20... | collective-permute-start | bytes 2359304 | tf_op jit(solution)/shard_map/ppermute | solution.py:185
  145.3 22.1 %copy-start.31 = (pred[128]{0:T(512)(128)(4,1)S(1)}, pred[128]{0:T(512)(128)(4,1)}, u32[]{:S(2)}) copy-start(pred[128]{0:T(512)(128)(4,1)} %get-tuple-element.89) | copy-start | bytes 388
  145.3 22.1 %copy-start.32 = (pred[128]{0:T(512)(128)(4,1)S(1)}, pred[128]{0:T(512)(128)(4,1)}, u32[]{:S(2)}) copy-start(pred[128]{0:T(512)(128)(4,1)} %get-tuple-element.90) | copy-start | bytes 388
  145.3 22.1 %copy-start.33 = (pred[128]{0:T(512)(128)(4,1)S(1)}, pred[128]{0:T(512)(128)(4,1)}, u32[]{:S(2)}) copy-start(pred[128]{0:T(512)(128)(4,1)} %broadcast_compare_fusion.1) | copy-start | bytes 388
  145.3 22.2 %copy-start.34 = (f32[128]{0:T(128)S(1)}, f32[128]{0:T(128)}, u32[]{:S(2)}) copy-start(f32[128]{0:T(128)} %fusion.29) | copy-start | bytes 1540
  167.0 4.3 copy-start.13
  171.2 3.4 copy-start.5
  171.3 3.4 copy-start.7
  171.3 3.4 copy-start.1
  171.3 3.4 copy-start.2
  174.7 5.5 %copy-start.15 = (f32[16,256,128]{2,1,0:T(8,128)}, f32[16,256,128]{2,1,0:T(8,128)S(1)}, u32[]{:S(2)}) copy-start(f32[16,256,128]{2,1,0:T(8,128)S(1)} %get-tuple-element.44.refs_1_) | copy-start | bytes 6291460
  174.7 5.5 %copy-start.19 = (bf16[2048,384]{1,0:T(8,128)(2,1)}, bf16[2048,384]{1,0:T(8,128)(2,1)S(1)}, u32[]{:S(2)}) copy-start(bf16[2048,384]{1,0:T(8,128)(2,1)S(1)} %get-tuple-element.43.refs_0_) | copy-start | bytes 4718596
  174.7 13.0 %copy-start.4 = (bf16[2048,128]{1,0:T(8,128)(2,1)}, bf16[2048,128]{1,0:T(8,128)(2,1)S(1)}, u32[]{:S(2)}) copy-start(bf16[2048,128]{1,0:T(8,128)(2,1)S(1)} %get-tuple-element.39.ac_ref.bc_ref.refs_0_) | copy-start | bytes 1572868
  180.2 7.5 %collective-permute-start.2 = (bf16[1024,2048]{1,0:T(8,128)(2,1)}, bf16[1024,2048]{1,0:T(8,128)(2,1)}, u32[]{:S(2)}, u32[]{:S(2)}) collective-permute-start(bf16[1024,2048]{1,0:T(8,128)(2,1)} %branch_far.1), channel_id=1, source_target_pairs={{0,1},{1,0},{2,3},{3,2},{4,5},{5,4},{6,7},{7,6},{8,9},{9,8},{10,11... | collective-permute-start | bytes 12582920 | tf_op jit(solution)/shard_map/ppermute | solution.py:185
  196.6 53.6 %collective-permute-start.3 = (bf16[512,2048]{1,0:T(8,128)(2,1)}, bf16[512,2048]{1,0:T(8,128)(2,1)}, u32[]{:S(2)}, u32[]{:S(2)}) collective-permute-start(bf16[512,2048]{1,0:T(8,128)(2,1)} %get-tuple-element.42.refs_4_), channel_id=1, source_target_pairs={{0,2},{2,0},{1,3},{3,1},{4,6},{6,4},{5,7},{7,5},{8,10},{10,8},{9,1... | collective-permute-start | bytes 6291464 | tf_op jit(solution)/shard_map/ppermute | solution.py:185
  224.6 13.4 %copy-start.6 = (f32[2048,128]{1,0:T(8,128)S(1)}, f32[2048,128]{1,0:T(8,128)}, u32[]{:S(2)}) copy-start(f32[2048,128]{1,0:T(8,128)} %copy-done.5) | copy-start | bytes 3145732
  235.9 57.1 %collective-permute-start.11 = (bf16[16,64,768]{2,1,0:T(8,128)(2,1)}, bf16[16,64,768]{2,1,0:T(8,128)(2,1)}, u32[]{:S(2)}, u32[]{:S(2)}) collective-permute-start(bf16[16,64,768]{2,1,0:T(8,128)(2,1)} %get-tuple-element.50.refs_6_), channel_id=1, source_target_pairs={{0,16},{16,0},{1,17},{17,1},{2,18},{18,2},{3,19},{19,3},{4,20},{20... | collective-permute-start | bytes 4718600 | tf_op jit(solution)/shard_map/ppermute | solution.py:185
  244.8 5.4 %copy-start.12 = (f32[512,2048]{1,0:T(8,128)S(1)}, f32[512,2048]{1,0:T(8,128)}, u32[]{:S(2)}) copy-start(f32[512,2048]{1,0:T(8,128)} %get-tuple-element.41.refs_0_) | copy-start | bytes 12582916
  250.2 4.3 copy-start
  267.6 17.2 %collective-permute-start.4 = (bf16[256,2048]{1,0:T(8,128)(2,1)}, bf16[256,2048]{1,0:T(8,128)(2,1)S(1)}, u32[]{:S(2)}, u32[]{:S(2)}) collective-permute-start(bf16[256,2048]{1,0:T(8,128)(2,1)} %get-tuple-element.53.refs_11_), channel_id=1, source_target_pairs={{0,1},{1,0},{2,3},{3,2},{4,5},{5,4},{6,7},{7,6},{8,9},{9,8},{10,11... | collective-permute-start | bytes 3145736 | tf_op jit(solution)/shard_map/ppermute | solution.py:185
  267.7 17.1 %collective-permute-start.5 = (bf16[256,2048]{1,0:T(8,128)(2,1)}, bf16[256,2048]{1,0:T(8,128)(2,1)S(1)}, u32[]{:S(2)}, u32[]{:S(2)}) collective-permute-start(bf16[256,2048]{1,0:T(8,128)(2,1)} %get-tuple-element.54.refs_12_), channel_id=1, source_target_pairs={{0,1},{1,0},{2,3},{3,2},{4,5},{5,4},{6,7},{7,6},{8,9},{9,8},{10,11... | collective-permute-start | bytes 3145736 | tf_op jit(solution)/shard_map/ppermute | solution.py:185
  268.2 16.7 %collective-permute-start.6 = (bf16[256,2048]{1,0:T(8,128)(2,1)}, bf16[256,2048]{1,0:T(8,128)(2,1)S(1)}, u32[]{:S(2)}, u32[]{:S(2)}) collective-permute-start(bf16[256,2048]{1,0:T(8,128)(2,1)} %get-tuple-element.55.refs_13_), channel_id=1, source_target_pairs={{0,1},{1,0},{2,3},{3,2},{4,5},{5,4},{6,7},{7,6},{8,9},{9,8},{10,11... | collective-permute-start | bytes 3145736 | tf_op jit(solution)/shard_map/ppermute | solution.py:185
  268.3 16.6 %collective-permute-start.7 = (bf16[256,2048]{1,0:T(8,128)(2,1)}, bf16[256,2048]{1,0:T(8,128)(2,1)}, u32[]{:S(2)}, u32[]{:S(2)}) collective-permute-start(bf16[256,2048]{1,0:T(8,128)(2,1)} %get-tuple-element.56.refs_14_), channel_id=1, source_target_pairs={{0,1},{1,0},{2,3},{3,2},{4,5},{5,4},{6,7},{7,6},{8,9},{9,8},{10,11... | collective-permute-start | bytes 3145736 | tf_op jit(solution)/shard_map/ppermute | solution.py:185
  292.2 31.6 %collective-permute-start.8 = (bf16[256,2048]{1,0:T(8,128)(2,1)}, bf16[256,2048]{1,0:T(8,128)(2,1)}, u32[]{:S(2)}, u32[]{:S(2)}) collective-permute-start(bf16[256,2048]{1,0:T(8,128)(2,1)} %get-tuple-element.59.refs_1_), channel_id=1, source_target_pairs={{0,2},{2,0},{1,3},{3,1},{4,6},{6,4},{5,7},{7,5},{8,10},{10,8},{9,1... | collective-permute-start | bytes 3145736 | tf_op jit(solution)/shard_map/ppermute | solution.py:185
  298.3 63.4 %all-to-all-start.2 = ((bf16[16,64,768]{2,1,0:T(8,128)(2,1)}), bf16[16,64,768]{2,1,0:T(8,128)(2,1)}, u32[]{:S(2)}, u32[]{:S(2)}) async-start(bf16[16,64,768]{2,1,0:T(8,128)(2,1)} %add_convert_fusion.refs_3_), calls=%async_computation.3 | async-start | bytes 3145728 | tf_op jit(solution)/shard_map/all_to_all | solution.py:725
  311.8 12.0 %copy-start.23 = (f32[512,2048]{1,0:T(8,128)S(1)}, f32[512,2048]{1,0:T(8,128)}, u32[]{:S(2)}) copy-start(f32[512,2048]{1,0:T(8,128)} %get-tuple-element.58) | copy-start | bytes 12582916
  311.8 20.6 %collective-permute-start.15 = (bf16[16,64,384]{2,1,0:T(8,128)(2,1)}, bf16[16,64,384]{2,1,0:T(8,128)(2,1)S(1)}, u32[]{:S(2)}, u32[]{:S(2)}) collective-permute-start(bf16[16,64,384]{2,1,0:T(8,128)(2,1)} %get-tuple-element.65.refs_3_), channel_id=1, source_target_pairs={{0,16},{16,0},{1,17},{17,1},{2,18},{18,2},{3,19},{19,3},{4,20},{20... | collective-permute-start | bytes 2359304 | tf_op jit(solution)/shard_map/ppermute | solution.py:185
  322.5 52.1 %collective-permute-start.17 = (bf16[480,2048]{1,0:T(8,128)(2,1)}, bf16[480,2048]{1,0:T(8,128)(2,1)}, u32[]{:S(2)}, u32[]{:S(2)}) collective-permute-start(bf16[480,2048]{1,0:T(8,128)(2,1)} %rows.1.refs_3_), channel_id=1, source_target_pairs={{0,16},{16,0},{1,17},{17,1},{2,18},{18,2},{3,19},{19,3},{4,20},{20... | collective-permute-start | bytes 5898248 | tf_op jit(solution)/shard_map/ppermute | solution.py:185
  326.3 6.1 %copy-start.28 = (f32[16,64,384]{2,1,0:T(8,128)S(1)}, f32[16,64,384]{2,1,0:T(8,128)}, u32[]{:S(2)}) copy-start(f32[16,64,384]{2,1,0:T(8,128)} %get-tuple-element.66) | copy-start | bytes 4718596
  326.3 30.7 %collective-permute-start.12 = (bf16[256,2048]{1,0:T(8,128)(2,1)}, bf16[256,2048]{1,0:T(8,128)(2,1)}, u32[]{:S(2)}, u32[]{:S(2)}) collective-permute-start(bf16[256,2048]{1,0:T(8,128)(2,1)} %after.4), channel_id=1, source_target_pairs={{0,2},{2,0},{1,3},{3,1},{4,6},{6,4},{5,7},{7,5},{8,10},{10,8},{9,1... | collective-permute-start | bytes 3145736 | tf_op jit(solution)/shard_map/ppermute | solution.py:185
  327.3 9.8 %copy-start.27 = (bf16[128,2048]{1,0:T(8,128)(2,1)S(1)}, bf16[128,2048]{1,0:T(8,128)(2,1)}, u32[]{:S(2)}) copy-start(bf16[128,2048]{1,0:T(8,128)(2,1)} %get-tuple-element.73.refs_1_) | copy-start | bytes 1572868
  333.5 47.0 %collective-permute-start.10 = (bf16[128,2048]{1,0:T(8,128)(2,1)}, bf16[128,2048]{1,0:T(8,128)(2,1)}, u32[]{:S(2)}, u32[]{:S(2)}) collective-permute-start(bf16[128,2048]{1,0:T(8,128)(2,1)} %get-tuple-element.72.refs_2_), channel_id=1, source_target_pairs={{0,12},{4,0},{8,4},{12,8},{1,13},{5,1},{9,5},{13,9},{2,14},{6,2},{... | collective-permute-start | bytes 1572872 | tf_op jit(solution)/shard_map/ppermute | solution.py:185
  337.1 62.4 %collective-permute-start.9 = (bf16[128,2048]{1,0:T(8,128)(2,1)S(1)}, bf16[128,2048]{1,0:T(8,128)(2,1)}, u32[]{:S(2)}, u32[]{:S(2)}) collective-permute-start(bf16[128,2048]{1,0:T(8,128)(2,1)S(1)} %copy-done.27), channel_id=1, source_target_pairs={{0,8},{4,12},{8,0},{12,4},{1,9},{5,13},{9,1},{13,5},{2,10},{6,14},... | collective-permute-start | bytes 1572872 | tf_op jit(solution)/shard_map/ppermute | solution.py:185
  359.2 40.2 %collective-permute-start.13 = (bf16[128,2048]{1,0:T(8,128)(2,1)}, bf16[128,2048]{1,0:T(8,128)(2,1)}, u32[]{:S(2)}, u32[]{:S(2)}) collective-permute-start(bf16[128,2048]{1,0:T(8,128)(2,1)} %add_convert_fusion.2), channel_id=1, source_target_pairs={{0,4},{4,8},{8,12},{12,0},{1,5},{5,9},{9,13},{13,1},{2,6},{6,10},{... | collective-permute-start | bytes 1572872 | tf_op jit(solution)/shard_map/ppermute | solution.py:185
  361.6 46.2 %collective-permute-start.14 = (bf16[16,64,768]{2,1,0:T(8,128)(2,1)}, bf16[16,64,768]{2,1,0:T(8,128)(2,1)S(1)}, u32[]{:S(2)}, u32[]{:S(2)}) collective-permute-start(bf16[16,64,768]{2,1,0:T(8,128)(2,1)} %all-to-all-done.2.refs_1_.own_ref), channel_id=1, source_target_pairs={{0,16},{16,0},{1,17},{17,1},{2,18},{18,2},{3,19},{19,3},{4,20},{20... | collective-permute-start | bytes 4718600 | tf_op jit(solution)/shard_map/ppermute | solution.py:185
  363.2 42.4 %all-to-all-start.3 = ((bf16[16,64,384]{2,1,0:T(8,128)(2,1)}), bf16[16,64,384]{2,1,0:T(8,128)(2,1)S(1)}, u32[]{:S(2)}, u32[]{:S(2)}) async-start(bf16[16,64,384]{2,1,0:T(8,128)(2,1)} %after.5), calls=%async_computation.4 | async-start | bytes 1572864 | tf_op jit(solution)/shard_map/all_to_all | solution.py:754
  399.5 3.7 copy-start.25
  399.5 3.7 copy-start.26
  405.5 19.6 %collective-permute-start.16 = (bf16[16,64,384]{2,1,0:T(8,128)(2,1)S(1)}, bf16[16,64,384]{2,1,0:T(8,128)(2,1)S(1)}, u32[]{:S(2)}, u32[]{:S(2)}) collective-permute-start(bf16[16,64,384]{2,1,0:T(8,128)(2,1)S(1)} %all-to-all-done.3.own_ref), channel_id=1, source_target_pairs={{0,16},{16,0},{1,17},{17,1},{2,18},{18,2},{3,19},{19,3},{4,20},{20... | collective-permute-start | bytes 2359304 | tf_op jit(solution)/shard_map/ppermute | solution.py:185
  (12 other events, 20.4 us)
Sparse Core Ops, SparseCore 0:
  10.9 124.4 all-gather.5
  137.5 73.9 all-gather.3
  268.9 51.1 reduce-scatter.1

commit v4 on v3

--- a/solution.py
+++ b/solution.py
@@ -482,7 +482,11 @@
 
 
 def dnormed_kernel(order_ref, a_ref, b_ref, as_ref, bs_ref, ag_ref, bg_ref, aq_ref, bq_ref, gu_ref, qkv_ref, *refs):
-    *far_refs, out_ref, sums_ref = refs if len(refs) == 2 else (*refs[:-2], refs[-1], refs[-2])
+    if len(refs) == 2:
+        far_refs, (out_ref, sums_ref) = (), refs
+    else:
+        keep_ref, got_ref, *far_refs, branch_ref, sums_ref, out_ref = refs
+        branch_ref[...] = (keep_ref[...] + got_ref[...].astype(f32)).astype(bf16)
     step = pl.program_id(0)
     gateup = jnp.concatenate([ag_ref[...], bg_ref[...]], axis=0)
     fused = jnp.concatenate([aq_ref[...], bq_ref[...]], axis=0)
@@ -510,7 +514,7 @@
             far_ref[...] = out_ref[...]
 
 
-def dnormed_share(order, *others, gathered, stats, dgateup, dfused, gu, qkv, far):
+def dnormed_share(order, *others, gathered, stats, dgateup, dfused, gu, qkv, far=()):
     width = gathered.shape[2]
     count = order.shape[0]
     step = 2 * LANES
@@ -519,11 +523,14 @@
     if far:
         outs = [pl.BlockSpec((step, width), lambda i, order: (0, 0)) for _ in range(count // 2)]
         shapes = [jax.ShapeDtypeStruct((step, width), bf16) for _ in range(count // 2)]
+        part = pl.BlockSpec((far[0].shape[0] // (count // 2), width), lambda i, order: (i, 0))
+        outs.append(part)
+        shapes.append(jax.ShapeDtypeStruct(far[0].shape, bf16))
     else:
         outs = [pl.BlockSpec((step, width), lambda i, order: (i, 0))]
         shapes = [jax.ShapeDtypeStruct((count * LANES, width), f32)]
     return pl.pallas_call(
-        ignoring(dnormed_kernel, 11, len(others)),
+        ignoring(dnormed_kernel, 11 + len(far), len(others)),
         name="dn_far" if far else "dn_near",
         grid_spec=pltpu.PrefetchScalarGridSpec(
             num_scalar_prefetch=1,
@@ -539,6 +546,7 @@
                 row(dfused, 1),
                 whole_block(gu),
                 whole_block(qkv),
+                *[part for _ in far],
                 *anywhere(others),
             ],
             out_specs=[*outs, pl.BlockSpec((8, width), lambda i, order: (0, 0))],
@@ -549,7 +557,7 @@
         cost_estimate=cost(
             2 * count * LANES * width * (dgateup.shape[1] + dfused.shape[1]), count * LANES * width * 8
         ),
-    )(order, gathered, gathered, stats, stats, dgateup, dgateup, dfused, dfused, gu, qkv, *others)
+    )(order, gathered, gathered, stats, stats, dgateup, dgateup, dfused, dfused, gu, qkv, *far, *others)
 
 
 def combine_kernel(near_ref, *refs):
@@ -581,25 +589,6 @@
         compiler_params=limits(48),
         cost_estimate=cost(0, rows * width * 9),
     )(near, *got, *others)
-
-
-def add_kernel(keep_ref, got_ref, out_ref):
-    out_ref[...] = (keep_ref[...] + got_ref[...].astype(f32)).astype(bf16)
-
-
-def add_up(keep, got, *others):
-    rows, width = keep.shape
-    row = pl.BlockSpec((LANES, width), lambda i: (i, 0))
-    return pl.pallas_call(
-        ignoring(add_kernel, 2, len(others)),
-        name="add_up",
-        grid=(rows // LANES,),
-        in_specs=[row, row, *anywhere(others)],
-        out_specs=row,
-        out_shape=jax.ShapeDtypeStruct((rows, width), bf16),
-        compiler_params=limits(16),
-        cost_estimate=cost(0, rows * width * 8),
-    )(keep, got, *others)
 
 
 def per_device(
@@ -703,13 +692,12 @@
     gu_got = other(gu_theirs)
     dfused, bias_sums = attend_back(fused, probs, dcontext, tables, tp, gu_theirs)
     share = functools.partial(dnormed_share, gathered=gathered, stats=stats, dgateup=dgateup, dfused=dfused, gu=gu_cols, qkv=qkv_cols)
-    branch = add_up(branch_keep, branch_got, dfused)
+    *far_shares, branch, far_sums = share(order[1], far=(branch_keep, branch_got))
     branch_own = lax.psum_scatter(branch, "z", scatter_dimension=0, tiled=True)
     tokens32 = tokens.astype(f32)
     block_output = (tokens32 + branch_own.astype(f32)).astype(bf16)
-    *far_shares, far_sums = share(order[1], branch, far=True)
     got = [shifted(far_share, "c", cs, 1) for far_share in far_shares]
-    near_share, near_sums = share(order[0], *far_shares, far=False)
+    near_share, near_sums = share(order[0], *far_shares)
     gain_sum, bias_sum = near_sums[0] + far_sums[0], near_sums[1] + far_sums[1]
 
     per_row = own_qkv // half

time: 437 us -> 434 us (level)
    pallas_call x3 -> x2, Pallas kernels: 29.9 us -> 26.7 us  [dnormed_share(): pl.pallas_call(ignoring(dnormed_kernel, 11 + len(far), len(others)), name...]
    unnamed x71 -> x57, local copies, waits for them, and re-layouts: 14.1 us -> 14.4 us
  transfers between devices with their start and end apart: 25 -> 25, of which waited for: 13 -> 13; matrix products, arithmetic and copies ran while one was open for 11% -> 11% of each run, Pallas kernels for 30% -> 29%
where the time goes in v4:
time: 434 us; the launch traced here: 433 us
  waiting for transfers between devices  169 us (39%)
  Pallas kernels  130 us (30%)
  starting transfers between devices  53.8 us (12%)
  other arithmetic  33.1 us (8%)
  local copies, waits for them, and re-layouts  32.4 us (7%)
  between operations  14.3 us (3%)
    all_to_all x2, waiting for transfers between devices, to_columns(): own = lax.all_to_all(own, TP, 0, 0, tiled=True)  78.5 us
    ppermute x18, waiting for transfers between devices, shifted(): return lax.ppermute(x, axis, [(i, (i + step) % size) for i in range(size)])  75.9 us
    pallas_call x2, Pallas kernels, dnormed_share(): pl.pallas_call(ignoring(dnormed_kernel, 11 + len(far), len(others)), name...  26.7 us
    ppermute x18, starting transfers between devices, shifted(): return lax.ppermute(x, axis, [(i, (i + step) % size) for i in range(size)])  21.9 us
    pallas_call x1, Pallas kernels, gate_forward(): pl.pallas_call(gate_kernel, name='gate_fwd', grid=(count // 2,), in_specs...  21.1 us
    pallas_call x2, Pallas kernels, split_grads(): pl.pallas_call(ignoring(grads_kernel, 3, len(others)), name='grads', grid...  20.1 us
    all_to_all x2, starting transfers between devices, to_columns(): own = lax.all_to_all(own, TP, 0, 0, tiled=True)  16 us
    unnamed x57, local copies, waits for them, and re-layouts  14.4 us
  transfers between devices with their start and end apart: 25, of which 13 were waited for; matrix products, arithmetic and copies ran while one was open for 11% of the time, Pallas kernels for 29%

profile of v4, /device:TPU:0, one launch (start us, length us, event | category | flops | bytes accessed | tf_op | source)
XLA Modules:
  0.0 432.7 jit_solution(12119403580445982474)
XLA Ops:
  8.6 1.9 pad_maximum_fusion
  11.3 1.8 copy-done.11
  13.1 2.0 pack.2
  15.1 7.5 %all-to-all-start = ((bf16[16,64,768]{2,1,0:T(8,128)(2,1)}), bf16[16,64,768]{2,1,0:T(8,128)(2,1)S(1)}, u32[]{:S(2)}, u32[]{:S(2)}) async-start(bf16[16,64,768]{2,1,0:T(8,128)(2,1)} %pack.2), calls=%async_computation | async-start | bytes 3145728 | tf_op jit(solution)/shard_map/all_to_all | solution.py:642
  24.2 48.9 %all-to-all-done = bf16[16,64,768]{2,1,0:T(8,128)(2,1)S(1)} async-done(((bf16[16,64,768]{2,1,0:T(8,128)(2,1)}), bf16[16,64,768]{2,1,0:T(8,128)(2,1)S(1)}, u32[]{:S(2)}, u32[]{:S(2)}) %all-to-all-start) | async-done | bytes 1572896 | tf_op jit(solution)/shard_map/all_to_all | solution.py:642
  73.1 8.5 %all-to-all-start.1 = ((bf16[16,64,384]{2,1,0:T(8,128)(2,1)}), bf16[16,64,384]{2,1,0:T(8,128)(2,1)S(1)}, u32[]{:S(2)}, u32[]{:S(2)}) async-start(bf16[16,64,384]{2,1,0:T(8,128)(2,1)} %pack.3), calls=%async_computation.1 | async-start | bytes 1572864 | tf_op jit(solution)/shard_map/all_to_all | solution.py:642
  81.6 1.8 collective-permute-start
  83.5 29.6 %all-to-all-done.1 = bf16[16,64,384]{2,1,0:T(8,128)(2,1)S(1)} async-done(((bf16[16,64,384]{2,1,0:T(8,128)(2,1)}), bf16[16,64,384]{2,1,0:T(8,128)(2,1)S(1)}, u32[]{:S(2)}, u32[]{:S(2)}) %all-to-all-start.1) | async-done | bytes 786464 | tf_op jit(solution)/shard_map/all_to_all | solution.py:642
  113.0 1.7 collective-permute-start.1
  114.9 3.2 maximum_maximum_fusion.w_ref.refs_3_
  118.5 16.9 %collective-permute-done.1 = bf16[16,64,384]{2,1,0:T(8,128)(2,1)} collective-permute-done((bf16[16,64,384]{2,1,0:T(8,128)(2,1)S(1)}, bf16[16,64,384]{2,1,0:T(8,128)(2,1)}, u32[]{:S(2)}, u32[]{:S(2)}) %collective-permute-start.1) | collective-permute-done | bytes 786464 | tf_op jit(solution)/shard_map/ppermute | solution.py:185
  136.7 2.2 broadcast_in_dim.91
  140.1 2.7 bitcast_dynamic-update-slice_fusion
  145.4 21.1 %gate_fwd.1 = (f32[2048,128]{1,0:T(8,128)}, bf16[2048,2048]{1,0:T(8,128)(2,1)}, f32[2048,384]{1,0:T(8,128)}, f32[2048,384]{1,0:T(8,128)}, bf16[2048,384]{1,0:T(8,128)(2,1)}, /*index=5*/f32[2048,384]{1,0:T(8,128)}) custom-call(bf16[16,144,2048]{2,1,0:T(8,128)(2,1)} %bitcast.77, bf16[16,144,2048]{2,1,0:T(8,128)(2,1)} %bitcast.78, f32[1,2048]{1,0:T(1,128)} %bitcast.90, ...), custom_call_target="tpu_custom_call" | custom-call | flops 1 | bytes 1 | tf_op jit(solution)/shard_map/gate_fwd/pallas_call | solution.py:312
  167.5 3.8 fusion
  171.4 3.3 attend.1
  174.8 5.5 %branch_far.1 = bf16[1024,2048]{1,0:T(8,128)(2,1)} custom-call(s32[8]{0:T(128)S(1)} %stack.134.order_ref, bf16[2048,128]{1,0:T(8,128)(2,1)S(1)} %get-tuple-element.43.ac_ref.bc_ref.refs_0_, bf16[2048,128]{1,0:T(8,128)(2,1)S(1)} %get-tuple-element.43.ac_ref.bc_ref.refs_0_, bf16[2048,384]{1,0:T(8,128)(2,1)S(1)} %copy-done.1, bf16[2048,384]{1,0:T(8,128)(2,1)S(1)} %copy-done.1, ...), custom_call_target="tpu_custom_call" | custom-call | flops 1 | bytes 1 | tf_op jit(solution)/shard_map/branch_far/pallas_call | solution.py:372
  180.4 7.4 %collective-permute-done.2.refs_0_ = bf16[1024,2048]{1,0:T(8,128)(2,1)} collective-permute-done((bf16[1024,2048]{1,0:T(8,128)(2,1)}, bf16[1024,2048]{1,0:T(8,128)(2,1)}, u32[]{:S(2)}, u32[]{:S(2)}) %collective-permute-start.2) | collective-permute-done | bytes 4194336 | tf_op jit(solution)/shard_map/ppermute | solution.py:185
  187.8 8.9 %branch_near.1 = (bf16[512,2048]{1,0:T(8,128)(2,1)}, f32[512,2048]{1,0:T(8,128)}) custom-call(s32[8]{0:T(128)S(1)} %stack.125.order_ref, bf16[2048,128]{1,0:T(8,128)(2,1)S(1)} %get-tuple-element.43.ac_ref.bc_ref.refs_0_, bf16[2048,128]{1,0:T(8,128)(2,1)S(1)} %get-tuple-element.43.ac_ref.bc_ref.refs_0_, bf16[2048,384]{1,0:T(8,128)(2,1)S(1)} %copy-done.1, ...), custom_call_target="tpu_custom_call" | custom-call | flops 1 | bytes 1 | tf_op jit(solution)/shard_map/branch_near/pallas_call | solution.py:372
  196.6 2.3 collective-permute-start.3
  198.9 12.6 %all-gather.4.cloned.1.call-done.refs_0_.refs_2_ = bf16[2048,2048]{1,0:T(8,128)(2,1)} async-done(((bf16[128,2048]{1,0:T(8,128)(2,1)}), bf16[2048,2048]{1,0:T(8,128)(2,1)}) %all-gather.4.cloned.1.call-update) | async-done | bytes 8388624 | tf_op jit(solution)/shard_map/all_gather | solution.py:636
  213.1 11.4 %gate_back.1 = (bf16[2048,768]{1,0:T(8,128)(2,1)}, bf16[2048,128]{1,0:T(8,128)(2,1)S(1)}) custom-call(bf16[2048,2048]{1,0:T(8,128)(2,1)} %all-gather.4.cloned.1.call-done.refs_0_.refs_2_, f32[2048,384]{1,0:T(8,128)} %get-tuple-element.40.refs_1_, f32[2048,384]{1,0:T(8,128)} %get-tuple-element.41.refs_2_, bf16[512,2048]{1,0:T(8,128)(2,1)S(1)} %copy-done.3, ...), custom_call_target="tpu_custom_call" | custom-call | flops 1 | bytes 1 | tf_op jit(solution)/shard_map/gate_back/pallas_call | solution.py:409
  225.3 11.3 %grads.2 = (f32[16,64,768]{2,1,0:T(8,128)}, bf16[16,64,768]{2,1,0:T(8,128)(2,1)}) custom-call(s32[1]{0:T(128)} %bitcast.12.part_ref.refs_0_, bf16[2048,2048]{1,0:T(8,128)(2,1)} %get-tuple-element.50.refs_1_, bf16[2048,768]{1,0:T(8,128)(2,1)} %get-tuple-element.46.refs_2_.refs_5_.refs_6_), custom_call_target="tpu_custom_call" | custom-call | flops 1 | bytes 1 | tf_op jit(solution)/shard_map/grads/pallas_call | solution.py:438
  244.2 5.4 %attend_back.1 = (bf16[2048,384]{1,0:T(8,128)(2,1)S(1)}, f32[1,384]{1,0:T(1,128)S(1)}) custom-call(bf16[2048,384]{1,0:T(8,128)(2,1)S(1)} %copy-done.17, f32[16,256,128]{2,1,0:T(8,128)S(1)} %copy-done.13, bf16[2048,128]{1,0:T(8,128)(2,1)S(1)} %copy-done.19, f32[2048,128]{1,0:T(8,128)S(1)} %copy-done.8, f32[2048,128]{1,0:T(8,128)S(1)} %copy-done.6, ...), custom_call_target="tpu_custom_call" | custom-call | flops 536870912 | bytes 12288000 | tf_op jit(solution)/shard_map/attend_back/pallas_call | solution.py:164
  250.8 14.2 %dn_far.1 = (bf16[256,2048]{1,0:T(8,128)(2,1)}, bf16[256,2048]{1,0:T(8,128)(2,1)}, bf16[256,2048]{1,0:T(8,128)(2,1)}, bf16[256,2048]{1,0:T(8,128)(2,1)}, bf16[512,2048]{1,0:T(8,128)(2,1)}, /*index=5*/f32[8,2048]{1,0:T(8,128)}) custom-call(s32[8]{0:T(128)} %stack.116.refs_0_, bf16[16,144,2048]{2,1,0:T(8,128)(2,1)} %bitcast.79, ...), custom_call_target="tpu_custom_call" | custom-call | flops 1 | bytes 1 | tf_op jit(solution)/shard_map/dn_far/pallas_call | solution.py:532
  267.0 12.5 %dn_near.1 = (f32[1024,2048]{1,0:T(8,128)}, f32[8,2048]{1,0:T(8,128)}) custom-call(s32[8]{0:T(128)} %stack.143.refs_0_, bf16[16,144,2048]{2,1,0:T(8,128)(2,1)} %bitcast.81, bf16[16,144,2048]{2,1,0:T(8,128)(2,1)} %bitcast.82, f32[2048,128]{1,0:T(8,128)} %get-tuple-element.39.refs_3_.refs_4_, f32[2048,128]{1,0:T(8,128)} %get-tuple-element.39.refs_3_.refs_4_, ...), custom_call_target="tpu_custom_call" | custom-call | flops 1 | bytes 1 | tf_op jit(solution)/shard_map/dn_near/pallas_call | solution.py:532
  282.2 6.4 %combine.1 = (bf16[256,2048]{1,0:T(8,128)(2,1)}, bf16[256,2048]{1,0:T(8,128)(2,1)S(1)}, f32[512,2048]{1,0:T(8,128)}) custom-call(f32[1024,2048]{1,0:T(8,128)} %get-tuple-element.59.refs_0_, bf16[256,2048]{1,0:T(8,128)(2,1)S(1)} %collective-permute-done.4.refs_1_, bf16[256,2048]{1,0:T(8,128)(2,1)S(1)} %collective-permute-done.5.refs_2_, ...), custom_call_target="tpu_custom_call" | custom-call | flops 1 | bytes 1 | tf_op jit(solution)/shard_map/combine/pallas_call | solution.py:581
  290.3 1.9 copy-done.23
  292.2 3.4 add_convert_fusion.refs_3_
  295.6 5.2 %all-to-all-start.2 = ((bf16[16,64,768]{2,1,0:T(8,128)(2,1)}), bf16[16,64,768]{2,1,0:T(8,128)(2,1)}, u32[]{:S(2)}, u32[]{:S(2)}) async-start(bf16[16,64,768]{2,1,0:T(8,128)(2,1)} %add_convert_fusion.refs_3_), calls=%async_computation.3 | async-start | bytes 3145728 | tf_op jit(solution)/shard_map/all_to_all | solution.py:713
  300.9 8.7 %grads.3 = (f32[16,64,384]{2,1,0:T(8,128)}, bf16[16,64,384]{2,1,0:T(8,128)(2,1)}) custom-call(s32[1]{0:T(128)} %bitcast.12.part_ref.refs_0_, bf16[2048,2048]{1,0:T(8,128)(2,1)} %get-tuple-element.50.refs_1_, bf16[2048,384]{1,0:T(8,128)(2,1)} %copy-done, bf16[16,64,768]{2,1,0:T(8,128)(2,1)} %add_convert_fusion.refs_3_), custom_call_target="tpu_custom_call" | custom-call | flops 1 | bytes 1 | tf_op jit(solution)/shard_map/grads/pallas_call | solution.py:438
  309.6 1.7 collective-permute-start.15
  311.3 8.8 %rows.1.refs_3_ = bf16[480,2048]{1,0:T(8,128)(2,1)} custom-call(bf16[2048,128]{1,0:T(8,128)(2,1)} %copy-done.4, bf16[2048,384]{1,0:T(8,128)(2,1)} %get-tuple-element.44.ah_ref.bh_ref.refs_1_, bf16[2048,2048]{1,0:T(8,128)(2,1)} %all-gather.4.cloned.1.call-done.refs_0_.refs_2_, bf16[16,64,384]{2,1,0:T(8,128)(2,1)} %get-tuple-element.67.refs_3_), custom_call_target="tpu_custom_call" | custom-call | flops 1 | bytes 1 | tf_op jit(solution)/shard_map/rows/pallas_call | solution.py:467
  321.0 2.5 add_convert_fusion.3
  325.4 4.8 %collective-permute-done.15 = bf16[16,64,384]{2,1,0:T(8,128)(2,1)S(1)} collective-permute-done((bf16[16,64,384]{2,1,0:T(8,128)(2,1)}, bf16[16,64,384]{2,1,0:T(8,128)(2,1)S(1)}, u32[]{:S(2)}, u32[]{:S(2)}) %collective-permute-start.15) | collective-permute-done | bytes 786464 | tf_op jit(solution)/shard_map/ppermute | solution.py:185
  331.3 3.7 collective-permute-start.10
  335.0 19.4 %collective-permute-done.12 = bf16[256,2048]{1,0:T(8,128)(2,1)} collective-permute-done((bf16[256,2048]{1,0:T(8,128)(2,1)}, bf16[256,2048]{1,0:T(8,128)(2,1)}, u32[]{:S(2)}, u32[]{:S(2)}) %collective-permute-start.12) | collective-permute-done | bytes 1048608 | tf_op jit(solution)/shard_map/ppermute | solution.py:185
  354.3 2.3 add_convert_fusion.2
  356.6 2.6 collective-permute-start.13
  360.7 10.5 %all-to-all-start.3 = ((bf16[16,64,384]{2,1,0:T(8,128)(2,1)}), bf16[16,64,384]{2,1,0:T(8,128)(2,1)S(1)}, u32[]{:S(2)}, u32[]{:S(2)}) async-start(bf16[16,64,384]{2,1,0:T(8,128)(2,1)} %after.5), calls=%async_computation.4 | async-start | bytes 1572864 | tf_op jit(solution)/shard_map/all_to_all | solution.py:742
  372.4 2.9 convert_add_fusion
  375.3 1.9 slice.164
  378.3 18.9 %collective-permute-done.9 = bf16[128,2048]{1,0:T(8,128)(2,1)} collective-permute-done((bf16[128,2048]{1,0:T(8,128)(2,1)S(1)}, bf16[128,2048]{1,0:T(8,128)(2,1)}, u32[]{:S(2)}, u32[]{:S(2)}) %collective-permute-start.9) | collective-permute-done | bytes 524320 | tf_op jit(solution)/shard_map/ppermute | solution.py:185
  397.2 2.5 fusion.31
  405.5 1.9 convert_add_fusion.2
  407.4 6.1 %unpack.3 = f32[128,11264]{1,0:T(8,128)} custom-call(s32[1]{0:T(128)} %bitcast.12.part_ref.refs_0_, bf16[16,64,768]{2,1,0:T(8,128)(2,1)} %all-to-all-done.2.refs_1_.own_ref, bf16[16,64,768]{2,1,0:T(8,128)(2,1)S(1)} %collective-permute-done.14.other_ref), custom_call_target="tpu_custom_call" | custom-call | flops 1 | bytes 1 | tf_op jit(solution)/shard_map/unpack/pallas_call | solution.py:266
  416.5 6.2 %collective-permute-done.16.other_ref = bf16[16,64,384]{2,1,0:T(8,128)(2,1)S(1)} collective-permute-done((bf16[16,64,384]{2,1,0:T(8,128)(2,1)S(1)}, bf16[16,64,384]{2,1,0:T(8,128)(2,1)S(1)}, u32[]{:S(2)}, u32[]{:S(2)}) %collective-permute-start.16) | collective-permute-done | bytes 786464 | tf_op jit(solution)/shard_map/ppermute | solution.py:185
  422.7 3.4 unpack.2
  (155 shorter events, 44.4 us)
Async XLA Ops:
  7.2 135.6 %all-gather.6.cloned.1.call-start = ((), (), s32[]{:S(2)}) async-start(), calls=%async_computation.7 | async-start | bytes 10027008 | tf_op jit(solution)/shard_map/all_gather | solution.py:634
  10.6 200.9 %all-gather.4.cloned.1.call-start = ((), (), s32[]{:S(2)}) async-start(), calls=%async_computation.5 | async-start | bytes 8912896 | tf_op jit(solution)/shard_map/all_gather | solution.py:636
  11.3 1.8 copy-start.11
  15.1 7.5 %copy-start.14 = (bf16[128,6144]{1,0:T(8,128)(2,1)S(1)}, bf16[128,6144]{1,0:T(8,128)(2,1)}, u32[]{:S(2)}) copy-start(bf16[128,6144]{1,0:T(8,128)(2,1)} %own_ref.3) | copy-start | bytes 4718596
  15.1 57.9 %all-to-all-start = ((bf16[16,64,768]{2,1,0:T(8,128)(2,1)}), bf16[16,64,768]{2,1,0:T(8,128)(2,1)S(1)}, u32[]{:S(2)}, u32[]{:S(2)}) async-start(bf16[16,64,768]{2,1,0:T(8,128)(2,1)} %pack.2), calls=%async_computation | async-start | bytes 3145728 | tf_op jit(solution)/shard_map/all_to_all | solution.py:642
  73.1 40.0 %all-to-all-start.1 = ((bf16[16,64,384]{2,1,0:T(8,128)(2,1)}), bf16[16,64,384]{2,1,0:T(8,128)(2,1)S(1)}, u32[]{:S(2)}, u32[]{:S(2)}) async-start(bf16[16,64,384]{2,1,0:T(8,128)(2,1)} %pack.3), calls=%async_computation.1 | async-start | bytes 1572864 | tf_op jit(solution)/shard_map/all_to_all | solution.py:642
  81.6 279.2 %reduce-scatter.2.cloned.1.call-start = ((), (), s32[]{:S(2)}) async-start(), calls=%async_computation.6 | async-start | bytes 2621440 | tf_op jit(solution)/shard_map/reduce_scatter | solution.py:696
  81.6 58.5 %collective-permute-start = (bf16[16,64,768]{2,1,0:T(8,128)(2,1)S(1)}, bf16[16,64,768]{2,1,0:T(8,128)(2,1)}, u32[]{:S(2)}, u32[]{:S(2)}) collective-permute-start(bf16[16,64,768]{2,1,0:T(8,128)(2,1)S(1)} %all-to-all-done), channel_id=1, source_target_pairs={{0,16},{16,0},{1,17},{17,1},{2,18},{18,2},{3,19},{19,3},{4,20},{20... | collective-permute-start | bytes 4718600 | tf_op jit(solution)/shard_map/ppermute | solution.py:185
  113.0 22.4 %collective-permute-start.1 = (bf16[16,64,384]{2,1,0:T(8,128)(2,1)S(1)}, bf16[16,64,384]{2,1,0:T(8,128)(2,1)}, u32[]{:S(2)}, u32[]{:S(2)}) collective-permute-start(bf16[16,64,384]{2,1,0:T(8,128)(2,1)S(1)} %all-to-all-done.1), channel_id=1, source_target_pairs={{0,16},{16,0},{1,17},{17,1},{2,18},{18,2},{3,19},{19,3},{4,20},{20... | collective-permute-start | bytes 2359304 | tf_op jit(solution)/shard_map/ppermute | solution.py:185
  136.7 3.4 copy-start.20
  167.1 4.2 copy-start.10
  171.3 3.4 copy-start.5
  171.3 3.4 copy-start.7
  171.3 3.4 copy-start.1
  171.3 3.4 copy-start.2
  174.7 5.5 %copy-start.12 = (f32[16,256,128]{2,1,0:T(8,128)}, f32[16,256,128]{2,1,0:T(8,128)S(1)}, u32[]{:S(2)}) copy-start(f32[16,256,128]{2,1,0:T(8,128)S(1)} %get-tuple-element.48.refs_1_) | copy-start | bytes 6291460
  174.7 5.5 %copy-start.16 = (bf16[2048,384]{1,0:T(8,128)(2,1)}, bf16[2048,384]{1,0:T(8,128)(2,1)S(1)}, u32[]{:S(2)}) copy-start(bf16[2048,384]{1,0:T(8,128)(2,1)S(1)} %get-tuple-element.47.refs_0_) | copy-start | bytes 4718596
  174.7 13.0 %copy-start.4 = (bf16[2048,128]{1,0:T(8,128)(2,1)}, bf16[2048,128]{1,0:T(8,128)(2,1)S(1)}, u32[]{:S(2)}) copy-start(bf16[2048,128]{1,0:T(8,128)(2,1)S(1)} %get-tuple-element.43.ac_ref.bc_ref.refs_0_) | copy-start | bytes 1572868
  180.3 7.5 %collective-permute-start.2 = (bf16[1024,2048]{1,0:T(8,128)(2,1)}, bf16[1024,2048]{1,0:T(8,128)(2,1)}, u32[]{:S(2)}, u32[]{:S(2)}) collective-permute-start(bf16[1024,2048]{1,0:T(8,128)(2,1)} %branch_far.1), channel_id=1, source_target_pairs={{0,1},{1,0},{2,3},{3,2},{4,5},{5,4},{6,7},{7,6},{8,9},{9,8},{10,11... | collective-permute-start | bytes 12582920 | tf_op jit(solution)/shard_map/ppermute | solution.py:185
  196.6 54.2 %collective-permute-start.3 = (bf16[512,2048]{1,0:T(8,128)(2,1)}, bf16[512,2048]{1,0:T(8,128)(2,1)}, u32[]{:S(2)}, u32[]{:S(2)}) collective-permute-start(bf16[512,2048]{1,0:T(8,128)(2,1)} %get-tuple-element.45.refs_4_), channel_id=1, source_target_pairs={{0,2},{2,0},{1,3},{3,1},{4,6},{6,4},{5,7},{7,5},{8,10},{10,8},{9,1... | collective-permute-start | bytes 6291464 | tf_op jit(solution)/shard_map/ppermute | solution.py:185
  211.5 1.6 copy-start.3
  225.3 13.5 %copy-start.6 = (f32[2048,128]{1,0:T(8,128)S(1)}, f32[2048,128]{1,0:T(8,128)}, u32[]{:S(2)}) copy-start(f32[2048,128]{1,0:T(8,128)} %copy-done.5) | copy-start | bytes 3145732
  225.3 13.5 %copy-start.8 = (f32[2048,128]{1,0:T(8,128)S(1)}, f32[2048,128]{1,0:T(8,128)}, u32[]{:S(2)}) copy-start(f32[2048,128]{1,0:T(8,128)} %copy-done.7) | copy-start | bytes 3145732
  236.6 53.6 %collective-permute-start.11 = (bf16[16,64,768]{2,1,0:T(8,128)(2,1)}, bf16[16,64,768]{2,1,0:T(8,128)(2,1)}, u32[]{:S(2)}, u32[]{:S(2)}) collective-permute-start(bf16[16,64,768]{2,1,0:T(8,128)(2,1)} %get-tuple-element.51.refs_6_), channel_id=1, source_target_pairs={{0,16},{16,0},{1,17},{17,1},{2,18},{18,2},{3,19},{19,3},{4,20},{20... | collective-permute-start | bytes 4718600 | tf_op jit(solution)/shard_map/ppermute | solution.py:185
  238.8 1.6 copy-start.13
  240.4 1.4 copy-start.15
  265.0 17.2 %collective-permute-start.4 = (bf16[256,2048]{1,0:T(8,128)(2,1)}, bf16[256,2048]{1,0:T(8,128)(2,1)S(1)}, u32[]{:S(2)}, u32[]{:S(2)}) collective-permute-start(bf16[256,2048]{1,0:T(8,128)(2,1)} %get-tuple-element.55.refs_11_), channel_id=1, source_target_pairs={{0,1},{1,0},{2,3},{3,2},{4,5},{5,4},{6,7},{7,6},{8,9},{9,8},{10,11... | collective-permute-start | bytes 3145736 | tf_op jit(solution)/shard_map/ppermute | solution.py:185
  265.1 17.1 %collective-permute-start.5 = (bf16[256,2048]{1,0:T(8,128)(2,1)}, bf16[256,2048]{1,0:T(8,128)(2,1)S(1)}, u32[]{:S(2)}, u32[]{:S(2)}) collective-permute-start(bf16[256,2048]{1,0:T(8,128)(2,1)} %get-tuple-element.56.refs_12_), channel_id=1, source_target_pairs={{0,1},{1,0},{2,3},{3,2},{4,5},{5,4},{6,7},{7,6},{8,9},{9,8},{10,11... | collective-permute-start | bytes 3145736 | tf_op jit(solution)/shard_map/ppermute | solution.py:185
  265.6 16.6 %collective-permute-start.6 = (bf16[256,2048]{1,0:T(8,128)(2,1)}, bf16[256,2048]{1,0:T(8,128)(2,1)S(1)}, u32[]{:S(2)}, u32[]{:S(2)}) collective-permute-start(bf16[256,2048]{1,0:T(8,128)(2,1)} %get-tuple-element.57.refs_13_), channel_id=1, source_target_pairs={{0,1},{1,0},{2,3},{3,2},{4,5},{5,4},{6,7},{7,6},{8,9},{9,8},{10,11... | collective-permute-start | bytes 3145736 | tf_op jit(solution)/shard_map/ppermute | solution.py:185
  265.6 16.6 %collective-permute-start.7 = (bf16[256,2048]{1,0:T(8,128)(2,1)}, bf16[256,2048]{1,0:T(8,128)(2,1)}, u32[]{:S(2)}, u32[]{:S(2)}) collective-permute-start(bf16[256,2048]{1,0:T(8,128)(2,1)} %get-tuple-element.58.refs_14_), channel_id=1, source_target_pairs={{0,1},{1,0},{2,3},{3,2},{4,5},{5,4},{6,7},{7,6},{8,9},{9,8},{10,11... | collective-permute-start | bytes 3145736 | tf_op jit(solution)/shard_map/ppermute | solution.py:185
  289.6 31.4 %collective-permute-start.8 = (bf16[256,2048]{1,0:T(8,128)(2,1)}, bf16[256,2048]{1,0:T(8,128)(2,1)}, u32[]{:S(2)}, u32[]{:S(2)}) collective-permute-start(bf16[256,2048]{1,0:T(8,128)(2,1)} %get-tuple-element.61.refs_1_), channel_id=1, source_target_pairs={{0,2},{2,0},{1,3},{3,1},{4,6},{6,4},{5,7},{7,5},{8,10},{10,8},{9,1... | collective-permute-start | bytes 3145736 | tf_op jit(solution)/shard_map/ppermute | solution.py:185
  290.3 1.9 copy-start.23
  295.6 63.7 %all-to-all-start.2 = ((bf16[16,64,768]{2,1,0:T(8,128)(2,1)}), bf16[16,64,768]{2,1,0:T(8,128)(2,1)}, u32[]{:S(2)}, u32[]{:S(2)}) async-start(bf16[16,64,768]{2,1,0:T(8,128)(2,1)} %add_convert_fusion.refs_3_), calls=%async_computation.3 | async-start | bytes 3145728 | tf_op jit(solution)/shard_map/all_to_all | solution.py:713
  309.6 11.4 %copy-start.22 = (f32[512,2048]{1,0:T(8,128)S(1)}, f32[512,2048]{1,0:T(8,128)}, u32[]{:S(2)}) copy-start(f32[512,2048]{1,0:T(8,128)} %get-tuple-element.60) | copy-start | bytes 12582916
  309.6 20.6 %collective-permute-start.15 = (bf16[16,64,384]{2,1,0:T(8,128)(2,1)}, bf16[16,64,384]{2,1,0:T(8,128)(2,1)S(1)}, u32[]{:S(2)}, u32[]{:S(2)}) collective-permute-start(bf16[16,64,384]{2,1,0:T(8,128)(2,1)} %get-tuple-element.67.refs_3_), channel_id=1, source_target_pairs={{0,16},{16,0},{1,17},{17,1},{2,18},{18,2},{3,19},{19,3},{4,20},{20... | collective-permute-start | bytes 2359304 | tf_op jit(solution)/shard_map/ppermute | solution.py:185
  320.1 52.3 %collective-permute-start.17 = (bf16[480,2048]{1,0:T(8,128)(2,1)}, bf16[480,2048]{1,0:T(8,128)(2,1)}, u32[]{:S(2)}, u32[]{:S(2)}) collective-permute-start(bf16[480,2048]{1,0:T(8,128)(2,1)} %rows.1.refs_3_), channel_id=1, source_target_pairs={{0,16},{16,0},{1,17},{17,1},{2,18},{18,2},{3,19},{19,3},{4,20},{20... | collective-permute-start | bytes 5898248 | tf_op jit(solution)/shard_map/ppermute | solution.py:185
  323.5 1.4 copy-start.21
  323.5 6.7 %copy-start.27 = (f32[16,64,384]{2,1,0:T(8,128)S(1)}, f32[16,64,384]{2,1,0:T(8,128)}, u32[]{:S(2)}) copy-start(f32[16,64,384]{2,1,0:T(8,128)} %get-tuple-element.68) | copy-start | bytes 4718596
  323.5 30.9 %collective-permute-start.12 = (bf16[256,2048]{1,0:T(8,128)(2,1)}, bf16[256,2048]{1,0:T(8,128)(2,1)}, u32[]{:S(2)}, u32[]{:S(2)}) collective-permute-start(bf16[256,2048]{1,0:T(8,128)(2,1)} %after.4), channel_id=1, source_target_pairs={{0,2},{2,0},{1,3},{3,1},{4,6},{6,4},{5,7},{7,5},{8,10},{10,8},{9,1... | collective-permute-start | bytes 3145736 | tf_op jit(solution)/shard_map/ppermute | solution.py:185
  324.9 10.1 %copy-start.26 = (bf16[128,2048]{1,0:T(8,128)(2,1)S(1)}, bf16[128,2048]{1,0:T(8,128)(2,1)}, u32[]{:S(2)}) copy-start(bf16[128,2048]{1,0:T(8,128)(2,1)} %get-tuple-element.75.refs_1_) | copy-start | bytes 1572868
  331.3 46.9 %collective-permute-start.10 = (bf16[128,2048]{1,0:T(8,128)(2,1)}, bf16[128,2048]{1,0:T(8,128)(2,1)}, u32[]{:S(2)}, u32[]{:S(2)}) collective-permute-start(bf16[128,2048]{1,0:T(8,128)(2,1)} %get-tuple-element.74.refs_2_), channel_id=1, source_target_pairs={{0,12},{4,0},{8,4},{12,8},{1,13},{5,1},{9,5},{13,9},{2,14},{6,2},{... | collective-permute-start | bytes 1572872 | tf_op jit(solution)/shard_map/ppermute | solution.py:185
  335.0 62.2 %collective-permute-start.9 = (bf16[128,2048]{1,0:T(8,128)(2,1)S(1)}, bf16[128,2048]{1,0:T(8,128)(2,1)}, u32[]{:S(2)}, u32[]{:S(2)}) collective-permute-start(bf16[128,2048]{1,0:T(8,128)(2,1)S(1)} %copy-done.26), channel_id=1, source_target_pairs={{0,8},{4,12},{8,0},{12,4},{1,9},{5,13},{9,1},{13,5},{2,10},{6,14},... | collective-permute-start | bytes 1572872 | tf_op jit(solution)/shard_map/ppermute | solution.py:185
  356.6 40.6 %collective-permute-start.13 = (bf16[128,2048]{1,0:T(8,128)(2,1)}, bf16[128,2048]{1,0:T(8,128)(2,1)}, u32[]{:S(2)}, u32[]{:S(2)}) collective-permute-start(bf16[128,2048]{1,0:T(8,128)(2,1)} %add_convert_fusion.2), channel_id=1, source_target_pairs={{0,4},{4,8},{8,12},{12,0},{1,5},{5,9},{9,13},{13,1},{2,6},{6,10},{... | collective-permute-start | bytes 1572872 | tf_op jit(solution)/shard_map/ppermute | solution.py:185
  359.3 46.2 %collective-permute-start.14 = (bf16[16,64,768]{2,1,0:T(8,128)(2,1)}, bf16[16,64,768]{2,1,0:T(8,128)(2,1)S(1)}, u32[]{:S(2)}, u32[]{:S(2)}) collective-permute-start(bf16[16,64,768]{2,1,0:T(8,128)(2,1)} %all-to-all-done.2.refs_1_.own_ref), channel_id=1, source_target_pairs={{0,16},{16,0},{1,17},{17,1},{2,18},{18,2},{3,19},{19,3},{4,20},{20... | collective-permute-start | bytes 4718600 | tf_op jit(solution)/shard_map/ppermute | solution.py:185
  360.7 42.4 %all-to-all-start.3 = ((bf16[16,64,384]{2,1,0:T(8,128)(2,1)}), bf16[16,64,384]{2,1,0:T(8,128)(2,1)S(1)}, u32[]{:S(2)}, u32[]{:S(2)}) async-start(bf16[16,64,384]{2,1,0:T(8,128)(2,1)} %after.5), calls=%async_computation.4 | async-start | bytes 1572864 | tf_op jit(solution)/shard_map/all_to_all | solution.py:742
  397.2 3.7 copy-start.24
  397.2 3.7 copy-start.25
  403.2 19.6 %collective-permute-start.16 = (bf16[16,64,384]{2,1,0:T(8,128)(2,1)S(1)}, bf16[16,64,384]{2,1,0:T(8,128)(2,1)S(1)}, u32[]{:S(2)}, u32[]{:S(2)}) collective-permute-start(bf16[16,64,384]{2,1,0:T(8,128)(2,1)S(1)} %all-to-all-done.3.own_ref), channel_id=1, source_target_pairs={{0,16},{16,0},{1,17},{17,1},{2,18},{18,2},{3,19},{19,3},{4,20},{20... | collective-permute-start | bytes 2359304 | tf_op jit(solution)/shard_map/ppermute | solution.py:185
  (5 other events, 5.4 us)
Sparse Core Ops, SparseCore 0:
  10.9 124.4 all-gather.5
  137.5 73.9 all-gather.3
  266.2 51.2 reduce-scatter.1

commit v5 on v4

--- a/solution.py
+++ b/solution.py
@@ -628,32 +628,12 @@
 
     small = jnp.concatenate([ln_gain, ln_bias, b_qkv, segments[0].astype(bf16)])
     of_params = 2 * rows + b_qkv.shape[0]
-    small_rows = up_to(-(-small.shape[0] // width), 16)
+    small_rows = up_to(-(-small.shape[0] // width), 8)
     small_rows_of = jnp.pad(small, (0, small_rows * width - small.shape[0])).reshape(small_rows, width)
     packed = jnp.concatenate([tokens, small_rows_of], axis=0)
     gathered = lax.all_gather(packed, TP, axis=0, tiled=False)
 
     cotangent_all = lax.all_gather(cotangent, TP, axis=0, tiled=True)
-
-    def other(own):
-        return shifted(own, "replica", groups, 1)
-
-    def to_columns(own):
-        own = lax.all_to_all(own, TP, 0, 0, tiled=True)
-        whole = jnp.zeros((tp, groups, half, own.shape[-1]), bf16)
-        whole = lax.dynamic_update_slice(whole, own[:, None], (0, part, 0, 0))
-        whole = lax.dynamic_update_slice(whole, other(own)[:, None], (0, 1 - part, 0, 0))
-        whole = whole.reshape(tp, rows, own.shape[-1])
-        if outer > 1:
-            whole = lax.all_gather(whole, "outer", axis=1, tiled=False)
-        return whole.reshape(width, own.shape[-1])
-
-    gu_cols = to_columns(pack(w_gateup, parts, groups, 2, tp, own_ffn, wide))
-    qkv_cols = to_columns(pack(w_qkv, parts, groups, 3, tp, PAIR, PAIR))
-    if outer > 1:
-        w_out = lax.all_gather(w_out, "outer", axis=0, tiled=True)
-        w_down = lax.all_gather(w_down, "outer", axis=0, tiled=True)
-    w_rows = jnp.concatenate([w_out, w_down, jnp.zeros((wide - own_ffn, width), bf16)], axis=0)
 
     vectors = gathered[:, length:, :].reshape(tp, -1)[:, : small.shape[0]]
     seg_all = vectors[:, of_params:].astype(jnp.int32)
@@ -666,6 +646,29 @@
     qkv_bias = vectors[:, 2 * rows :].reshape(3, tp, PAIR).astype(f32)
     my_bias = lax.dynamic_index_in_dim(qkv_bias, me, 1, keepdims=False).reshape(1, own_qkv)
     tables = rotary_tables(seg_all)
+
+    def other(own):
+        return shifted(own, "replica", groups, 1)
+
+    def to_columns(own, *others):
+        own = lax.all_to_all(own, TP, 0, 0, tiled=True)
+        whole = jnp.zeros((tp, groups, half, own.shape[-1]), bf16)
+        whole = lax.dynamic_update_slice(whole, own[:, None], (0, part, 0, 0))
+        moved = other(own)
+        if others:
+            moved = after(moved, *others)
+        whole = lax.dynamic_update_slice(whole, moved[:, None], (0, 1 - part, 0, 0))
+        whole = whole.reshape(tp, rows, own.shape[-1])
+        if outer > 1:
+            whole = lax.all_gather(whole, "outer", axis=1, tiled=False)
+        return whole.reshape(width, own.shape[-1])
+
+    gu_cols = to_columns(pack(w_gateup, parts, groups, 2, tp, own_ffn, wide))
+    qkv_cols = to_columns(pack(w_qkv, parts, groups, 3, tp, PAIR, PAIR), *tables)
+    if outer > 1:
+        w_out = lax.all_gather(w_out, "outer", axis=0, tiled=True)
+        w_down = lax.all_gather(w_down, "outer", axis=0, tiled=True)
+    w_rows = jnp.concatenate([w_out, w_down, jnp.zeros((wide - own_ffn, width), bf16)], axis=0)
 
     stats, normed, gate, up, hidden, joined = gate_forward(gathered, gain_all, bias_all, gu_cols, qkv_cols)
     fused, context, probs = attend(joined, my_bias, tables, tp)

time: 434 us -> 431 us (level)
  waiting for transfers between devices: 169 us -> 151 us
  local copies, waits for them, and re-layouts: 32.4 us -> 41 us
    ppermute x18, waiting for transfers between devices: 75.9 us -> 57.1 us  [shifted(): return lax.ppermute(x, axis, [(i, (i + step) % size) for i in range(size)])]
    all_gather x1, waiting for transfers between devices: 0.01 us -> 8.92 us  [per_device(): gathered = lax.all_gather(packed, TP, axis=0, tiled=False)]
    unnamed x57 -> x65, local copies, waits for them, and re-layouts: 14.4 us -> 21.9 us
    all_gather x1, waiting for transfers between devices: 12.6 us -> 7.76 us  [per_device(): cotangent_all = lax.all_gather(cotangent, TP, axis=0, tiled=True)]
  transfers between devices with their start and end apart: 25 -> 25, of which waited for: 13 -> 12; matrix products, arithmetic and copies ran while one was open for 11% -> 12% of each run, Pallas kernels for 29% -> 30%
where the time goes in v5:
time: 431 us; the launch traced here: 429 us
  waiting for transfers between devices  151 us (35%)
  Pallas kernels  131 us (30%)
  starting transfers between devices  56.9 us (13%)
  local copies, waits for them, and re-layouts  41 us (10%)
  other arithmetic  35.3 us (8%)
  between operations  14.3 us (3%)
    all_to_all x2, waiting for transfers between devices, to_columns(): own = lax.all_to_all(own, TP, 0, 0, tiled=True)  75.6 us
    ppermute x18, waiting for transfers between devices, shifted(): return lax.ppermute(x, axis, [(i, (i + step) % size) for i in range(size)])  57.1 us
    pallas_call x2, Pallas kernels, dnormed_share(): pl.pallas_call(ignoring(dnormed_kernel, 11 + len(far), len(others)), name...  26.9 us
    ppermute x18, starting transfers between devices, shifted(): return lax.ppermute(x, axis, [(i, (i + step) % size) for i in range(size)])  23.9 us
    unnamed x65, local copies, waits for them, and re-layouts  21.9 us
    pallas_call x1, Pallas kernels, gate_forward(): pl.pallas_call(gate_kernel, name='gate_fwd', grid=(count // 2,), in_specs...  21 us
    pallas_call x2, Pallas kernels, split_grads(): pl.pallas_call(ignoring(grads_kernel, 3, len(others)), name='grads', grid...  20 us
    all_to_all x2, starting transfers between devices, to_columns(): own = lax.all_to_all(own, TP, 0, 0, tiled=True)  17.7 us
  transfers between devices with their start and end apart: 25, of which 12 were waited for; matrix products, arithmetic and copies ran while one was open for 12% of the time, Pallas kernels for 30%

profile of v5, /device:TPU:0, one launch (start us, length us, event | category | flops | bytes accessed | tf_op | source)
XLA Modules:
  0.0 429.0 jit_solution(3915523833843313664)
XLA Ops:
  8.6 1.9 pad_maximum_fusion
  11.3 1.8 copy-done.13
  13.1 2.0 pack.2
  15.1 7.6 %all-to-all-start = ((bf16[16,64,768]{2,1,0:T(8,128)(2,1)}), bf16[16,64,768]{2,1,0:T(8,128)(2,1)}, u32[]{:S(2)}, u32[]{:S(2)}) async-start(bf16[16,64,768]{2,1,0:T(8,128)(2,1)} %pack.2), calls=%async_computation | async-start | bytes 3145728 | tf_op jit(solution)/shard_map/all_to_all | solution.py:654
  24.2 47.9 %all-to-all-done = bf16[16,64,768]{2,1,0:T(8,128)(2,1)} async-done(((bf16[16,64,768]{2,1,0:T(8,128)(2,1)}), bf16[16,64,768]{2,1,0:T(8,128)(2,1)}, u32[]{:S(2)}, u32[]{:S(2)}) %all-to-all-start) | async-done | bytes 1572896 | tf_op jit(solution)/shard_map/all_to_all | solution.py:654
  72.1 10.1 %all-to-all-start.1 = ((bf16[16,64,384]{2,1,0:T(8,128)(2,1)}), bf16[16,64,384]{2,1,0:T(8,128)(2,1)S(1)}, u32[]{:S(2)}, u32[]{:S(2)}) async-start(bf16[16,64,384]{2,1,0:T(8,128)(2,1)} %pack.3), calls=%async_computation.1 | async-start | bytes 1572864 | tf_op jit(solution)/shard_map/all_to_all | solution.py:654
  86.0 27.8 %all-to-all-done.1 = bf16[16,64,384]{2,1,0:T(8,128)(2,1)S(1)} async-done(((bf16[16,64,384]{2,1,0:T(8,128)(2,1)}), bf16[16,64,384]{2,1,0:T(8,128)(2,1)S(1)}, u32[]{:S(2)}, u32[]{:S(2)}) %all-to-all-start.1) | async-done | bytes 786464 | tf_op jit(solution)/shard_map/all_to_all | solution.py:654
  115.8 2.0 broadcast_in_dim.91
  117.8 2.7 bitcast_dynamic-update-slice_fusion.1
  120.5 2.7 bitcast_dynamic-update-slice_fusion
  123.3 8.9 %all-gather.6.cloned.1.call-done = bf16[2176,2048]{1,0:T(8,128)(2,1)} async-done(((bf16[136,2048]{1,0:T(8,128)(2,1)}), bf16[2176,2048]{1,0:T(8,128)(2,1)}) %all-gather.6.cloned.1.call-update) | async-done | bytes 8912912 | tf_op jit(solution)/shard_map/all_gather | solution.py:634
  136.9 5.7 %fusion = (f32[2048,128]{1,0:T(8,128)}, f32[2048,128]{1,0:T(8,128)}, f32[2048,128]{1,0:T(8,128)}) fusion(f32[128]{0:T(128)S(1)} %fusion.29, f32[2048]{0:T(1024)S(1)} %convert_bitcast_fusion, pred[128]{0:T(512)(128)(4,1)S(1)} %get-tuple-element.91, pred[128]{0:T(512)(128)(4,1)S(1)} %get-tuple-element.92, pred[128]{0:T(512)(128)(4,1)S(1)} %broadcast_compare_fusion.1), kind=kLoop, calls=%fused_computation.12 | loop fusion | flops 1310720 | bytes 3154816 | tf_op jit(solution)/shard_map/jit(_where)/select_n | solution.py:52
  146.1 21.0 %gate_fwd.1 = (f32[2048,128]{1,0:T(8,128)}, bf16[2048,2048]{1,0:T(8,128)(2,1)}, f32[2048,384]{1,0:T(8,128)}, f32[2048,384]{1,0:T(8,128)}, bf16[2048,384]{1,0:T(8,128)(2,1)}, /*index=5*/f32[2048,384]{1,0:T(8,128)}) custom-call(bf16[16,136,2048]{2,1,0:T(8,128)(2,1)} %bitcast.77, bf16[16,136,2048]{2,1,0:T(8,128)(2,1)} %bitcast.78, f32[1,2048]{1,0:T(1,128)} %bitcast.90, ...), custom_call_target="tpu_custom_call" | custom-call | flops 1 | bytes 1 | tf_op jit(solution)/shard_map/gate_fwd/pallas_call | solution.py:312
  171.5 1.9 copy-done.12
  173.4 3.3 attend.1
  176.8 5.5 %branch_far.1 = bf16[1024,2048]{1,0:T(8,128)(2,1)} custom-call(s32[8]{0:T(128)S(1)} %stack.134.order_ref, bf16[2048,128]{1,0:T(8,128)(2,1)S(1)} %get-tuple-element.43.ac_ref.bc_ref.refs_0_, bf16[2048,128]{1,0:T(8,128)(2,1)S(1)} %get-tuple-element.43.ac_ref.bc_ref.refs_0_, bf16[2048,384]{1,0:T(8,128)(2,1)S(1)} %copy-done.1, bf16[2048,384]{1,0:T(8,128)(2,1)S(1)} %copy-done.1, ...), custom_call_target="tpu_custom_call" | custom-call | flops 1 | bytes 1 | tf_op jit(solution)/shard_map/branch_far/pallas_call | solution.py:372
  182.6 7.2 %collective-permute-done.2.refs_0_ = bf16[1024,2048]{1,0:T(8,128)(2,1)} collective-permute-done((bf16[1024,2048]{1,0:T(8,128)(2,1)}, bf16[1024,2048]{1,0:T(8,128)(2,1)}, u32[]{:S(2)}, u32[]{:S(2)}) %collective-permute-start.2) | collective-permute-done | bytes 4194336 | tf_op jit(solution)/shard_map/ppermute | solution.py:185
  189.7 8.9 %branch_near.1 = (bf16[512,2048]{1,0:T(8,128)(2,1)}, f32[512,2048]{1,0:T(8,128)}) custom-call(s32[8]{0:T(128)S(1)} %stack.125.order_ref, bf16[2048,128]{1,0:T(8,128)(2,1)S(1)} %get-tuple-element.43.ac_ref.bc_ref.refs_0_, bf16[2048,128]{1,0:T(8,128)(2,1)S(1)} %get-tuple-element.43.ac_ref.bc_ref.refs_0_, bf16[2048,384]{1,0:T(8,128)(2,1)S(1)} %copy-done.1, ...), custom_call_target="tpu_custom_call" | custom-call | flops 1 | bytes 1 | tf_op jit(solution)/shard_map/branch_near/pallas_call | solution.py:372
  198.6 1.8 collective-permute-start.3
  200.4 7.8 %all-gather.4.cloned.1.call-done.refs_0_.refs_2_ = bf16[2048,2048]{1,0:T(8,128)(2,1)} async-done(((bf16[128,2048]{1,0:T(8,128)(2,1)}), bf16[2048,2048]{1,0:T(8,128)(2,1)}) %all-gather.4.cloned.1.call-update) | async-done | bytes 8388624 | tf_op jit(solution)/shard_map/all_gather | solution.py:636
  209.8 11.4 %gate_back.1 = (bf16[2048,768]{1,0:T(8,128)(2,1)}, bf16[2048,128]{1,0:T(8,128)(2,1)S(1)}) custom-call(bf16[2048,2048]{1,0:T(8,128)(2,1)} %all-gather.4.cloned.1.call-done.refs_0_.refs_2_, f32[2048,384]{1,0:T(8,128)} %get-tuple-element.40.refs_1_, f32[2048,384]{1,0:T(8,128)} %get-tuple-element.41.refs_2_, bf16[512,2048]{1,0:T(8,128)(2,1)S(1)} %copy-done.3, ...), custom_call_target="tpu_custom_call" | custom-call | flops 1 | bytes 1 | tf_op jit(solution)/shard_map/gate_back/pallas_call | solution.py:409
  221.2 11.2 %grads.2 = (f32[16,64,768]{2,1,0:T(8,128)}, bf16[16,64,768]{2,1,0:T(8,128)(2,1)}) custom-call(s32[1]{0:T(128)} %bitcast.12.part_ref.refs_0_, bf16[2048,2048]{1,0:T(8,128)(2,1)} %get-tuple-element.50.refs_1_, bf16[2048,768]{1,0:T(8,128)(2,1)} %get-tuple-element.46.refs_2_.refs_5_.refs_6_), custom_call_target="tpu_custom_call" | custom-call | flops 1 | bytes 1 | tf_op jit(solution)/shard_map/grads/pallas_call | solution.py:438
  240.2 5.4 %attend_back.1 = (bf16[2048,384]{1,0:T(8,128)(2,1)S(1)}, f32[1,384]{1,0:T(1,128)S(1)}) custom-call(bf16[2048,384]{1,0:T(8,128)(2,1)S(1)} %copy-done.19, f32[16,256,128]{2,1,0:T(8,128)S(1)} %copy-done.15, bf16[2048,128]{1,0:T(8,128)(2,1)S(1)} %get-tuple-element.49.refs_2_, f32[2048,128]{1,0:T(8,128)S(1)} %copy-done.8, f32[2048,128]{1,0:T(8,128)S(1)} %copy-done.6, ...), custom_call_target="tpu_custom_call" | custom-call | flops 536870912 | bytes 12288000 | tf_op jit(solution)/shard_map/attend_back/pallas_call | solution.py:164
  246.8 14.4 %dn_far.1 = (bf16[256,2048]{1,0:T(8,128)(2,1)}, bf16[256,2048]{1,0:T(8,128)(2,1)}, bf16[256,2048]{1,0:T(8,128)(2,1)}, bf16[256,2048]{1,0:T(8,128)(2,1)}, bf16[512,2048]{1,0:T(8,128)(2,1)}, /*index=5*/f32[8,2048]{1,0:T(8,128)}) custom-call(s32[8]{0:T(128)} %stack.116.refs_0_, bf16[16,136,2048]{2,1,0:T(8,128)(2,1)} %bitcast.79, ...), custom_call_target="tpu_custom_call" | custom-call | flops 1 | bytes 1 | tf_op jit(solution)/shard_map/dn_far/pallas_call | solution.py:532
  263.3 12.5 %dn_near.1 = (f32[1024,2048]{1,0:T(8,128)}, f32[8,2048]{1,0:T(8,128)}) custom-call(s32[8]{0:T(128)} %stack.143.refs_0_, bf16[16,136,2048]{2,1,0:T(8,128)(2,1)} %bitcast.81, bf16[16,136,2048]{2,1,0:T(8,128)(2,1)} %bitcast.82, f32[2048,128]{1,0:T(8,128)} %get-tuple-element.39.refs_3_.refs_4_, f32[2048,128]{1,0:T(8,128)} %get-tuple-element.39.refs_3_.refs_4_, ...), custom_call_target="tpu_custom_call" | custom-call | flops 1 | bytes 1 | tf_op jit(solution)/shard_map/dn_near/pallas_call | solution.py:532
  278.5 6.4 %combine.1 = (bf16[256,2048]{1,0:T(8,128)(2,1)}, bf16[256,2048]{1,0:T(8,128)(2,1)S(1)}, f32[512,2048]{1,0:T(8,128)}) custom-call(f32[1024,2048]{1,0:T(8,128)} %get-tuple-element.59.refs_0_, bf16[256,2048]{1,0:T(8,128)(2,1)S(1)} %collective-permute-done.4.refs_1_, bf16[256,2048]{1,0:T(8,128)(2,1)S(1)} %collective-permute-done.5.refs_2_, ...), custom_call_target="tpu_custom_call" | custom-call | flops 1 | bytes 1 | tf_op jit(solution)/shard_map/combine/pallas_call | solution.py:581
  287.6 1.9 copy-done.23
  289.5 3.5 add_convert_fusion.refs_3_
  292.9 4.7 %all-to-all-start.2 = ((bf16[16,64,768]{2,1,0:T(8,128)(2,1)}), bf16[16,64,768]{2,1,0:T(8,128)(2,1)}, u32[]{:S(2)}, u32[]{:S(2)}) async-start(bf16[16,64,768]{2,1,0:T(8,128)(2,1)} %add_convert_fusion.refs_3_), calls=%async_computation.3 | async-start | bytes 3145728 | tf_op jit(solution)/shard_map/all_to_all | solution.py:716
  297.7 8.8 %grads.3 = (f32[16,64,384]{2,1,0:T(8,128)}, bf16[16,64,384]{2,1,0:T(8,128)(2,1)}) custom-call(s32[1]{0:T(128)} %bitcast.12.part_ref.refs_0_, bf16[2048,2048]{1,0:T(8,128)(2,1)} %get-tuple-element.50.refs_1_, bf16[2048,384]{1,0:T(8,128)(2,1)} %copy-done, bf16[16,64,768]{2,1,0:T(8,128)(2,1)} %add_convert_fusion.refs_3_), custom_call_target="tpu_custom_call" | custom-call | flops 1 | bytes 1 | tf_op jit(solution)/shard_map/grads/pallas_call | solution.py:438
  307.6 8.8 %rows.1.refs_3_ = bf16[480,2048]{1,0:T(8,128)(2,1)} custom-call(bf16[2048,128]{1,0:T(8,128)(2,1)} %copy-done.9, bf16[2048,384]{1,0:T(8,128)(2,1)} %get-tuple-element.44.ah_ref.bh_ref.refs_1_, bf16[2048,2048]{1,0:T(8,128)(2,1)} %all-gather.4.cloned.1.call-done.refs_0_.refs_2_, bf16[16,64,384]{2,1,0:T(8,128)(2,1)} %get-tuple-element.67.refs_3_), custom_call_target="tpu_custom_call" | custom-call | flops 1 | bytes 1 | tf_op jit(solution)/shard_map/rows/pallas_call | solution.py:467
  317.6 2.5 add_convert_fusion.3
  320.1 2.6 collective-permute-start.12
  323.2 3.8 collective-permute-done.15
  328.1 3.7 collective-permute-start.10
  331.8 18.8 %collective-permute-done.12 = bf16[256,2048]{1,0:T(8,128)(2,1)} collective-permute-done((bf16[256,2048]{1,0:T(8,128)(2,1)}, bf16[256,2048]{1,0:T(8,128)(2,1)}, u32[]{:S(2)}, u32[]{:S(2)}) %collective-permute-start.12) | collective-permute-done | bytes 1048608 | tf_op jit(solution)/shard_map/ppermute | solution.py:185
  350.6 2.3 add_convert_fusion.2
  352.9 2.7 collective-permute-start.13
  357.0 10.4 %all-to-all-start.3 = ((bf16[16,64,384]{2,1,0:T(8,128)(2,1)}), bf16[16,64,384]{2,1,0:T(8,128)(2,1)S(1)}, u32[]{:S(2)}, u32[]{:S(2)}) async-start(bf16[16,64,384]{2,1,0:T(8,128)(2,1)} %after.7), calls=%async_computation.4 | async-start | bytes 1572864 | tf_op jit(solution)/shard_map/all_to_all | solution.py:745
  367.4 1.8 collective-permute-done.17
  369.2 2.9 convert_add_fusion
  372.1 1.9 slice.164
  375.0 18.2 %collective-permute-done.9 = bf16[128,2048]{1,0:T(8,128)(2,1)} collective-permute-done((bf16[128,2048]{1,0:T(8,128)(2,1)S(1)}, bf16[128,2048]{1,0:T(8,128)(2,1)}, u32[]{:S(2)}, u32[]{:S(2)}) %collective-permute-start.9) | collective-permute-done | bytes 524320 | tf_op jit(solution)/shard_map/ppermute | solution.py:185
  393.2 2.5 fusion.31
  402.3 1.9 convert_add_fusion.2
  404.3 6.1 %unpack.3 = f32[128,11264]{1,0:T(8,128)} custom-call(s32[1]{0:T(128)} %bitcast.12.part_ref.refs_0_, bf16[16,64,768]{2,1,0:T(8,128)(2,1)} %all-to-all-done.2.refs_1_.own_ref, bf16[16,64,768]{2,1,0:T(8,128)(2,1)S(1)} %collective-permute-done.14.other_ref), custom_call_target="tpu_custom_call" | custom-call | flops 1 | bytes 1 | tf_op jit(solution)/shard_map/unpack/pallas_call | solution.py:266
  413.4 5.7 %collective-permute-done.16.other_ref = bf16[16,64,384]{2,1,0:T(8,128)(2,1)S(1)} collective-permute-done((bf16[16,64,384]{2,1,0:T(8,128)(2,1)S(1)}, bf16[16,64,384]{2,1,0:T(8,128)(2,1)S(1)}, u32[]{:S(2)}, u32[]{:S(2)}) %collective-permute-start.16) | collective-permute-done | bytes 786464 | tf_op jit(solution)/shard_map/ppermute | solution.py:185
  419.1 3.4 unpack.2
  (164 shorter events, 56.2 us)
Async XLA Ops:
  7.2 125.0 %all-gather.6.cloned.1.call-start = ((), (), s32[]{:S(2)}) async-start(), calls=%async_computation.7 | async-start | bytes 9469952 | tf_op jit(solution)/shard_map/all_gather | solution.py:634
  10.5 197.6 %all-gather.4.cloned.1.call-start = ((), (), s32[]{:S(2)}) async-start(), calls=%async_computation.5 | async-start | bytes 8912896 | tf_op jit(solution)/shard_map/all_gather | solution.py:636
  11.3 1.8 copy-start.13
  15.1 7.6 %copy-start.16 = (bf16[128,6144]{1,0:T(8,128)(2,1)S(1)}, bf16[128,6144]{1,0:T(8,128)(2,1)}, u32[]{:S(2)}) copy-start(bf16[128,6144]{1,0:T(8,128)(2,1)} %own_ref.3) | copy-start | bytes 4718596
  15.1 57.0 %all-to-all-start = ((bf16[16,64,768]{2,1,0:T(8,128)(2,1)}), bf16[16,64,768]{2,1,0:T(8,128)(2,1)}, u32[]{:S(2)}, u32[]{:S(2)}) async-start(bf16[16,64,768]{2,1,0:T(8,128)(2,1)} %pack.2), calls=%async_computation | async-start | bytes 3145728 | tf_op jit(solution)/shard_map/all_to_all | solution.py:654
  22.7 61.6 %copy-start.29 = (bf16[352,2048]{1,0:T(8,128)(2,1)S(1)}, bf16[352,2048]{1,0:T(8,128)(2,1)}, u32[]{:S(2)}) copy-start(bf16[352,2048]{1,0:T(8,128)(2,1)} %param.18) | copy-start | bytes 4325380
  22.7 61.6 %copy-start.31 = (bf16[128,2048]{1,0:T(8,128)(2,1)S(1)}, bf16[128,2048]{1,0:T(8,128)(2,1)}, u32[]{:S(2)}) copy-start(bf16[128,2048]{1,0:T(8,128)(2,1)} %param.16) | copy-start | bytes 1572868
  72.1 41.7 %all-to-all-start.1 = ((bf16[16,64,384]{2,1,0:T(8,128)(2,1)}), bf16[16,64,384]{2,1,0:T(8,128)(2,1)S(1)}, u32[]{:S(2)}, u32[]{:S(2)}) async-start(bf16[16,64,384]{2,1,0:T(8,128)(2,1)} %pack.3), calls=%async_computation.1 | async-start | bytes 1572864 | tf_op jit(solution)/shard_map/all_to_all | solution.py:654
  82.2 274.8 %reduce-scatter.2.cloned.1.call-start = ((), (), s32[]{:S(2)}) async-start(), calls=%async_computation.6 | async-start | bytes 2621440 | tf_op jit(solution)/shard_map/reduce_scatter | solution.py:699
  82.2 38.3 %collective-permute-start = (bf16[16,64,768]{2,1,0:T(8,128)(2,1)}, bf16[16,64,768]{2,1,0:T(8,128)(2,1)}, u32[]{:S(2)}, u32[]{:S(2)}) collective-permute-start(bf16[16,64,768]{2,1,0:T(8,128)(2,1)} %all-to-all-done), channel_id=1, source_target_pairs={{0,16},{16,0},{1,17},{17,1},{2,18},{18,2},{3,19},{19,3},{4,20},{20... | collective-permute-start | bytes 4718600 | tf_op jit(solution)/shard_map/ppermute | solution.py:185
  113.8 28.9 %collective-permute-start.1 = (bf16[16,64,384]{2,1,0:T(8,128)(2,1)S(1)}, bf16[16,64,384]{2,1,0:T(8,128)(2,1)S(1)}, u32[]{:S(2)}, u32[]{:S(2)}) collective-permute-start(bf16[16,64,384]{2,1,0:T(8,128)(2,1)S(1)} %all-to-all-done.1), channel_id=1, source_target_pairs={{0,16},{16,0},{1,17},{17,1},{2,18},{18,2},{3,19},{19,3},{4,20},{20... | collective-permute-start | bytes 2359304 | tf_op jit(solution)/shard_map/ppermute | solution.py:185
  146.1 21.7 %copy-start.4 = (f32[2048,128]{1,0:T(8,128)S(1)}, f32[2048,128]{1,0:T(8,128)}, u32[]{:S(2)}) copy-start(f32[2048,128]{1,0:T(8,128)} %get-tuple-element.86.refs_3_.before_ref.refs_5_) | copy-start | bytes 3145732
  171.4 1.9 copy-start.12
  173.4 3.4 copy-start.1
  173.4 3.4 copy-start.2
  176.7 5.5 %copy-start.14 = (f32[16,256,128]{2,1,0:T(8,128)}, f32[16,256,128]{2,1,0:T(8,128)S(1)}, u32[]{:S(2)}) copy-start(f32[16,256,128]{2,1,0:T(8,128)S(1)} %get-tuple-element.48.refs_1_) | copy-start | bytes 6291460
  176.7 5.5 %copy-start.18 = (bf16[2048,384]{1,0:T(8,128)(2,1)}, bf16[2048,384]{1,0:T(8,128)(2,1)S(1)}, u32[]{:S(2)}) copy-start(bf16[2048,384]{1,0:T(8,128)(2,1)S(1)} %get-tuple-element.47.refs_0_) | copy-start | bytes 4718596
  176.7 13.0 %copy-start.9 = (bf16[2048,128]{1,0:T(8,128)(2,1)}, bf16[2048,128]{1,0:T(8,128)(2,1)S(1)}, u32[]{:S(2)}) copy-start(bf16[2048,128]{1,0:T(8,128)(2,1)S(1)} %get-tuple-element.43.ac_ref.bc_ref.refs_0_) | copy-start | bytes 1572868
  182.2 7.5 %collective-permute-start.2 = (bf16[1024,2048]{1,0:T(8,128)(2,1)}, bf16[1024,2048]{1,0:T(8,128)(2,1)}, u32[]{:S(2)}, u32[]{:S(2)}) collective-permute-start(bf16[1024,2048]{1,0:T(8,128)(2,1)} %branch_far.1), channel_id=1, source_target_pairs={{0,1},{1,0},{2,3},{3,2},{4,5},{5,4},{6,7},{7,6},{8,9},{9,8},{10,11... | collective-permute-start | bytes 12582920 | tf_op jit(solution)/shard_map/ppermute | solution.py:185
  198.6 48.1 %collective-permute-start.3 = (bf16[512,2048]{1,0:T(8,128)(2,1)}, bf16[512,2048]{1,0:T(8,128)(2,1)}, u32[]{:S(2)}, u32[]{:S(2)}) collective-permute-start(bf16[512,2048]{1,0:T(8,128)(2,1)} %get-tuple-element.45.refs_4_), channel_id=1, source_target_pairs={{0,2},{2,0},{1,3},{3,1},{4,6},{6,4},{5,7},{7,5},{8,10},{10,8},{9,1... | collective-permute-start | bytes 6291464 | tf_op jit(solution)/shard_map/ppermute | solution.py:185
  208.2 1.6 copy-start.3
  221.2 13.4 %copy-start.6 = (f32[2048,128]{1,0:T(8,128)S(1)}, f32[2048,128]{1,0:T(8,128)}, u32[]{:S(2)}) copy-start(f32[2048,128]{1,0:T(8,128)} %get-tuple-element.87.refs_2_.after_ref.refs_4_) | copy-start | bytes 3145732
  232.5 55.1 %collective-permute-start.11 = (bf16[16,64,768]{2,1,0:T(8,128)(2,1)}, bf16[16,64,768]{2,1,0:T(8,128)(2,1)}, u32[]{:S(2)}, u32[]{:S(2)}) collective-permute-start(bf16[16,64,768]{2,1,0:T(8,128)(2,1)} %get-tuple-element.51.refs_6_), channel_id=1, source_target_pairs={{0,16},{16,0},{1,17},{17,1},{2,18},{18,2},{3,19},{19,3},{4,20},{20... | collective-permute-start | bytes 4718600 | tf_op jit(solution)/shard_map/ppermute | solution.py:185
  235.8 1.6 copy-start.15
  237.4 1.4 copy-start.17
  238.8 1.4 copy-start.19
  261.2 17.3 %collective-permute-start.4 = (bf16[256,2048]{1,0:T(8,128)(2,1)}, bf16[256,2048]{1,0:T(8,128)(2,1)S(1)}, u32[]{:S(2)}, u32[]{:S(2)}) collective-permute-start(bf16[256,2048]{1,0:T(8,128)(2,1)} %get-tuple-element.55.refs_11_), channel_id=1, source_target_pairs={{0,1},{1,0},{2,3},{3,2},{4,5},{5,4},{6,7},{7,6},{8,9},{9,8},{10,11... | collective-permute-start | bytes 3145736 | tf_op jit(solution)/shard_map/ppermute | solution.py:185
  261.2 17.2 %collective-permute-start.5 = (bf16[256,2048]{1,0:T(8,128)(2,1)}, bf16[256,2048]{1,0:T(8,128)(2,1)S(1)}, u32[]{:S(2)}, u32[]{:S(2)}) collective-permute-start(bf16[256,2048]{1,0:T(8,128)(2,1)} %get-tuple-element.56.refs_12_), channel_id=1, source_target_pairs={{0,1},{1,0},{2,3},{3,2},{4,5},{5,4},{6,7},{7,6},{8,9},{9,8},{10,11... | collective-permute-start | bytes 3145736 | tf_op jit(solution)/shard_map/ppermute | solution.py:185
  261.7 16.7 %collective-permute-start.6 = (bf16[256,2048]{1,0:T(8,128)(2,1)}, bf16[256,2048]{1,0:T(8,128)(2,1)S(1)}, u32[]{:S(2)}, u32[]{:S(2)}) collective-permute-start(bf16[256,2048]{1,0:T(8,128)(2,1)} %get-tuple-element.57.refs_13_), channel_id=1, source_target_pairs={{0,1},{1,0},{2,3},{3,2},{4,5},{5,4},{6,7},{7,6},{8,9},{9,8},{10,11... | collective-permute-start | bytes 3145736 | tf_op jit(solution)/shard_map/ppermute | solution.py:185
  261.8 16.6 %collective-permute-start.7 = (bf16[256,2048]{1,0:T(8,128)(2,1)}, bf16[256,2048]{1,0:T(8,128)(2,1)}, u32[]{:S(2)}, u32[]{:S(2)}) collective-permute-start(bf16[256,2048]{1,0:T(8,128)(2,1)} %get-tuple-element.58.refs_14_), channel_id=1, source_target_pairs={{0,1},{1,0},{2,3},{3,2},{4,5},{5,4},{6,7},{7,6},{8,9},{9,8},{10,11... | collective-permute-start | bytes 3145736 | tf_op jit(solution)/shard_map/ppermute | solution.py:185
  285.8 31.8 %collective-permute-start.8 = (bf16[256,2048]{1,0:T(8,128)(2,1)}, bf16[256,2048]{1,0:T(8,128)(2,1)}, u32[]{:S(2)}, u32[]{:S(2)}) collective-permute-start(bf16[256,2048]{1,0:T(8,128)(2,1)} %get-tuple-element.61.refs_1_), channel_id=1, source_target_pairs={{0,2},{2,0},{1,3},{3,1},{4,6},{6,4},{5,7},{7,5},{8,10},{10,8},{9,1... | collective-permute-start | bytes 3145736 | tf_op jit(solution)/shard_map/ppermute | solution.py:185
  287.6 1.9 copy-start.23
  292.9 62.6 %all-to-all-start.2 = ((bf16[16,64,768]{2,1,0:T(8,128)(2,1)}), bf16[16,64,768]{2,1,0:T(8,128)(2,1)}, u32[]{:S(2)}, u32[]{:S(2)}) async-start(bf16[16,64,768]{2,1,0:T(8,128)(2,1)} %add_convert_fusion.refs_3_), calls=%async_computation.3 | async-start | bytes 3145728 | tf_op jit(solution)/shard_map/all_to_all | solution.py:716
  306.4 11.2 %copy-start.22 = (f32[512,2048]{1,0:T(8,128)S(1)}, f32[512,2048]{1,0:T(8,128)}, u32[]{:S(2)}) copy-start(f32[512,2048]{1,0:T(8,128)} %get-tuple-element.60) | copy-start | bytes 12582916
  306.4 20.6 %collective-permute-start.15 = (bf16[16,64,384]{2,1,0:T(8,128)(2,1)}, bf16[16,64,384]{2,1,0:T(8,128)(2,1)S(1)}, u32[]{:S(2)}, u32[]{:S(2)}) collective-permute-start(bf16[16,64,384]{2,1,0:T(8,128)(2,1)} %get-tuple-element.67.refs_3_), channel_id=1, source_target_pairs={{0,16},{16,0},{1,17},{17,1},{2,18},{18,2},{3,19},{19,3},{4,20},{20... | collective-permute-start | bytes 2359304 | tf_op jit(solution)/shard_map/ppermute | solution.py:185
  316.4 52.8 %collective-permute-start.17 = (bf16[480,2048]{1,0:T(8,128)(2,1)}, bf16[480,2048]{1,0:T(8,128)(2,1)}, u32[]{:S(2)}, u32[]{:S(2)}) collective-permute-start(bf16[480,2048]{1,0:T(8,128)(2,1)} %rows.1.refs_3_), channel_id=1, source_target_pairs={{0,16},{16,0},{1,17},{17,1},{2,18},{18,2},{3,19},{19,3},{4,20},{20... | collective-permute-start | bytes 5898248 | tf_op jit(solution)/shard_map/ppermute | solution.py:185
  320.1 2.6 copy-start.21
  320.1 6.9 %copy-start.28 = (f32[16,64,384]{2,1,0:T(8,128)S(1)}, f32[16,64,384]{2,1,0:T(8,128)}, u32[]{:S(2)}) copy-start(f32[16,64,384]{2,1,0:T(8,128)} %get-tuple-element.68) | copy-start | bytes 4718596
  320.1 30.5 %collective-permute-start.12 = (bf16[256,2048]{1,0:T(8,128)(2,1)}, bf16[256,2048]{1,0:T(8,128)(2,1)}, u32[]{:S(2)}, u32[]{:S(2)}) collective-permute-start(bf16[256,2048]{1,0:T(8,128)(2,1)} %after.6), channel_id=1, source_target_pairs={{0,2},{2,0},{1,3},{3,1},{4,6},{6,4},{5,7},{7,5},{8,10},{10,8},{9,1... | collective-permute-start | bytes 3145736 | tf_op jit(solution)/shard_map/ppermute | solution.py:185
  322.7 9.1 %copy-start.27 = (bf16[128,2048]{1,0:T(8,128)(2,1)S(1)}, bf16[128,2048]{1,0:T(8,128)(2,1)}, u32[]{:S(2)}) copy-start(bf16[128,2048]{1,0:T(8,128)(2,1)} %get-tuple-element.75.refs_1_) | copy-start | bytes 1572868
  328.1 47.0 %collective-permute-start.10 = (bf16[128,2048]{1,0:T(8,128)(2,1)}, bf16[128,2048]{1,0:T(8,128)(2,1)}, u32[]{:S(2)}, u32[]{:S(2)}) collective-permute-start(bf16[128,2048]{1,0:T(8,128)(2,1)} %get-tuple-element.74.refs_2_), channel_id=1, source_target_pairs={{0,12},{4,0},{8,4},{12,8},{1,13},{5,1},{9,5},{13,9},{2,14},{6,2},{... | collective-permute-start | bytes 1572872 | tf_op jit(solution)/shard_map/ppermute | solution.py:185
  331.8 61.5 %collective-permute-start.9 = (bf16[128,2048]{1,0:T(8,128)(2,1)S(1)}, bf16[128,2048]{1,0:T(8,128)(2,1)}, u32[]{:S(2)}, u32[]{:S(2)}) collective-permute-start(bf16[128,2048]{1,0:T(8,128)(2,1)S(1)} %copy-done.27), channel_id=1, source_target_pairs={{0,8},{4,12},{8,0},{12,4},{1,9},{5,13},{9,1},{13,5},{2,10},{6,14},... | collective-permute-start | bytes 1572872 | tf_op jit(solution)/shard_map/ppermute | solution.py:185
  352.9 40.4 %collective-permute-start.13 = (bf16[128,2048]{1,0:T(8,128)(2,1)}, bf16[128,2048]{1,0:T(8,128)(2,1)}, u32[]{:S(2)}, u32[]{:S(2)}) collective-permute-start(bf16[128,2048]{1,0:T(8,128)(2,1)} %add_convert_fusion.2), channel_id=1, source_target_pairs={{0,4},{4,8},{8,12},{12,0},{1,5},{5,9},{9,13},{13,1},{2,6},{6,10},{... | collective-permute-start | bytes 1572872 | tf_op jit(solution)/shard_map/ppermute | solution.py:185
  355.6 46.7 %collective-permute-start.14 = (bf16[16,64,768]{2,1,0:T(8,128)(2,1)}, bf16[16,64,768]{2,1,0:T(8,128)(2,1)S(1)}, u32[]{:S(2)}, u32[]{:S(2)}) collective-permute-start(bf16[16,64,768]{2,1,0:T(8,128)(2,1)} %all-to-all-done.2.refs_1_.own_ref), channel_id=1, source_target_pairs={{0,16},{16,0},{1,17},{17,1},{2,18},{18,2},{3,19},{19,3},{4,20},{20... | collective-permute-start | bytes 4718600 | tf_op jit(solution)/shard_map/ppermute | solution.py:185
  357.0 42.4 %all-to-all-start.3 = ((bf16[16,64,384]{2,1,0:T(8,128)(2,1)}), bf16[16,64,384]{2,1,0:T(8,128)(2,1)S(1)}, u32[]{:S(2)}, u32[]{:S(2)}) async-start(bf16[16,64,384]{2,1,0:T(8,128)(2,1)} %after.7), calls=%async_computation.4 | async-start | bytes 1572864 | tf_op jit(solution)/shard_map/all_to_all | solution.py:745
  393.2 3.7 copy-start.25
  393.2 3.7 copy-start.26
  399.4 19.7 %collective-permute-start.16 = (bf16[16,64,384]{2,1,0:T(8,128)(2,1)S(1)}, bf16[16,64,384]{2,1,0:T(8,128)(2,1)S(1)}, u32[]{:S(2)}, u32[]{:S(2)}) collective-permute-start(bf16[16,64,384]{2,1,0:T(8,128)(2,1)S(1)} %all-to-all-done.3.own_ref), channel_id=1, source_target_pairs={{0,16},{16,0},{1,17},{17,1},{2,18},{18,2},{3,19},{19,3},{4,20},{20... | collective-permute-start | bytes 2359304 | tf_op jit(solution)/shard_map/ppermute | solution.py:185
  (9 other events, 10.0 us)
Sparse Core Ops, SparseCore 0:
  10.9 121.2 all-gather.5
  134.3 73.7 all-gather.3
  262.4 50.4 reduce-scatter.1

commit v6 on v5

--- a/solution.py
+++ b/solution.py
@@ -176,7 +176,7 @@
         ],
         out_specs=[row(width), pl.BlockSpec((1, width), lambda i: (0, 0))],
         out_shape=[jax.ShapeDtypeStruct((tokens, width), bf16), jax.ShapeDtypeStruct((1, width), f32)],
-        compiler_params=pltpu.CompilerParams(vmem_limit_bytes=32 << 20),
+        compiler_params=pltpu.CompilerParams(vmem_limit_bytes=60 << 20),
         cost_estimate=pl.CostEstimate(flops=tokens * length * PAIR * 16, bytes_accessed=tokens * 6000, transcendentals=0),
     )(fused, probs, dcontext, own, after, before, *others)
 

time: 431 us -> 431 us (level)
  local copies, waits for them, and re-layouts: 41 us -> 34.7 us
    unnamed x65, local copies, waits for them, and re-layouts: 21.9 us -> 15.5 us
  transfers between devices with their start and end apart: 25 -> 25, of which waited for: 12 -> 13; matrix products, arithmetic and copies ran while one was open for 12% -> 12% of each run, Pallas kernels for 30% -> 30%
where the time goes in v6:
time: 431 us; the launch traced here: 429 us
  waiting for transfers between devices  155 us (36%)
  Pallas kernels  133 us (31%)
  starting transfers between devices  55.5 us (13%)
  other arithmetic  36.9 us (9%)
  local copies, waits for them, and re-layouts  34.7 us (8%)
  between operations  14.3 us (3%)
    all_to_all x2, waiting for transfers between devices, to_columns(): own = lax.all_to_all(own, TP, 0, 0, tiled=True)  74.1 us
    ppermute x18, waiting for transfers between devices, shifted(): return lax.ppermute(x, axis, [(i, (i + step) % size) for i in range(size)])  60.5 us
    pallas_call x2, Pallas kernels, dnormed_share(): pl.pallas_call(ignoring(dnormed_kernel, 11 + len(far), len(others)), name...  26.6 us
    ppermute x18, starting transfers between devices, shifted(): return lax.ppermute(x, axis, [(i, (i + step) % size) for i in range(size)])  22.6 us
    pallas_call x1, Pallas kernels, gate_forward(): pl.pallas_call(gate_kernel, name='gate_fwd', grid=(count // 2,), in_specs...  20.9 us
    pallas_call x2, Pallas kernels, split_grads(): pl.pallas_call(ignoring(grads_kernel, 3, len(others)), name='grads', grid...  19.9 us
    all_to_all x2, starting transfers between devices, to_columns(): own = lax.all_to_all(own, TP, 0, 0, tiled=True)  17.7 us
    unnamed x65, local copies, waits for them, and re-layouts  15.5 us
  transfers between devices with their start and end apart: 25, of which 13 were waited for; matrix products, arithmetic and copies ran while one was open for 12% of the time, Pallas kernels for 30%

profile of v6, /device:TPU:0, one launch (start us, length us, event | category | flops | bytes accessed | tf_op | source)
XLA Modules:
  0.0 428.9 jit_solution(12449772415983114022)
XLA Ops:
  8.6 1.9 pad_maximum_fusion
  11.3 1.8 copy-done.10
  13.1 2.0 pack.2
  15.1 7.6 %all-to-all-start = ((bf16[16,64,768]{2,1,0:T(8,128)(2,1)}), bf16[16,64,768]{2,1,0:T(8,128)(2,1)}, u32[]{:S(2)}, u32[]{:S(2)}) async-start(bf16[16,64,768]{2,1,0:T(8,128)(2,1)} %pack.2), calls=%async_computation | async-start | bytes 3145728 | tf_op jit(solution)/shard_map/all_to_all | solution.py:654
  24.2 47.9 %all-to-all-done = bf16[16,64,768]{2,1,0:T(8,128)(2,1)} async-done(((bf16[16,64,768]{2,1,0:T(8,128)(2,1)}), bf16[16,64,768]{2,1,0:T(8,128)(2,1)}, u32[]{:S(2)}, u32[]{:S(2)}) %all-to-all-start) | async-done | bytes 1572896 | tf_op jit(solution)/shard_map/all_to_all | solution.py:654
  72.1 10.2 %all-to-all-start.1 = ((bf16[16,64,384]{2,1,0:T(8,128)(2,1)}), bf16[16,64,384]{2,1,0:T(8,128)(2,1)}, u32[]{:S(2)}, u32[]{:S(2)}) async-start(bf16[16,64,384]{2,1,0:T(8,128)(2,1)} %pack.3), calls=%async_computation.1 | async-start | bytes 1572864 | tf_op jit(solution)/shard_map/all_to_all | solution.py:654
  82.3 1.8 collective-permute-start
  87.6 26.3 %all-to-all-done.1 = bf16[16,64,384]{2,1,0:T(8,128)(2,1)} async-done(((bf16[16,64,384]{2,1,0:T(8,128)(2,1)}), bf16[16,64,384]{2,1,0:T(8,128)(2,1)}, u32[]{:S(2)}, u32[]{:S(2)}) %all-to-all-start.1) | async-done | bytes 786464 | tf_op jit(solution)/shard_map/all_to_all | solution.py:654
  116.9 2.1 bitcast_dynamic-update-slice_fusion.3
  122.7 9.5 %all-gather.6.cloned.1.call-done = bf16[2176,2048]{1,0:T(8,128)(2,1)} async-done(((bf16[136,2048]{1,0:T(8,128)(2,1)}), bf16[2176,2048]{1,0:T(8,128)(2,1)}) %all-gather.6.cloned.1.call-update) | async-done | bytes 8912912 | tf_op jit(solution)/shard_map/all_gather | solution.py:634
  136.9 5.9 %fusion = (f32[2048,128]{1,0:T(8,128)}, f32[2048,128]{1,0:T(8,128)}, f32[2048,128]{1,0:T(8,128)}) fusion(f32[128]{0:T(128)S(1)} %copy-done.29, f32[2048]{0:T(1024)S(1)} %convert_bitcast_fusion, pred[128]{0:T(512)(128)(4,1)S(1)} %copy-done.30, pred[128]{0:T(512)(128)(4,1)S(1)} %copy-done.31, pred[128]{0:T(512)(128)(4,1)S(1)} %copy-done.28), kind=kLoop, calls=%fused_computation.12 | loop fusion | flops 1310720 | bytes 3154816 | tf_op jit(solution)/shard_map/jit(_where)/select_n | solution.py:52
  142.9 2.2 bitcast_dynamic-update-slice_fusion.2
  145.1 20.9 %gate_fwd.1 = (f32[2048,128]{1,0:T(8,128)}, bf16[2048,2048]{1,0:T(8,128)(2,1)}, f32[2048,384]{1,0:T(8,128)}, f32[2048,384]{1,0:T(8,128)}, bf16[2048,384]{1,0:T(8,128)(2,1)}, /*index=5*/f32[2048,384]{1,0:T(8,128)}) custom-call(bf16[16,136,2048]{2,1,0:T(8,128)(2,1)} %bitcast.77, bf16[16,136,2048]{2,1,0:T(8,128)(2,1)} %bitcast.78, f32[1,2048]{1,0:T(1,128)} %bitcast.90, ...), custom_call_target="tpu_custom_call" | custom-call | flops 1 | bytes 1 | tf_op jit(solution)/shard_map/gate_fwd/pallas_call | solution.py:312
  170.7 1.9 copy-done.9
  172.6 3.3 attend.1
  176.0 5.5 %branch_far.1 = bf16[1024,2048]{1,0:T(8,128)(2,1)} custom-call(s32[8]{0:T(128)S(1)} %stack.134.order_ref, bf16[2048,128]{1,0:T(8,128)(2,1)S(1)} %get-tuple-element.43.ac_ref.bc_ref.refs_0_, bf16[2048,128]{1,0:T(8,128)(2,1)S(1)} %get-tuple-element.43.ac_ref.bc_ref.refs_0_, bf16[2048,384]{1,0:T(8,128)(2,1)S(1)} %copy-done, bf16[2048,384]{1,0:T(8,128)(2,1)S(1)} %copy-done, ...), custom_call_target="tpu_custom_call" | custom-call | flops 1 | bytes 1 | tf_op jit(solution)/shard_map/branch_far/pallas_call | solution.py:372
  181.9 7.1 %collective-permute-done.2.refs_0_ = bf16[1024,2048]{1,0:T(8,128)(2,1)} collective-permute-done((bf16[1024,2048]{1,0:T(8,128)(2,1)}, bf16[1024,2048]{1,0:T(8,128)(2,1)}, u32[]{:S(2)}, u32[]{:S(2)}) %collective-permute-start.2) | collective-permute-done | bytes 4194336 | tf_op jit(solution)/shard_map/ppermute | solution.py:185
  189.0 8.9 %branch_near.1 = (bf16[512,2048]{1,0:T(8,128)(2,1)}, f32[512,2048]{1,0:T(8,128)}) custom-call(s32[8]{0:T(128)S(1)} %stack.125.order_ref, bf16[2048,128]{1,0:T(8,128)(2,1)S(1)} %get-tuple-element.43.ac_ref.bc_ref.refs_0_, bf16[2048,128]{1,0:T(8,128)(2,1)S(1)} %get-tuple-element.43.ac_ref.bc_ref.refs_0_, bf16[2048,384]{1,0:T(8,128)(2,1)S(1)} %copy-done, ...), custom_call_target="tpu_custom_call" | custom-call | flops 1 | bytes 1 | tf_op jit(solution)/shard_map/branch_near/pallas_call | solution.py:372
  199.3 8.8 %all-gather.4.cloned.1.call-done.refs_0_.refs_2_ = bf16[2048,2048]{1,0:T(8,128)(2,1)} async-done(((bf16[128,2048]{1,0:T(8,128)(2,1)}), bf16[2048,2048]{1,0:T(8,128)(2,1)}) %all-gather.4.cloned.1.call-update) | async-done | bytes 8388624 | tf_op jit(solution)/shard_map/all_gather | solution.py:636
  209.8 11.4 %gate_back.1 = (bf16[2048,768]{1,0:T(8,128)(2,1)}, bf16[2048,128]{1,0:T(8,128)(2,1)S(1)}) custom-call(bf16[2048,2048]{1,0:T(8,128)(2,1)} %all-gather.4.cloned.1.call-done.refs_0_.refs_2_, f32[2048,384]{1,0:T(8,128)} %get-tuple-element.40.refs_1_, f32[2048,384]{1,0:T(8,128)} %get-tuple-element.41.refs_2_, bf16[512,2048]{1,0:T(8,128)(2,1)S(1)} %copy-done.2, ...), custom_call_target="tpu_custom_call" | custom-call | flops 1 | bytes 1 | tf_op jit(solution)/shard_map/gate_back/pallas_call | solution.py:409
  222.0 11.2 %grads.2 = (f32[16,64,768]{2,1,0:T(8,128)}, bf16[16,64,768]{2,1,0:T(8,128)(2,1)}) custom-call(s32[1]{0:T(128)} %bitcast.12.part_ref.refs_0_, bf16[2048,2048]{1,0:T(8,128)(2,1)} %get-tuple-element.50.refs_1_, bf16[2048,768]{1,0:T(8,128)(2,1)} %get-tuple-element.46.refs_2_.refs_5_.refs_6_), custom_call_target="tpu_custom_call" | custom-call | flops 1 | bytes 1 | tf_op jit(solution)/shard_map/grads/pallas_call | solution.py:438
  235.3 8.2 %attend_back.1 = (bf16[2048,384]{1,0:T(8,128)(2,1)}, f32[1,384]{1,0:T(1,128)}) custom-call(bf16[2048,384]{1,0:T(8,128)(2,1)} %copy-done.13, f32[16,256,128]{2,1,0:T(8,128)} %copy-done.11, bf16[2048,128]{1,0:T(8,128)(2,1)} %copy-done.14, f32[2048,128]{1,0:T(8,128)} %get-tuple-element.88.refs_1_.own_ref.refs_3_, ...), custom_call_target="tpu_custom_call" | custom-call | flops 536870912 | bytes 12288000 | tf_op jit(solution)/shard_map/attend_back/pallas_call | solution.py:164
  243.5 2.4 collective-permute-done.3.refs_12_
  247.2 14.2 %dn_far.1 = (bf16[256,2048]{1,0:T(8,128)(2,1)}, bf16[256,2048]{1,0:T(8,128)(2,1)}, bf16[256,2048]{1,0:T(8,128)(2,1)}, bf16[256,2048]{1,0:T(8,128)(2,1)}, bf16[512,2048]{1,0:T(8,128)(2,1)}, /*index=5*/f32[8,2048]{1,0:T(8,128)}) custom-call(s32[8]{0:T(128)} %stack.116.refs_0_, bf16[16,136,2048]{2,1,0:T(8,128)(2,1)} %bitcast.79, ...), custom_call_target="tpu_custom_call" | custom-call | flops 1 | bytes 1 | tf_op jit(solution)/shard_map/dn_far/pallas_call | solution.py:532
  263.5 12.4 %dn_near.1 = (f32[1024,2048]{1,0:T(8,128)}, f32[8,2048]{1,0:T(8,128)}) custom-call(s32[8]{0:T(128)} %stack.143.refs_0_, bf16[16,136,2048]{2,1,0:T(8,128)(2,1)} %bitcast.81, bf16[16,136,2048]{2,1,0:T(8,128)(2,1)} %bitcast.82, f32[2048,128]{1,0:T(8,128)} %get-tuple-element.39.refs_3_.refs_4_, f32[2048,128]{1,0:T(8,128)} %get-tuple-element.39.refs_3_.refs_4_, ...), custom_call_target="tpu_custom_call" | custom-call | flops 1 | bytes 1 | tf_op jit(solution)/shard_map/dn_near/pallas_call | solution.py:532
  278.7 6.4 %combine.1 = (bf16[256,2048]{1,0:T(8,128)(2,1)}, bf16[256,2048]{1,0:T(8,128)(2,1)S(1)}, f32[512,2048]{1,0:T(8,128)}) custom-call(f32[1024,2048]{1,0:T(8,128)} %get-tuple-element.59.refs_0_, bf16[256,2048]{1,0:T(8,128)(2,1)S(1)} %collective-permute-done.4.refs_1_, bf16[256,2048]{1,0:T(8,128)(2,1)S(1)} %collective-permute-done.5.refs_2_, ...), custom_call_target="tpu_custom_call" | custom-call | flops 1 | bytes 1 | tf_op jit(solution)/shard_map/combine/pallas_call | solution.py:581
  287.5 1.9 copy-done.18
  289.4 3.4 add_convert_fusion.refs_3_
  292.8 4.7 %all-to-all-start.2 = ((bf16[16,64,768]{2,1,0:T(8,128)(2,1)}), bf16[16,64,768]{2,1,0:T(8,128)(2,1)}, u32[]{:S(2)}, u32[]{:S(2)}) async-start(bf16[16,64,768]{2,1,0:T(8,128)(2,1)} %add_convert_fusion.refs_3_), calls=%async_computation.3 | async-start | bytes 3145728 | tf_op jit(solution)/shard_map/all_to_all | solution.py:716
  297.5 8.8 %grads.3 = (f32[16,64,384]{2,1,0:T(8,128)}, bf16[16,64,384]{2,1,0:T(8,128)(2,1)}) custom-call(s32[1]{0:T(128)} %bitcast.12.part_ref.refs_0_, bf16[2048,2048]{1,0:T(8,128)(2,1)} %get-tuple-element.50.refs_1_, bf16[2048,384]{1,0:T(8,128)(2,1)} %get-tuple-element.52.refs_7_.refs_8_.refs_2_, bf16[16,64,768]{2,1,0:T(8,128)(2,1)} %add_convert_fusion.refs_3_), custom_call_target="tpu_custom_call" | custom-call | flops 1 | bytes 1 | tf_op jit(solution)/shard_map/grads/pallas_call | solution.py:438
  307.5 8.8 %rows.1.refs_3_ = bf16[480,2048]{1,0:T(8,128)(2,1)} custom-call(bf16[2048,128]{1,0:T(8,128)(2,1)} %copy-done.6, bf16[2048,384]{1,0:T(8,128)(2,1)} %get-tuple-element.44.ah_ref.bh_ref.refs_1_, bf16[2048,2048]{1,0:T(8,128)(2,1)} %all-gather.4.cloned.1.call-done.refs_0_.refs_2_, bf16[16,64,384]{2,1,0:T(8,128)(2,1)} %get-tuple-element.67.refs_3_), custom_call_target="tpu_custom_call" | custom-call | flops 1 | bytes 1 | tf_op jit(solution)/shard_map/rows/pallas_call | solution.py:467
  317.5 2.5 add_convert_fusion.3
  320.0 1.8 collective-permute-start.12
  322.3 4.6 %collective-permute-done.15 = bf16[16,64,384]{2,1,0:T(8,128)(2,1)S(1)} collective-permute-done((bf16[16,64,384]{2,1,0:T(8,128)(2,1)}, bf16[16,64,384]{2,1,0:T(8,128)(2,1)S(1)}, u32[]{:S(2)}, u32[]{:S(2)}) %collective-permute-start.15) | collective-permute-done | bytes 786464 | tf_op jit(solution)/shard_map/ppermute | solution.py:185
  327.9 3.7 collective-permute-start.10
  331.8 19.1 %collective-permute-done.12 = bf16[256,2048]{1,0:T(8,128)(2,1)} collective-permute-done((bf16[256,2048]{1,0:T(8,128)(2,1)}, bf16[256,2048]{1,0:T(8,128)(2,1)}, u32[]{:S(2)}, u32[]{:S(2)}) %collective-permute-start.12) | collective-permute-done | bytes 1048608 | tf_op jit(solution)/shard_map/ppermute | solution.py:185
  350.8 2.3 add_convert_fusion.2
  353.1 2.4 collective-permute-start.13
  357.0 10.3 %all-to-all-start.3 = ((bf16[16,64,384]{2,1,0:T(8,128)(2,1)}), bf16[16,64,384]{2,1,0:T(8,128)(2,1)S(1)}, u32[]{:S(2)}, u32[]{:S(2)}) async-start(bf16[16,64,384]{2,1,0:T(8,128)(2,1)} %after.7), calls=%async_computation.4 | async-start | bytes 1572864 | tf_op jit(solution)/shard_map/all_to_all | solution.py:745
  367.4 1.8 collective-permute-done.17
  369.1 2.9 convert_add_fusion
  372.0 1.9 slice.164
  374.9 18.4 %collective-permute-done.9 = bf16[128,2048]{1,0:T(8,128)(2,1)} collective-permute-done((bf16[128,2048]{1,0:T(8,128)(2,1)S(1)}, bf16[128,2048]{1,0:T(8,128)(2,1)}, u32[]{:S(2)}, u32[]{:S(2)}) %collective-permute-start.9) | collective-permute-done | bytes 524320 | tf_op jit(solution)/shard_map/ppermute | solution.py:185
  393.3 2.5 fusion.31
  402.1 1.9 convert_add_fusion.2
  404.1 6.1 %unpack.3 = f32[128,11264]{1,0:T(8,128)} custom-call(s32[1]{0:T(128)} %bitcast.12.part_ref.refs_0_, bf16[16,64,768]{2,1,0:T(8,128)(2,1)} %all-to-all-done.2.refs_1_.own_ref, bf16[16,64,768]{2,1,0:T(8,128)(2,1)S(1)} %collective-permute-done.14.other_ref), custom_call_target="tpu_custom_call" | custom-call | flops 1 | bytes 1 | tf_op jit(solution)/shard_map/unpack/pallas_call | solution.py:266
  413.2 5.8 %collective-permute-done.16.other_ref = bf16[16,64,384]{2,1,0:T(8,128)(2,1)S(1)} collective-permute-done((bf16[16,64,384]{2,1,0:T(8,128)(2,1)S(1)}, bf16[16,64,384]{2,1,0:T(8,128)(2,1)S(1)}, u32[]{:S(2)}, u32[]{:S(2)}) %collective-permute-start.16) | collective-permute-done | bytes 786464 | tf_op jit(solution)/shard_map/ppermute | solution.py:185
  419.0 3.4 unpack.2
  (164 shorter events, 54.0 us)
Async XLA Ops:
  7.2 125.0 %all-gather.6.cloned.1.call-start = ((), (), s32[]{:S(2)}) async-start(), calls=%async_computation.7 | async-start | bytes 9469952 | tf_op jit(solution)/shard_map/all_gather | solution.py:634
  10.5 197.6 %all-gather.4.cloned.1.call-start = ((), (), s32[]{:S(2)}) async-start(), calls=%async_computation.5 | async-start | bytes 8912896 | tf_op jit(solution)/shard_map/all_gather | solution.py:636
  11.3 1.8 copy-start.10
  15.1 7.6 %copy-start.12 = (bf16[128,6144]{1,0:T(8,128)(2,1)S(1)}, bf16[128,6144]{1,0:T(8,128)(2,1)}, u32[]{:S(2)}) copy-start(bf16[128,6144]{1,0:T(8,128)(2,1)} %own_ref.3) | copy-start | bytes 4718596
  15.1 57.0 %all-to-all-start = ((bf16[16,64,768]{2,1,0:T(8,128)(2,1)}), bf16[16,64,768]{2,1,0:T(8,128)(2,1)}, u32[]{:S(2)}, u32[]{:S(2)}) async-start(bf16[16,64,768]{2,1,0:T(8,128)(2,1)} %pack.2), calls=%async_computation | async-start | bytes 3145728 | tf_op jit(solution)/shard_map/all_to_all | solution.py:654
  22.7 63.2 %copy-start.24 = (bf16[352,2048]{1,0:T(8,128)(2,1)S(1)}, bf16[352,2048]{1,0:T(8,128)(2,1)}, u32[]{:S(2)}) copy-start(bf16[352,2048]{1,0:T(8,128)(2,1)} %param.18) | copy-start | bytes 4325380
  22.7 63.2 %copy-start.26 = (bf16[128,2048]{1,0:T(8,128)(2,1)S(1)}, bf16[128,2048]{1,0:T(8,128)(2,1)}, u32[]{:S(2)}) copy-start(bf16[128,2048]{1,0:T(8,128)(2,1)} %param.16) | copy-start | bytes 1572868
  72.1 41.8 %all-to-all-start.1 = ((bf16[16,64,384]{2,1,0:T(8,128)(2,1)}), bf16[16,64,384]{2,1,0:T(8,128)(2,1)}, u32[]{:S(2)}, u32[]{:S(2)}) async-start(bf16[16,64,384]{2,1,0:T(8,128)(2,1)} %pack.3), calls=%async_computation.1 | async-start | bytes 1572864 | tf_op jit(solution)/shard_map/all_to_all | solution.py:654
  82.2 274.8 %reduce-scatter.2.cloned.1.call-start = ((), (), s32[]{:S(2)}) async-start(), calls=%async_computation.6 | async-start | bytes 2621440 | tf_op jit(solution)/shard_map/reduce_scatter | solution.py:699
  82.3 38.7 %collective-permute-start = (bf16[16,64,768]{2,1,0:T(8,128)(2,1)}, bf16[16,64,768]{2,1,0:T(8,128)(2,1)}, u32[]{:S(2)}, u32[]{:S(2)}) collective-permute-start(bf16[16,64,768]{2,1,0:T(8,128)(2,1)} %all-to-all-done), channel_id=1, source_target_pairs={{0,16},{16,0},{1,17},{17,1},{2,18},{18,2},{3,19},{19,3},{4,20},{20... | collective-permute-start | bytes 4718600 | tf_op jit(solution)/shard_map/ppermute | solution.py:185
  113.9 29.0 %collective-permute-start.1 = (bf16[16,64,384]{2,1,0:T(8,128)(2,1)}, bf16[16,64,384]{2,1,0:T(8,128)(2,1)}, u32[]{:S(2)}, u32[]{:S(2)}) collective-permute-start(bf16[16,64,384]{2,1,0:T(8,128)(2,1)} %all-to-all-done.1), channel_id=1, source_target_pairs={{0,16},{16,0},{1,17},{17,1},{2,18},{18,2},{3,19},{19,3},{4,20},{20... | collective-permute-start | bytes 2359304 | tf_op jit(solution)/shard_map/ppermute | solution.py:185
  122.6 20.3 %copy-start.15 = (bf16[16,2,64,768]{3,2,1,0:T(8,128)(2,1)}, bf16[16,2,64,768]{3,2,1,0:T(8,128)(2,1)S(1)}, u32[]{:S(2)}) copy-start(bf16[16,2,64,768]{3,2,1,0:T(8,128)(2,1)S(1)} %bitcast_dynamic-update-slice_fusion) | copy-start | bytes 9437188
  122.6 14.3 %copy-start.28 = (pred[128]{0:T(512)(128)(4,1)S(1)}, pred[128]{0:T(512)(128)(4,1)}, u32[]{:S(2)}) copy-start(pred[128]{0:T(512)(128)(4,1)} %broadcast_compare_fusion.1) | copy-start | bytes 388
  122.6 14.3 %copy-start.29 = (f32[128]{0:T(128)S(1)}, f32[128]{0:T(128)}, u32[]{:S(2)}) copy-start(f32[128]{0:T(128)} %fusion.29) | copy-start | bytes 1540
  122.6 14.3 %copy-start.30 = (pred[128]{0:T(512)(128)(4,1)S(1)}, pred[128]{0:T(512)(128)(4,1)}, u32[]{:S(2)}) copy-start(pred[128]{0:T(512)(128)(4,1)} %get-tuple-element.91) | copy-start | bytes 388
  122.7 14.3 %copy-start.31 = (pred[128]{0:T(512)(128)(4,1)S(1)}, pred[128]{0:T(512)(128)(4,1)}, u32[]{:S(2)}) copy-start(pred[128]{0:T(512)(128)(4,1)} %get-tuple-element.92) | copy-start | bytes 388
  145.1 21.7 %copy-start.3 = (f32[2048,128]{1,0:T(8,128)S(1)}, f32[2048,128]{1,0:T(8,128)}, u32[]{:S(2)}) copy-start(f32[2048,128]{1,0:T(8,128)} %get-tuple-element.86.refs_3_.before_ref.refs_5_) | copy-start | bytes 3145732
  170.7 1.9 copy-start.9
  172.6 3.4 copy-start
  172.6 3.4 copy-start.1
  175.9 5.5 %copy-start.11 = (f32[16,256,128]{2,1,0:T(8,128)}, f32[16,256,128]{2,1,0:T(8,128)S(1)}, u32[]{:S(2)}) copy-start(f32[16,256,128]{2,1,0:T(8,128)S(1)} %get-tuple-element.48.refs_1_) | copy-start | bytes 6291460
  176.0 5.5 %copy-start.13 = (bf16[2048,384]{1,0:T(8,128)(2,1)}, bf16[2048,384]{1,0:T(8,128)(2,1)S(1)}, u32[]{:S(2)}) copy-start(bf16[2048,384]{1,0:T(8,128)(2,1)S(1)} %get-tuple-element.47.refs_0_) | copy-start | bytes 4718596
  176.0 13.0 %copy-start.6 = (bf16[2048,128]{1,0:T(8,128)(2,1)}, bf16[2048,128]{1,0:T(8,128)(2,1)S(1)}, u32[]{:S(2)}) copy-start(bf16[2048,128]{1,0:T(8,128)(2,1)S(1)} %get-tuple-element.43.ac_ref.bc_ref.refs_0_) | copy-start | bytes 1572868
  181.5 7.5 %collective-permute-start.2 = (bf16[1024,2048]{1,0:T(8,128)(2,1)}, bf16[1024,2048]{1,0:T(8,128)(2,1)}, u32[]{:S(2)}, u32[]{:S(2)}) collective-permute-start(bf16[1024,2048]{1,0:T(8,128)(2,1)} %branch_far.1), channel_id=1, source_target_pairs={{0,1},{1,0},{2,3},{3,2},{4,5},{5,4},{6,7},{7,6},{8,9},{9,8},{10,11... | collective-permute-start | bytes 12582920 | tf_op jit(solution)/shard_map/ppermute | solution.py:185
  197.9 48.0 %collective-permute-start.3 = (bf16[512,2048]{1,0:T(8,128)(2,1)}, bf16[512,2048]{1,0:T(8,128)(2,1)S(1)}, u32[]{:S(2)}, u32[]{:S(2)}) collective-permute-start(bf16[512,2048]{1,0:T(8,128)(2,1)} %get-tuple-element.45.refs_4_), channel_id=1, source_target_pairs={{0,2},{2,0},{1,3},{3,1},{4,6},{6,4},{5,7},{7,5},{8,10},{10,8},{9,1... | collective-permute-start | bytes 6291464 | tf_op jit(solution)/shard_map/ppermute | solution.py:185
  233.1 54.4 %collective-permute-start.11 = (bf16[16,64,768]{2,1,0:T(8,128)(2,1)}, bf16[16,64,768]{2,1,0:T(8,128)(2,1)}, u32[]{:S(2)}, u32[]{:S(2)}) collective-permute-start(bf16[16,64,768]{2,1,0:T(8,128)(2,1)} %get-tuple-element.51.refs_6_), channel_id=1, source_target_pairs={{0,16},{16,0},{1,17},{17,1},{2,18},{18,2},{3,19},{19,3},{4,20},{20... | collective-permute-start | bytes 4718600 | tf_op jit(solution)/shard_map/ppermute | solution.py:185
  261.4 1.9 copy-start.27
  261.4 17.2 %collective-permute-start.4 = (bf16[256,2048]{1,0:T(8,128)(2,1)}, bf16[256,2048]{1,0:T(8,128)(2,1)S(1)}, u32[]{:S(2)}, u32[]{:S(2)}) collective-permute-start(bf16[256,2048]{1,0:T(8,128)(2,1)} %get-tuple-element.55.refs_11_), channel_id=1, source_target_pairs={{0,1},{1,0},{2,3},{3,2},{4,5},{5,4},{6,7},{7,6},{8,9},{9,8},{10,11... | collective-permute-start | bytes 3145736 | tf_op jit(solution)/shard_map/ppermute | solution.py:185
  261.5 17.1 %collective-permute-start.5 = (bf16[256,2048]{1,0:T(8,128)(2,1)}, bf16[256,2048]{1,0:T(8,128)(2,1)S(1)}, u32[]{:S(2)}, u32[]{:S(2)}) collective-permute-start(bf16[256,2048]{1,0:T(8,128)(2,1)} %get-tuple-element.56.refs_12_), channel_id=1, source_target_pairs={{0,1},{1,0},{2,3},{3,2},{4,5},{5,4},{6,7},{7,6},{8,9},{9,8},{10,11... | collective-permute-start | bytes 3145736 | tf_op jit(solution)/shard_map/ppermute | solution.py:185
  262.0 16.6 %collective-permute-start.6 = (bf16[256,2048]{1,0:T(8,128)(2,1)}, bf16[256,2048]{1,0:T(8,128)(2,1)S(1)}, u32[]{:S(2)}, u32[]{:S(2)}) collective-permute-start(bf16[256,2048]{1,0:T(8,128)(2,1)} %get-tuple-element.57.refs_13_), channel_id=1, source_target_pairs={{0,1},{1,0},{2,3},{3,2},{4,5},{5,4},{6,7},{7,6},{8,9},{9,8},{10,11... | collective-permute-start | bytes 3145736 | tf_op jit(solution)/shard_map/ppermute | solution.py:185
  262.1 16.6 %collective-permute-start.7 = (bf16[256,2048]{1,0:T(8,128)(2,1)}, bf16[256,2048]{1,0:T(8,128)(2,1)}, u32[]{:S(2)}, u32[]{:S(2)}) collective-permute-start(bf16[256,2048]{1,0:T(8,128)(2,1)} %get-tuple-element.58.refs_14_), channel_id=1, source_target_pairs={{0,1},{1,0},{2,3},{3,2},{4,5},{5,4},{6,7},{7,6},{8,9},{9,8},{10,11... | collective-permute-start | bytes 3145736 | tf_op jit(solution)/shard_map/ppermute | solution.py:185
  286.1 31.5 %collective-permute-start.8 = (bf16[256,2048]{1,0:T(8,128)(2,1)}, bf16[256,2048]{1,0:T(8,128)(2,1)}, u32[]{:S(2)}, u32[]{:S(2)}) collective-permute-start(bf16[256,2048]{1,0:T(8,128)(2,1)} %get-tuple-element.61.refs_1_), channel_id=1, source_target_pairs={{0,2},{2,0},{1,3},{3,1},{4,6},{6,4},{5,7},{7,5},{8,10},{10,8},{9,1... | collective-permute-start | bytes 3145736 | tf_op jit(solution)/shard_map/ppermute | solution.py:185
  287.5 1.9 copy-start.18
  292.8 62.7 %all-to-all-start.2 = ((bf16[16,64,768]{2,1,0:T(8,128)(2,1)}), bf16[16,64,768]{2,1,0:T(8,128)(2,1)}, u32[]{:S(2)}, u32[]{:S(2)}) async-start(bf16[16,64,768]{2,1,0:T(8,128)(2,1)} %add_convert_fusion.refs_3_), calls=%async_computation.3 | async-start | bytes 3145728 | tf_op jit(solution)/shard_map/all_to_all | solution.py:716
  306.3 11.2 %copy-start.17 = (f32[512,2048]{1,0:T(8,128)S(1)}, f32[512,2048]{1,0:T(8,128)}, u32[]{:S(2)}) copy-start(f32[512,2048]{1,0:T(8,128)} %get-tuple-element.60) | copy-start | bytes 12582916
  306.3 20.6 %collective-permute-start.15 = (bf16[16,64,384]{2,1,0:T(8,128)(2,1)}, bf16[16,64,384]{2,1,0:T(8,128)(2,1)S(1)}, u32[]{:S(2)}, u32[]{:S(2)}) collective-permute-start(bf16[16,64,384]{2,1,0:T(8,128)(2,1)} %get-tuple-element.67.refs_3_), channel_id=1, source_target_pairs={{0,16},{16,0},{1,17},{17,1},{2,18},{18,2},{3,19},{19,3},{4,20},{20... | collective-permute-start | bytes 2359304 | tf_op jit(solution)/shard_map/ppermute | solution.py:185
  316.3 52.8 %collective-permute-start.17 = (bf16[480,2048]{1,0:T(8,128)(2,1)}, bf16[480,2048]{1,0:T(8,128)(2,1)}, u32[]{:S(2)}, u32[]{:S(2)}) collective-permute-start(bf16[480,2048]{1,0:T(8,128)(2,1)} %rows.1.refs_3_), channel_id=1, source_target_pairs={{0,16},{16,0},{1,17},{17,1},{2,18},{18,2},{3,19},{19,3},{4,20},{20... | collective-permute-start | bytes 5898248 | tf_op jit(solution)/shard_map/ppermute | solution.py:185
  320.0 6.9 %copy-start.23 = (f32[16,64,384]{2,1,0:T(8,128)S(1)}, f32[16,64,384]{2,1,0:T(8,128)}, u32[]{:S(2)}) copy-start(f32[16,64,384]{2,1,0:T(8,128)} %get-tuple-element.68) | copy-start | bytes 4718596
  320.0 30.8 %collective-permute-start.12 = (bf16[256,2048]{1,0:T(8,128)(2,1)}, bf16[256,2048]{1,0:T(8,128)(2,1)}, u32[]{:S(2)}, u32[]{:S(2)}) collective-permute-start(bf16[256,2048]{1,0:T(8,128)(2,1)} %after.6), channel_id=1, source_target_pairs={{0,2},{2,0},{1,3},{3,1},{4,6},{6,4},{5,7},{7,5},{8,10},{10,8},{9,1... | collective-permute-start | bytes 3145736 | tf_op jit(solution)/shard_map/ppermute | solution.py:185
  321.8 9.8 %copy-start.21 = (bf16[128,2048]{1,0:T(8,128)(2,1)S(1)}, bf16[128,2048]{1,0:T(8,128)(2,1)}, u32[]{:S(2)}) copy-start(bf16[128,2048]{1,0:T(8,128)(2,1)} %get-tuple-element.75.refs_1_) | copy-start | bytes 1572868
  327.9 47.0 %collective-permute-start.10 = (bf16[128,2048]{1,0:T(8,128)(2,1)}, bf16[128,2048]{1,0:T(8,128)(2,1)}, u32[]{:S(2)}, u32[]{:S(2)}) collective-permute-start(bf16[128,2048]{1,0:T(8,128)(2,1)} %get-tuple-element.74.refs_2_), channel_id=1, source_target_pairs={{0,12},{4,0},{8,4},{12,8},{1,13},{5,1},{9,5},{13,9},{2,14},{6,2},{... | collective-permute-start | bytes 1572872 | tf_op jit(solution)/shard_map/ppermute | solution.py:185
  331.6 61.7 %collective-permute-start.9 = (bf16[128,2048]{1,0:T(8,128)(2,1)S(1)}, bf16[128,2048]{1,0:T(8,128)(2,1)}, u32[]{:S(2)}, u32[]{:S(2)}) collective-permute-start(bf16[128,2048]{1,0:T(8,128)(2,1)S(1)} %copy-done.21), channel_id=1, source_target_pairs={{0,8},{4,12},{8,0},{12,4},{1,9},{5,13},{9,1},{13,5},{2,10},{6,14},... | collective-permute-start | bytes 1572872 | tf_op jit(solution)/shard_map/ppermute | solution.py:185
  353.1 40.2 %collective-permute-start.13 = (bf16[128,2048]{1,0:T(8,128)(2,1)}, bf16[128,2048]{1,0:T(8,128)(2,1)}, u32[]{:S(2)}, u32[]{:S(2)}) collective-permute-start(bf16[128,2048]{1,0:T(8,128)(2,1)} %add_convert_fusion.2), channel_id=1, source_target_pairs={{0,4},{4,8},{8,12},{12,0},{1,5},{5,9},{9,13},{13,1},{2,6},{6,10},{... | collective-permute-start | bytes 1572872 | tf_op jit(solution)/shard_map/ppermute | solution.py:185
  355.5 46.6 %collective-permute-start.14 = (bf16[16,64,768]{2,1,0:T(8,128)(2,1)}, bf16[16,64,768]{2,1,0:T(8,128)(2,1)S(1)}, u32[]{:S(2)}, u32[]{:S(2)}) collective-permute-start(bf16[16,64,768]{2,1,0:T(8,128)(2,1)} %all-to-all-done.2.refs_1_.own_ref), channel_id=1, source_target_pairs={{0,16},{16,0},{1,17},{17,1},{2,18},{18,2},{3,19},{19,3},{4,20},{20... | collective-permute-start | bytes 4718600 | tf_op jit(solution)/shard_map/ppermute | solution.py:185
  357.0 42.3 %all-to-all-start.3 = ((bf16[16,64,384]{2,1,0:T(8,128)(2,1)}), bf16[16,64,384]{2,1,0:T(8,128)(2,1)S(1)}, u32[]{:S(2)}, u32[]{:S(2)}) async-start(bf16[16,64,384]{2,1,0:T(8,128)(2,1)} %after.7), calls=%async_computation.4 | async-start | bytes 1572864 | tf_op jit(solution)/shard_map/all_to_all | solution.py:745
  393.3 3.7 copy-start.19
  393.3 3.7 copy-start.20
  399.4 19.6 %collective-permute-start.16 = (bf16[16,64,384]{2,1,0:T(8,128)(2,1)S(1)}, bf16[16,64,384]{2,1,0:T(8,128)(2,1)S(1)}, u32[]{:S(2)}, u32[]{:S(2)}) collective-permute-start(bf16[16,64,384]{2,1,0:T(8,128)(2,1)S(1)} %all-to-all-done.3.own_ref), channel_id=1, source_target_pairs={{0,16},{16,0},{1,17},{17,1},{2,18},{18,2},{3,19},{19,3},{4,20},{20... | collective-permute-start | bytes 2359304 | tf_op jit(solution)/shard_map/ppermute | solution.py:185
  (9 other events, 11.3 us)
Sparse Core Ops, SparseCore 0:
  10.9 121.2 all-gather.5
  134.3 73.7 all-gather.3
  262.7 50.3 reduce-scatter.1

commit v7 on v6

--- a/solution.py
+++ b/solution.py
@@ -413,7 +413,7 @@
         in_specs=[row(width), row(wide), row(wide), whole_block(w), *anywhere(others)],
         out_specs=[row(2 * wide), row(PAIR)],
         out_shape=[jax.ShapeDtypeStruct((tokens, 2 * wide), bf16), jax.ShapeDtypeStruct((tokens, PAIR), bf16)],
-        compiler_params=limits(48),
+        compiler_params=limits(60),
         cost_estimate=cost(2 * tokens * width * (PAIR + wide), tokens * (2 * width + 12 * wide)),
     )(cotangent, gate, up, w, *others)
 

time: 431 us -> 431 us (level)
    unnamed x65 -> x61, local copies, waits for them, and re-layouts: 15.5 us -> 13.1 us
  transfers between devices with their start and end apart: 25 -> 25, of which waited for: 13 -> 14; matrix products, arithmetic and copies ran while one was open for 12% -> 12% of each run, Pallas kernels for 30% -> 30%
where the time goes in v7:
time: 431 us; the launch traced here: 429 us
  waiting for transfers between devices  156 us (36%)
  Pallas kernels  134 us (31%)
  starting transfers between devices  55.3 us (13%)
  other arithmetic  37 us (9%)
  local copies, waits for them, and re-layouts  32.3 us (7%)
  between operations  14.3 us (3%)
    all_to_all x2, waiting for transfers between devices, to_columns(): own = lax.all_to_all(own, TP, 0, 0, tiled=True)  74.1 us
    ppermute x18, waiting for transfers between devices, shifted(): return lax.ppermute(x, axis, [(i, (i + step) % size) for i in range(size)])  62.1 us
    pallas_call x2, Pallas kernels, dnormed_share(): pl.pallas_call(ignoring(dnormed_kernel, 11 + len(far), len(others)), name...  26.6 us
    ppermute x18, starting transfers between devices, shifted(): return lax.ppermute(x, axis, [(i, (i + step) % size) for i in range(size)])  22.4 us
    pallas_call x1, Pallas kernels, gate_forward(): pl.pallas_call(gate_kernel, name='gate_fwd', grid=(count // 2,), in_specs...  20.9 us
    pallas_call x2, Pallas kernels, split_grads(): pl.pallas_call(ignoring(grads_kernel, 3, len(others)), name='grads', grid...  19.9 us
    all_to_all x2, starting transfers between devices, to_columns(): own = lax.all_to_all(own, TP, 0, 0, tiled=True)  17.7 us
    pallas_call x2, Pallas kernels, branches(): pl.pallas_call(functools.partial(branch_kernel, got is None), name='branc...  14.4 us
  transfers between devices with their start and end apart: 25, of which 14 were waited for; matrix products, arithmetic and copies ran while one was open for 12% of the time, Pallas kernels for 30%

profile of v7, /device:TPU:0, one launch (start us, length us, event | category | flops | bytes accessed | tf_op | source)
XLA Modules:
  0.0 428.9 jit_solution(9321232406263917337)
XLA Ops:
  8.6 1.9 pad_maximum_fusion
  11.3 1.8 copy-done.9
  13.1 2.0 pack.2
  15.1 7.6 %all-to-all-start = ((bf16[16,64,768]{2,1,0:T(8,128)(2,1)}), bf16[16,64,768]{2,1,0:T(8,128)(2,1)}, u32[]{:S(2)}, u32[]{:S(2)}) async-start(bf16[16,64,768]{2,1,0:T(8,128)(2,1)} %pack.2), calls=%async_computation | async-start | bytes 3145728 | tf_op jit(solution)/shard_map/all_to_all | solution.py:654
  24.2 47.9 %all-to-all-done = bf16[16,64,768]{2,1,0:T(8,128)(2,1)} async-done(((bf16[16,64,768]{2,1,0:T(8,128)(2,1)}), bf16[16,64,768]{2,1,0:T(8,128)(2,1)}, u32[]{:S(2)}, u32[]{:S(2)}) %all-to-all-start) | async-done | bytes 1572896 | tf_op jit(solution)/shard_map/all_to_all | solution.py:654
  72.1 10.2 %all-to-all-start.1 = ((bf16[16,64,384]{2,1,0:T(8,128)(2,1)}), bf16[16,64,384]{2,1,0:T(8,128)(2,1)}, u32[]{:S(2)}, u32[]{:S(2)}) async-start(bf16[16,64,384]{2,1,0:T(8,128)(2,1)} %pack.3), calls=%async_computation.1 | async-start | bytes 1572864 | tf_op jit(solution)/shard_map/all_to_all | solution.py:654
  82.3 1.8 collective-permute-start
  86.0 1.7 maximum_maximum_fusion.w_ref.refs_3_
  87.7 26.2 %all-to-all-done.1 = bf16[16,64,384]{2,1,0:T(8,128)(2,1)} async-done(((bf16[16,64,384]{2,1,0:T(8,128)(2,1)}), bf16[16,64,384]{2,1,0:T(8,128)(2,1)}, u32[]{:S(2)}, u32[]{:S(2)}) %all-to-all-start.1) | async-done | bytes 786464 | tf_op jit(solution)/shard_map/all_to_all | solution.py:654
  116.9 2.1 bitcast_dynamic-update-slice_fusion.3
  122.7 9.5 %all-gather.6.cloned.1.call-done = bf16[2176,2048]{1,0:T(8,128)(2,1)} async-done(((bf16[136,2048]{1,0:T(8,128)(2,1)}), bf16[2176,2048]{1,0:T(8,128)(2,1)}) %all-gather.6.cloned.1.call-update) | async-done | bytes 8912912 | tf_op jit(solution)/shard_map/all_gather | solution.py:634
  136.9 5.9 %fusion = (f32[2048,128]{1,0:T(8,128)}, f32[2048,128]{1,0:T(8,128)}, f32[2048,128]{1,0:T(8,128)}) fusion(f32[128]{0:T(128)S(1)} %copy-done.27, f32[2048]{0:T(1024)S(1)} %convert_bitcast_fusion, pred[128]{0:T(512)(128)(4,1)S(1)} %copy-done.28, pred[128]{0:T(512)(128)(4,1)S(1)} %copy-done.29, pred[128]{0:T(512)(128)(4,1)S(1)} %copy-done.26), kind=kLoop, calls=%fused_computation.12 | loop fusion | flops 1310720 | bytes 3154816 | tf_op jit(solution)/shard_map/jit(_where)/select_n | solution.py:52
  142.9 2.1 bitcast_dynamic-update-slice_fusion.2
  145.0 20.9 %gate_fwd.1 = (f32[2048,128]{1,0:T(8,128)}, bf16[2048,2048]{1,0:T(8,128)(2,1)}, f32[2048,384]{1,0:T(8,128)}, f32[2048,384]{1,0:T(8,128)}, bf16[2048,384]{1,0:T(8,128)(2,1)}, /*index=5*/f32[2048,384]{1,0:T(8,128)}) custom-call(bf16[16,136,2048]{2,1,0:T(8,128)(2,1)} %bitcast.77, bf16[16,136,2048]{2,1,0:T(8,128)(2,1)} %bitcast.78, f32[1,2048]{1,0:T(1,128)} %bitcast.90, ...), custom_call_target="tpu_custom_call" | custom-call | flops 1 | bytes 1 | tf_op jit(solution)/shard_map/gate_fwd/pallas_call | solution.py:312
  170.7 1.9 copy-done.8
  172.5 3.3 attend.1
  175.9 5.5 %branch_far.1 = bf16[1024,2048]{1,0:T(8,128)(2,1)} custom-call(s32[8]{0:T(128)S(1)} %stack.134.order_ref, bf16[2048,128]{1,0:T(8,128)(2,1)S(1)} %get-tuple-element.43.ac_ref.bc_ref.refs_0_, bf16[2048,128]{1,0:T(8,128)(2,1)S(1)} %get-tuple-element.43.ac_ref.bc_ref.refs_0_, bf16[2048,384]{1,0:T(8,128)(2,1)S(1)} %copy-done, bf16[2048,384]{1,0:T(8,128)(2,1)S(1)} %copy-done, ...), custom_call_target="tpu_custom_call" | custom-call | flops 1 | bytes 1 | tf_op jit(solution)/shard_map/branch_far/pallas_call | solution.py:372
  181.8 7.1 %collective-permute-done.2.refs_0_ = bf16[1024,2048]{1,0:T(8,128)(2,1)} collective-permute-done((bf16[1024,2048]{1,0:T(8,128)(2,1)}, bf16[1024,2048]{1,0:T(8,128)(2,1)}, u32[]{:S(2)}, u32[]{:S(2)}) %collective-permute-start.2) | collective-permute-done | bytes 4194336 | tf_op jit(solution)/shard_map/ppermute | solution.py:185
  188.9 8.9 %branch_near.1 = (bf16[512,2048]{1,0:T(8,128)(2,1)}, f32[512,2048]{1,0:T(8,128)}) custom-call(s32[8]{0:T(128)S(1)} %stack.125.order_ref, bf16[2048,128]{1,0:T(8,128)(2,1)S(1)} %get-tuple-element.43.ac_ref.bc_ref.refs_0_, bf16[2048,128]{1,0:T(8,128)(2,1)S(1)} %get-tuple-element.43.ac_ref.bc_ref.refs_0_, bf16[2048,384]{1,0:T(8,128)(2,1)S(1)} %copy-done, ...), custom_call_target="tpu_custom_call" | custom-call | flops 1 | bytes 1 | tf_op jit(solution)/shard_map/branch_near/pallas_call | solution.py:372
  199.3 8.9 %all-gather.4.cloned.1.call-done.refs_0_.refs_2_ = bf16[2048,2048]{1,0:T(8,128)(2,1)} async-done(((bf16[128,2048]{1,0:T(8,128)(2,1)}), bf16[2048,2048]{1,0:T(8,128)(2,1)}) %all-gather.4.cloned.1.call-update) | async-done | bytes 8388624 | tf_op jit(solution)/shard_map/all_gather | solution.py:636
  208.2 12.3 %gate_back.1 = (bf16[2048,768]{1,0:T(8,128)(2,1)}, bf16[2048,128]{1,0:T(8,128)(2,1)}) custom-call(bf16[2048,2048]{1,0:T(8,128)(2,1)} %all-gather.4.cloned.1.call-done.refs_0_.refs_2_, f32[2048,384]{1,0:T(8,128)} %get-tuple-element.40.refs_1_, f32[2048,384]{1,0:T(8,128)} %get-tuple-element.41.refs_2_, bf16[512,2048]{1,0:T(8,128)(2,1)} %maximum_maximum_fusion.w_ref.refs_3_, ...), custom_call_target="tpu_custom_call" | custom-call | flops 1 | bytes 1 | tf_op jit(solution)/shard_map/gate_back/pallas_call | solution.py:409
  220.5 11.2 %grads.2 = (f32[16,64,768]{2,1,0:T(8,128)}, bf16[16,64,768]{2,1,0:T(8,128)(2,1)}) custom-call(s32[1]{0:T(128)} %bitcast.12.part_ref.refs_0_, bf16[2048,2048]{1,0:T(8,128)(2,1)} %get-tuple-element.50.refs_1_, bf16[2048,768]{1,0:T(8,128)(2,1)} %get-tuple-element.46.refs_2_.refs_5_.refs_6_), custom_call_target="tpu_custom_call" | custom-call | flops 1 | bytes 1 | tf_op jit(solution)/shard_map/grads/pallas_call | solution.py:438
  233.8 8.2 %attend_back.1 = (bf16[2048,384]{1,0:T(8,128)(2,1)}, f32[1,384]{1,0:T(1,128)}) custom-call(bf16[2048,384]{1,0:T(8,128)(2,1)} %copy-done.12, f32[16,256,128]{2,1,0:T(8,128)} %copy-done.10, bf16[2048,128]{1,0:T(8,128)(2,1)} %get-tuple-element.49.refs_2_, f32[2048,128]{1,0:T(8,128)} %get-tuple-element.88.refs_1_.own_ref.refs_3_, ...), custom_call_target="tpu_custom_call" | custom-call | flops 536870912 | bytes 12288000 | tf_op jit(solution)/shard_map/attend_back/pallas_call | solution.py:164
  242.0 3.8 collective-permute-done.3.refs_12_
  247.2 14.2 %dn_far.1 = (bf16[256,2048]{1,0:T(8,128)(2,1)}, bf16[256,2048]{1,0:T(8,128)(2,1)}, bf16[256,2048]{1,0:T(8,128)(2,1)}, bf16[256,2048]{1,0:T(8,128)(2,1)}, bf16[512,2048]{1,0:T(8,128)(2,1)}, /*index=5*/f32[8,2048]{1,0:T(8,128)}) custom-call(s32[8]{0:T(128)} %stack.116.refs_0_, bf16[16,136,2048]{2,1,0:T(8,128)(2,1)} %bitcast.79, ...), custom_call_target="tpu_custom_call" | custom-call | flops 1 | bytes 1 | tf_op jit(solution)/shard_map/dn_far/pallas_call | solution.py:532
  263.5 12.4 %dn_near.1 = (f32[1024,2048]{1,0:T(8,128)}, f32[8,2048]{1,0:T(8,128)}) custom-call(s32[8]{0:T(128)} %stack.143.refs_0_, bf16[16,136,2048]{2,1,0:T(8,128)(2,1)} %bitcast.81, bf16[16,136,2048]{2,1,0:T(8,128)(2,1)} %bitcast.82, f32[2048,128]{1,0:T(8,128)} %get-tuple-element.39.refs_3_.refs_4_, f32[2048,128]{1,0:T(8,128)} %get-tuple-element.39.refs_3_.refs_4_, ...), custom_call_target="tpu_custom_call" | custom-call | flops 1 | bytes 1 | tf_op jit(solution)/shard_map/dn_near/pallas_call | solution.py:532
  278.6 6.4 %combine.1 = (bf16[256,2048]{1,0:T(8,128)(2,1)}, bf16[256,2048]{1,0:T(8,128)(2,1)S(1)}, f32[512,2048]{1,0:T(8,128)}) custom-call(f32[1024,2048]{1,0:T(8,128)} %get-tuple-element.59.refs_0_, bf16[256,2048]{1,0:T(8,128)(2,1)S(1)} %collective-permute-done.4.refs_1_, bf16[256,2048]{1,0:T(8,128)(2,1)S(1)} %collective-permute-done.5.refs_2_, ...), custom_call_target="tpu_custom_call" | custom-call | flops 1 | bytes 1 | tf_op jit(solution)/shard_map/combine/pallas_call | solution.py:581
  287.5 1.9 copy-done.16
  289.4 3.4 add_convert_fusion.refs_3_
  292.8 4.7 %all-to-all-start.2 = ((bf16[16,64,768]{2,1,0:T(8,128)(2,1)}), bf16[16,64,768]{2,1,0:T(8,128)(2,1)}, u32[]{:S(2)}, u32[]{:S(2)}) async-start(bf16[16,64,768]{2,1,0:T(8,128)(2,1)} %add_convert_fusion.refs_3_), calls=%async_computation.3 | async-start | bytes 3145728 | tf_op jit(solution)/shard_map/all_to_all | solution.py:716
  297.5 8.7 %grads.3 = (f32[16,64,384]{2,1,0:T(8,128)}, bf16[16,64,384]{2,1,0:T(8,128)(2,1)}) custom-call(s32[1]{0:T(128)} %bitcast.12.part_ref.refs_0_, bf16[2048,2048]{1,0:T(8,128)(2,1)} %get-tuple-element.50.refs_1_, bf16[2048,384]{1,0:T(8,128)(2,1)} %get-tuple-element.52.refs_7_.refs_8_.refs_2_, bf16[16,64,768]{2,1,0:T(8,128)(2,1)} %add_convert_fusion.refs_3_), custom_call_target="tpu_custom_call" | custom-call | flops 1 | bytes 1 | tf_op jit(solution)/shard_map/grads/pallas_call | solution.py:438
  307.6 8.8 %rows.1.refs_3_ = bf16[480,2048]{1,0:T(8,128)(2,1)} custom-call(bf16[2048,128]{1,0:T(8,128)(2,1)} %copy-done.5, bf16[2048,384]{1,0:T(8,128)(2,1)} %get-tuple-element.44.ah_ref.bh_ref.refs_1_, bf16[2048,2048]{1,0:T(8,128)(2,1)} %all-gather.4.cloned.1.call-done.refs_0_.refs_2_, bf16[16,64,384]{2,1,0:T(8,128)(2,1)} %get-tuple-element.67.refs_3_), custom_call_target="tpu_custom_call" | custom-call | flops 1 | bytes 1 | tf_op jit(solution)/shard_map/rows/pallas_call | solution.py:467
  317.6 2.5 add_convert_fusion.3
  322.2 4.7 %collective-permute-done.15 = bf16[16,64,384]{2,1,0:T(8,128)(2,1)S(1)} collective-permute-done((bf16[16,64,384]{2,1,0:T(8,128)(2,1)}, bf16[16,64,384]{2,1,0:T(8,128)(2,1)S(1)}, u32[]{:S(2)}, u32[]{:S(2)}) %collective-permute-start.15) | collective-permute-done | bytes 786464 | tf_op jit(solution)/shard_map/ppermute | solution.py:185
  327.9 3.7 collective-permute-start.10
  331.7 19.1 %collective-permute-done.12 = bf16[256,2048]{1,0:T(8,128)(2,1)} collective-permute-done((bf16[256,2048]{1,0:T(8,128)(2,1)}, bf16[256,2048]{1,0:T(8,128)(2,1)}, u32[]{:S(2)}, u32[]{:S(2)}) %collective-permute-start.12) | collective-permute-done | bytes 1048608 | tf_op jit(solution)/shard_map/ppermute | solution.py:185
  350.8 2.3 add_convert_fusion.2
  353.1 2.5 collective-permute-start.13
  357.0 10.3 %all-to-all-start.3 = ((bf16[16,64,384]{2,1,0:T(8,128)(2,1)}), bf16[16,64,384]{2,1,0:T(8,128)(2,1)S(1)}, u32[]{:S(2)}, u32[]{:S(2)}) async-start(bf16[16,64,384]{2,1,0:T(8,128)(2,1)} %after.7), calls=%async_computation.4 | async-start | bytes 1572864 | tf_op jit(solution)/shard_map/all_to_all | solution.py:745
  367.3 1.7 collective-permute-done.17
  369.1 2.9 convert_add_fusion
  371.9 1.9 slice.164
  374.9 18.4 %collective-permute-done.9 = bf16[128,2048]{1,0:T(8,128)(2,1)} collective-permute-done((bf16[128,2048]{1,0:T(8,128)(2,1)S(1)}, bf16[128,2048]{1,0:T(8,128)(2,1)}, u32[]{:S(2)}, u32[]{:S(2)}) %collective-permute-start.9) | collective-permute-done | bytes 524320 | tf_op jit(solution)/shard_map/ppermute | solution.py:185
  393.3 2.5 fusion.31
  402.1 1.9 convert_add_fusion.2
  404.0 6.1 %unpack.3 = f32[128,11264]{1,0:T(8,128)} custom-call(s32[1]{0:T(128)} %bitcast.12.part_ref.refs_0_, bf16[16,64,768]{2,1,0:T(8,128)(2,1)} %all-to-all-done.2.refs_1_.own_ref, bf16[16,64,768]{2,1,0:T(8,128)(2,1)S(1)} %collective-permute-done.14.other_ref), custom_call_target="tpu_custom_call" | custom-call | flops 1 | bytes 1 | tf_op jit(solution)/shard_map/unpack/pallas_call | solution.py:266
  413.1 5.8 %collective-permute-done.16.other_ref = bf16[16,64,384]{2,1,0:T(8,128)(2,1)S(1)} collective-permute-done((bf16[16,64,384]{2,1,0:T(8,128)(2,1)S(1)}, bf16[16,64,384]{2,1,0:T(8,128)(2,1)S(1)}, u32[]{:S(2)}, u32[]{:S(2)}) %collective-permute-start.16) | collective-permute-done | bytes 786464 | tf_op jit(solution)/shard_map/ppermute | solution.py:185
  419.0 3.4 unpack.2
  (160 shorter events, 51.8 us)
Async XLA Ops:
  7.2 125.0 %all-gather.6.cloned.1.call-start = ((), (), s32[]{:S(2)}) async-start(), calls=%async_computation.7 | async-start | bytes 9469952 | tf_op jit(solution)/shard_map/all_gather | solution.py:634
  10.5 197.6 %all-gather.4.cloned.1.call-start = ((), (), s32[]{:S(2)}) async-start(), calls=%async_computation.5 | async-start | bytes 8912896 | tf_op jit(solution)/shard_map/all_gather | solution.py:636
  11.3 1.8 copy-start.9
  15.1 7.6 %copy-start.11 = (bf16[128,6144]{1,0:T(8,128)(2,1)S(1)}, bf16[128,6144]{1,0:T(8,128)(2,1)}, u32[]{:S(2)}) copy-start(bf16[128,6144]{1,0:T(8,128)(2,1)} %own_ref.3) | copy-start | bytes 4718596
  15.1 57.0 %all-to-all-start = ((bf16[16,64,768]{2,1,0:T(8,128)(2,1)}), bf16[16,64,768]{2,1,0:T(8,128)(2,1)}, u32[]{:S(2)}, u32[]{:S(2)}) async-start(bf16[16,64,768]{2,1,0:T(8,128)(2,1)} %pack.2), calls=%async_computation | async-start | bytes 3145728 | tf_op jit(solution)/shard_map/all_to_all | solution.py:654
  22.7 63.2 %copy-start.22 = (bf16[352,2048]{1,0:T(8,128)(2,1)S(1)}, bf16[352,2048]{1,0:T(8,128)(2,1)}, u32[]{:S(2)}) copy-start(bf16[352,2048]{1,0:T(8,128)(2,1)} %param.18) | copy-start | bytes 4325380
  22.7 63.2 %copy-start.24 = (bf16[128,2048]{1,0:T(8,128)(2,1)S(1)}, bf16[128,2048]{1,0:T(8,128)(2,1)}, u32[]{:S(2)}) copy-start(bf16[128,2048]{1,0:T(8,128)(2,1)} %param.16) | copy-start | bytes 1572868
  72.1 41.8 %all-to-all-start.1 = ((bf16[16,64,384]{2,1,0:T(8,128)(2,1)}), bf16[16,64,384]{2,1,0:T(8,128)(2,1)}, u32[]{:S(2)}, u32[]{:S(2)}) async-start(bf16[16,64,384]{2,1,0:T(8,128)(2,1)} %pack.3), calls=%async_computation.1 | async-start | bytes 1572864 | tf_op jit(solution)/shard_map/all_to_all | solution.py:654
  82.2 274.8 %reduce-scatter.2.cloned.1.call-start = ((), (), s32[]{:S(2)}) async-start(), calls=%async_computation.6 | async-start | bytes 2621440 | tf_op jit(solution)/shard_map/reduce_scatter | solution.py:699
  82.3 38.7 %collective-permute-start = (bf16[16,64,768]{2,1,0:T(8,128)(2,1)}, bf16[16,64,768]{2,1,0:T(8,128)(2,1)}, u32[]{:S(2)}, u32[]{:S(2)}) collective-permute-start(bf16[16,64,768]{2,1,0:T(8,128)(2,1)} %all-to-all-done), channel_id=1, source_target_pairs={{0,16},{16,0},{1,17},{17,1},{2,18},{18,2},{3,19},{19,3},{4,20},{20... | collective-permute-start | bytes 4718600 | tf_op jit(solution)/shard_map/ppermute | solution.py:185
  113.9 29.0 %collective-permute-start.1 = (bf16[16,64,384]{2,1,0:T(8,128)(2,1)}, bf16[16,64,384]{2,1,0:T(8,128)(2,1)}, u32[]{:S(2)}, u32[]{:S(2)}) collective-permute-start(bf16[16,64,384]{2,1,0:T(8,128)(2,1)} %all-to-all-done.1), channel_id=1, source_target_pairs={{0,16},{16,0},{1,17},{17,1},{2,18},{18,2},{3,19},{19,3},{4,20},{20... | collective-permute-start | bytes 2359304 | tf_op jit(solution)/shard_map/ppermute | solution.py:185
  122.6 20.3 %copy-start.13 = (bf16[16,2,64,768]{3,2,1,0:T(8,128)(2,1)}, bf16[16,2,64,768]{3,2,1,0:T(8,128)(2,1)S(1)}, u32[]{:S(2)}) copy-start(bf16[16,2,64,768]{3,2,1,0:T(8,128)(2,1)S(1)} %bitcast_dynamic-update-slice_fusion) | copy-start | bytes 9437188
  122.6 14.3 %copy-start.26 = (pred[128]{0:T(512)(128)(4,1)S(1)}, pred[128]{0:T(512)(128)(4,1)}, u32[]{:S(2)}) copy-start(pred[128]{0:T(512)(128)(4,1)} %broadcast_compare_fusion.1) | copy-start | bytes 388
  122.6 14.3 %copy-start.27 = (f32[128]{0:T(128)S(1)}, f32[128]{0:T(128)}, u32[]{:S(2)}) copy-start(f32[128]{0:T(128)} %fusion.29) | copy-start | bytes 1540
  122.6 14.3 %copy-start.28 = (pred[128]{0:T(512)(128)(4,1)S(1)}, pred[128]{0:T(512)(128)(4,1)}, u32[]{:S(2)}) copy-start(pred[128]{0:T(512)(128)(4,1)} %get-tuple-element.91) | copy-start | bytes 388
  122.6 14.3 %copy-start.29 = (pred[128]{0:T(512)(128)(4,1)S(1)}, pred[128]{0:T(512)(128)(4,1)}, u32[]{:S(2)}) copy-start(pred[128]{0:T(512)(128)(4,1)} %get-tuple-element.92) | copy-start | bytes 388
  145.0 21.7 %copy-start.2 = (f32[2048,128]{1,0:T(8,128)S(1)}, f32[2048,128]{1,0:T(8,128)}, u32[]{:S(2)}) copy-start(f32[2048,128]{1,0:T(8,128)} %get-tuple-element.86.refs_3_.before_ref.refs_5_) | copy-start | bytes 3145732
  170.7 1.9 copy-start.8
  172.5 3.4 copy-start
  172.5 3.4 copy-start.1
  175.9 5.5 %copy-start.10 = (f32[16,256,128]{2,1,0:T(8,128)}, f32[16,256,128]{2,1,0:T(8,128)S(1)}, u32[]{:S(2)}) copy-start(f32[16,256,128]{2,1,0:T(8,128)S(1)} %get-tuple-element.48.refs_1_) | copy-start | bytes 6291460
  175.9 5.5 %copy-start.12 = (bf16[2048,384]{1,0:T(8,128)(2,1)}, bf16[2048,384]{1,0:T(8,128)(2,1)S(1)}, u32[]{:S(2)}) copy-start(bf16[2048,384]{1,0:T(8,128)(2,1)S(1)} %get-tuple-element.47.refs_0_) | copy-start | bytes 4718596
  175.9 13.0 %copy-start.5 = (bf16[2048,128]{1,0:T(8,128)(2,1)}, bf16[2048,128]{1,0:T(8,128)(2,1)S(1)}, u32[]{:S(2)}) copy-start(bf16[2048,128]{1,0:T(8,128)(2,1)S(1)} %get-tuple-element.43.ac_ref.bc_ref.refs_0_) | copy-start | bytes 1572868
  181.4 7.5 %collective-permute-start.2 = (bf16[1024,2048]{1,0:T(8,128)(2,1)}, bf16[1024,2048]{1,0:T(8,128)(2,1)}, u32[]{:S(2)}, u32[]{:S(2)}) collective-permute-start(bf16[1024,2048]{1,0:T(8,128)(2,1)} %branch_far.1), channel_id=1, source_target_pairs={{0,1},{1,0},{2,3},{3,2},{4,5},{5,4},{6,7},{7,6},{8,9},{9,8},{10,11... | collective-permute-start | bytes 12582920 | tf_op jit(solution)/shard_map/ppermute | solution.py:185
  197.8 48.0 %collective-permute-start.3 = (bf16[512,2048]{1,0:T(8,128)(2,1)}, bf16[512,2048]{1,0:T(8,128)(2,1)S(1)}, u32[]{:S(2)}, u32[]{:S(2)}) collective-permute-start(bf16[512,2048]{1,0:T(8,128)(2,1)} %get-tuple-element.45.refs_4_), channel_id=1, source_target_pairs={{0,2},{2,0},{1,3},{3,1},{4,6},{6,4},{5,7},{7,5},{8,10},{10,8},{9,1... | collective-permute-start | bytes 6291464 | tf_op jit(solution)/shard_map/ppermute | solution.py:185
  231.6 55.9 %collective-permute-start.11 = (bf16[16,64,768]{2,1,0:T(8,128)(2,1)}, bf16[16,64,768]{2,1,0:T(8,128)(2,1)}, u32[]{:S(2)}, u32[]{:S(2)}) collective-permute-start(bf16[16,64,768]{2,1,0:T(8,128)(2,1)} %get-tuple-element.51.refs_6_), channel_id=1, source_target_pairs={{0,16},{16,0},{1,17},{17,1},{2,18},{18,2},{3,19},{19,3},{4,20},{20... | collective-permute-start | bytes 4718600 | tf_op jit(solution)/shard_map/ppermute | solution.py:185
  261.3 1.9 copy-start.25
  261.4 17.3 %collective-permute-start.4 = (bf16[256,2048]{1,0:T(8,128)(2,1)}, bf16[256,2048]{1,0:T(8,128)(2,1)S(1)}, u32[]{:S(2)}, u32[]{:S(2)}) collective-permute-start(bf16[256,2048]{1,0:T(8,128)(2,1)} %get-tuple-element.55.refs_11_), channel_id=1, source_target_pairs={{0,1},{1,0},{2,3},{3,2},{4,5},{5,4},{6,7},{7,6},{8,9},{9,8},{10,11... | collective-permute-start | bytes 3145736 | tf_op jit(solution)/shard_map/ppermute | solution.py:185
  261.4 17.2 %collective-permute-start.5 = (bf16[256,2048]{1,0:T(8,128)(2,1)}, bf16[256,2048]{1,0:T(8,128)(2,1)S(1)}, u32[]{:S(2)}, u32[]{:S(2)}) collective-permute-start(bf16[256,2048]{1,0:T(8,128)(2,1)} %get-tuple-element.56.refs_12_), channel_id=1, source_target_pairs={{0,1},{1,0},{2,3},{3,2},{4,5},{5,4},{6,7},{7,6},{8,9},{9,8},{10,11... | collective-permute-start | bytes 3145736 | tf_op jit(solution)/shard_map/ppermute | solution.py:185
  261.9 16.7 %collective-permute-start.6 = (bf16[256,2048]{1,0:T(8,128)(2,1)}, bf16[256,2048]{1,0:T(8,128)(2,1)S(1)}, u32[]{:S(2)}, u32[]{:S(2)}) collective-permute-start(bf16[256,2048]{1,0:T(8,128)(2,1)} %get-tuple-element.57.refs_13_), channel_id=1, source_target_pairs={{0,1},{1,0},{2,3},{3,2},{4,5},{5,4},{6,7},{7,6},{8,9},{9,8},{10,11... | collective-permute-start | bytes 3145736 | tf_op jit(solution)/shard_map/ppermute | solution.py:185
  262.0 16.6 %collective-permute-start.7 = (bf16[256,2048]{1,0:T(8,128)(2,1)}, bf16[256,2048]{1,0:T(8,128)(2,1)}, u32[]{:S(2)}, u32[]{:S(2)}) collective-permute-start(bf16[256,2048]{1,0:T(8,128)(2,1)} %get-tuple-element.58.refs_14_), channel_id=1, source_target_pairs={{0,1},{1,0},{2,3},{3,2},{4,5},{5,4},{6,7},{7,6},{8,9},{9,8},{10,11... | collective-permute-start | bytes 3145736 | tf_op jit(solution)/shard_map/ppermute | solution.py:185
  286.1 31.5 %collective-permute-start.8 = (bf16[256,2048]{1,0:T(8,128)(2,1)}, bf16[256,2048]{1,0:T(8,128)(2,1)}, u32[]{:S(2)}, u32[]{:S(2)}) collective-permute-start(bf16[256,2048]{1,0:T(8,128)(2,1)} %get-tuple-element.61.refs_1_), channel_id=1, source_target_pairs={{0,2},{2,0},{1,3},{3,1},{4,6},{6,4},{5,7},{7,5},{8,10},{10,8},{9,1... | collective-permute-start | bytes 3145736 | tf_op jit(solution)/shard_map/ppermute | solution.py:185
  287.5 1.9 copy-start.16
  292.8 62.8 %all-to-all-start.2 = ((bf16[16,64,768]{2,1,0:T(8,128)(2,1)}), bf16[16,64,768]{2,1,0:T(8,128)(2,1)}, u32[]{:S(2)}, u32[]{:S(2)}) async-start(bf16[16,64,768]{2,1,0:T(8,128)(2,1)} %add_convert_fusion.refs_3_), calls=%async_computation.3 | async-start | bytes 3145728 | tf_op jit(solution)/shard_map/all_to_all | solution.py:716
  306.2 11.3 %copy-start.15 = (f32[512,2048]{1,0:T(8,128)S(1)}, f32[512,2048]{1,0:T(8,128)}, u32[]{:S(2)}) copy-start(f32[512,2048]{1,0:T(8,128)} %get-tuple-element.60) | copy-start | bytes 12582916
  306.2 20.6 %collective-permute-start.15 = (bf16[16,64,384]{2,1,0:T(8,128)(2,1)}, bf16[16,64,384]{2,1,0:T(8,128)(2,1)S(1)}, u32[]{:S(2)}, u32[]{:S(2)}) collective-permute-start(bf16[16,64,384]{2,1,0:T(8,128)(2,1)} %get-tuple-element.67.refs_3_), channel_id=1, source_target_pairs={{0,16},{16,0},{1,17},{17,1},{2,18},{18,2},{3,19},{19,3},{4,20},{20... | collective-permute-start | bytes 2359304 | tf_op jit(solution)/shard_map/ppermute | solution.py:185
  316.3 52.7 %collective-permute-start.17 = (bf16[480,2048]{1,0:T(8,128)(2,1)}, bf16[480,2048]{1,0:T(8,128)(2,1)}, u32[]{:S(2)}, u32[]{:S(2)}) collective-permute-start(bf16[480,2048]{1,0:T(8,128)(2,1)} %rows.1.refs_3_), channel_id=1, source_target_pairs={{0,16},{16,0},{1,17},{17,1},{2,18},{18,2},{3,19},{19,3},{4,20},{20... | collective-permute-start | bytes 5898248 | tf_op jit(solution)/shard_map/ppermute | solution.py:185
  320.0 6.8 %copy-start.21 = (f32[16,64,384]{2,1,0:T(8,128)S(1)}, f32[16,64,384]{2,1,0:T(8,128)}, u32[]{:S(2)}) copy-start(f32[16,64,384]{2,1,0:T(8,128)} %get-tuple-element.68) | copy-start | bytes 4718596
  320.0 30.8 %collective-permute-start.12 = (bf16[256,2048]{1,0:T(8,128)(2,1)}, bf16[256,2048]{1,0:T(8,128)(2,1)}, u32[]{:S(2)}, u32[]{:S(2)}) collective-permute-start(bf16[256,2048]{1,0:T(8,128)(2,1)} %after.6), channel_id=1, source_target_pairs={{0,2},{2,0},{1,3},{3,1},{4,6},{6,4},{5,7},{7,5},{8,10},{10,8},{9,1... | collective-permute-start | bytes 3145736 | tf_op jit(solution)/shard_map/ppermute | solution.py:185
  321.7 9.9 %copy-start.19 = (bf16[128,2048]{1,0:T(8,128)(2,1)S(1)}, bf16[128,2048]{1,0:T(8,128)(2,1)}, u32[]{:S(2)}) copy-start(bf16[128,2048]{1,0:T(8,128)(2,1)} %get-tuple-element.75.refs_1_) | copy-start | bytes 1572868
  327.9 47.0 %collective-permute-start.10 = (bf16[128,2048]{1,0:T(8,128)(2,1)}, bf16[128,2048]{1,0:T(8,128)(2,1)}, u32[]{:S(2)}, u32[]{:S(2)}) collective-permute-start(bf16[128,2048]{1,0:T(8,128)(2,1)} %get-tuple-element.74.refs_2_), channel_id=1, source_target_pairs={{0,12},{4,0},{8,4},{12,8},{1,13},{5,1},{9,5},{13,9},{2,14},{6,2},{... | collective-permute-start | bytes 1572872 | tf_op jit(solution)/shard_map/ppermute | solution.py:185
  331.6 61.7 %collective-permute-start.9 = (bf16[128,2048]{1,0:T(8,128)(2,1)S(1)}, bf16[128,2048]{1,0:T(8,128)(2,1)}, u32[]{:S(2)}, u32[]{:S(2)}) collective-permute-start(bf16[128,2048]{1,0:T(8,128)(2,1)S(1)} %copy-done.19), channel_id=1, source_target_pairs={{0,8},{4,12},{8,0},{12,4},{1,9},{5,13},{9,1},{13,5},{2,10},{6,14},... | collective-permute-start | bytes 1572872 | tf_op jit(solution)/shard_map/ppermute | solution.py:185
  353.1 40.2 %collective-permute-start.13 = (bf16[128,2048]{1,0:T(8,128)(2,1)}, bf16[128,2048]{1,0:T(8,128)(2,1)}, u32[]{:S(2)}, u32[]{:S(2)}) collective-permute-start(bf16[128,2048]{1,0:T(8,128)(2,1)} %add_convert_fusion.2), channel_id=1, source_target_pairs={{0,4},{4,8},{8,12},{12,0},{1,5},{5,9},{9,13},{13,1},{2,6},{6,10},{... | collective-permute-start | bytes 1572872 | tf_op jit(solution)/shard_map/ppermute | solution.py:185
  355.6 46.5 %collective-permute-start.14 = (bf16[16,64,768]{2,1,0:T(8,128)(2,1)}, bf16[16,64,768]{2,1,0:T(8,128)(2,1)S(1)}, u32[]{:S(2)}, u32[]{:S(2)}) collective-permute-start(bf16[16,64,768]{2,1,0:T(8,128)(2,1)} %all-to-all-done.2.refs_1_.own_ref), channel_id=1, source_target_pairs={{0,16},{16,0},{1,17},{17,1},{2,18},{18,2},{3,19},{19,3},{4,20},{20... | collective-permute-start | bytes 4718600 | tf_op jit(solution)/shard_map/ppermute | solution.py:185
  357.0 42.4 %all-to-all-start.3 = ((bf16[16,64,384]{2,1,0:T(8,128)(2,1)}), bf16[16,64,384]{2,1,0:T(8,128)(2,1)S(1)}, u32[]{:S(2)}, u32[]{:S(2)}) async-start(bf16[16,64,384]{2,1,0:T(8,128)(2,1)} %after.7), calls=%async_computation.4 | async-start | bytes 1572864 | tf_op jit(solution)/shard_map/all_to_all | solution.py:745
  393.3 3.7 copy-start.17
  393.3 3.7 copy-start.18
  399.4 19.6 %collective-permute-start.16 = (bf16[16,64,384]{2,1,0:T(8,128)(2,1)S(1)}, bf16[16,64,384]{2,1,0:T(8,128)(2,1)S(1)}, u32[]{:S(2)}, u32[]{:S(2)}) collective-permute-start(bf16[16,64,384]{2,1,0:T(8,128)(2,1)S(1)} %all-to-all-done.3.own_ref), channel_id=1, source_target_pairs={{0,16},{16,0},{1,17},{17,1},{2,18},{18,2},{3,19},{19,3},{4,20},{20... | collective-permute-start | bytes 2359304 | tf_op jit(solution)/shard_map/ppermute | solution.py:185
  (7 other events, 8.8 us)
Sparse Core Ops, SparseCore 0:
  10.9 121.2 all-gather.5
  134.3 73.7 all-gather.3
  262.6 50.3 reduce-scatter.1

commit v8 on v6

--- a/solution.py
+++ b/solution.py
@@ -15,7 +15,7 @@
 TP = ("z", "y", "c")
 LANES = 128
 SEQUENCES = 8
-CHUNK = 512
+CHUNK = 1024
 
 epsilon = 1e-05
 rope_base = 10000.0

time: 431 us -> 431 us (level)
  transfers between devices with their start and end apart: 25 -> 25, of which waited for: 13 -> 14; matrix products, arithmetic and copies ran while one was open for 12% -> 12% of each run, Pallas kernels for 30% -> 30%
where the time goes in v8:
time: 431 us; the launch traced here: 429 us
  waiting for transfers between devices  155 us (36%)
  Pallas kernels  133 us (31%)
  starting transfers between devices  55.4 us (13%)
  other arithmetic  36.9 us (9%)
  local copies, waits for them, and re-layouts  34.7 us (8%)
  between operations  14.3 us (3%)
    all_to_all x2, waiting for transfers between devices, to_columns(): own = lax.all_to_all(own, TP, 0, 0, tiled=True)  74.1 us
    ppermute x18, waiting for transfers between devices, shifted(): return lax.ppermute(x, axis, [(i, (i + step) % size) for i in range(size)])  60.5 us
    pallas_call x2, Pallas kernels, dnormed_share(): pl.pallas_call(ignoring(dnormed_kernel, 11 + len(far), len(others)), name...  26.7 us
    ppermute x18, starting transfers between devices, shifted(): return lax.ppermute(x, axis, [(i, (i + step) % size) for i in range(size)])  22.5 us
    pallas_call x1, Pallas kernels, gate_forward(): pl.pallas_call(gate_kernel, name='gate_fwd', grid=(count // 2,), in_specs...  20.9 us
    pallas_call x2, Pallas kernels, split_grads(): pl.pallas_call(ignoring(grads_kernel, 3, len(others)), name='grads', grid...  19.9 us
    all_to_all x2, starting transfers between devices, to_columns(): own = lax.all_to_all(own, TP, 0, 0, tiled=True)  17.7 us
    unnamed x65, local copies, waits for them, and re-layouts  15.5 us
  transfers between devices with their start and end apart: 25, of which 14 were waited for; matrix products, arithmetic and copies ran while one was open for 12% of the time, Pallas kernels for 30%

profile of v8, /device:TPU:0, one launch (start us, length us, event | category | flops | bytes accessed | tf_op | source)
XLA Modules:
  0.0 429.0 jit_solution(16748235778716587097)
XLA Ops:
  8.6 1.9 pad_maximum_fusion
  11.3 1.8 copy-done.10
  13.1 2.0 pack.2
  15.1 7.6 %all-to-all-start = ((bf16[16,64,768]{2,1,0:T(8,128)(2,1)}), bf16[16,64,768]{2,1,0:T(8,128)(2,1)}, u32[]{:S(2)}, u32[]{:S(2)}) async-start(bf16[16,64,768]{2,1,0:T(8,128)(2,1)} %pack.2), calls=%async_computation | async-start | bytes 3145728 | tf_op jit(solution)/shard_map/all_to_all | solution.py:654
  24.2 47.9 %all-to-all-done = bf16[16,64,768]{2,1,0:T(8,128)(2,1)} async-done(((bf16[16,64,768]{2,1,0:T(8,128)(2,1)}), bf16[16,64,768]{2,1,0:T(8,128)(2,1)}, u32[]{:S(2)}, u32[]{:S(2)}) %all-to-all-start) | async-done | bytes 1572896 | tf_op jit(solution)/shard_map/all_to_all | solution.py:654
  72.1 10.2 %all-to-all-start.1 = ((bf16[16,64,384]{2,1,0:T(8,128)(2,1)}), bf16[16,64,384]{2,1,0:T(8,128)(2,1)}, u32[]{:S(2)}, u32[]{:S(2)}) async-start(bf16[16,64,384]{2,1,0:T(8,128)(2,1)} %pack.3), calls=%async_computation.1 | async-start | bytes 1572864 | tf_op jit(solution)/shard_map/all_to_all | solution.py:654
  82.3 1.8 collective-permute-start
  87.6 26.3 %all-to-all-done.1 = bf16[16,64,384]{2,1,0:T(8,128)(2,1)} async-done(((bf16[16,64,384]{2,1,0:T(8,128)(2,1)}), bf16[16,64,384]{2,1,0:T(8,128)(2,1)}, u32[]{:S(2)}, u32[]{:S(2)}) %all-to-all-start.1) | async-done | bytes 786464 | tf_op jit(solution)/shard_map/all_to_all | solution.py:654
  116.9 2.1 bitcast_dynamic-update-slice_fusion.3
  122.7 9.5 %all-gather.6.cloned.1.call-done = bf16[2176,2048]{1,0:T(8,128)(2,1)} async-done(((bf16[136,2048]{1,0:T(8,128)(2,1)}), bf16[2176,2048]{1,0:T(8,128)(2,1)}) %all-gather.6.cloned.1.call-update) | async-done | bytes 8912912 | tf_op jit(solution)/shard_map/all_gather | solution.py:634
  136.9 5.9 %fusion = (f32[2048,128]{1,0:T(8,128)}, f32[2048,128]{1,0:T(8,128)}, f32[2048,128]{1,0:T(8,128)}) fusion(f32[128]{0:T(128)S(1)} %copy-done.29, f32[2048]{0:T(1024)S(1)} %convert_bitcast_fusion, pred[128]{0:T(512)(128)(4,1)S(1)} %copy-done.30, pred[128]{0:T(512)(128)(4,1)S(1)} %copy-done.31, pred[128]{0:T(512)(128)(4,1)S(1)} %copy-done.28), kind=kLoop, calls=%fused_computation.12 | loop fusion | flops 1310720 | bytes 3154816 | tf_op jit(solution)/shard_map/jit(_where)/select_n | solution.py:52
  142.9 2.2 bitcast_dynamic-update-slice_fusion.2
  145.1 20.9 %gate_fwd.1 = (f32[2048,128]{1,0:T(8,128)}, bf16[2048,2048]{1,0:T(8,128)(2,1)}, f32[2048,384]{1,0:T(8,128)}, f32[2048,384]{1,0:T(8,128)}, bf16[2048,384]{1,0:T(8,128)(2,1)}, /*index=5*/f32[2048,384]{1,0:T(8,128)}) custom-call(bf16[16,136,2048]{2,1,0:T(8,128)(2,1)} %bitcast.77, bf16[16,136,2048]{2,1,0:T(8,128)(2,1)} %bitcast.78, f32[1,2048]{1,0:T(1,128)} %bitcast.90, ...), custom_call_target="tpu_custom_call" | custom-call | flops 1 | bytes 1 | tf_op jit(solution)/shard_map/gate_fwd/pallas_call | solution.py:312
  170.7 1.9 copy-done.9
  172.6 3.3 attend.1
  176.0 5.5 %branch_far.1 = bf16[1024,2048]{1,0:T(8,128)(2,1)} custom-call(s32[8]{0:T(128)S(1)} %stack.134.order_ref, bf16[2048,128]{1,0:T(8,128)(2,1)S(1)} %get-tuple-element.43.ac_ref.bc_ref.refs_0_, bf16[2048,128]{1,0:T(8,128)(2,1)S(1)} %get-tuple-element.43.ac_ref.bc_ref.refs_0_, bf16[2048,384]{1,0:T(8,128)(2,1)S(1)} %copy-done, bf16[2048,384]{1,0:T(8,128)(2,1)S(1)} %copy-done, ...), custom_call_target="tpu_custom_call" | custom-call | flops 1 | bytes 1 | tf_op jit(solution)/shard_map/branch_far/pallas_call | solution.py:372
  181.9 7.1 %collective-permute-done.2.refs_0_ = bf16[1024,2048]{1,0:T(8,128)(2,1)} collective-permute-done((bf16[1024,2048]{1,0:T(8,128)(2,1)}, bf16[1024,2048]{1,0:T(8,128)(2,1)}, u32[]{:S(2)}, u32[]{:S(2)}) %collective-permute-start.2) | collective-permute-done | bytes 4194336 | tf_op jit(solution)/shard_map/ppermute | solution.py:185
  189.0 8.9 %branch_near.1 = (bf16[512,2048]{1,0:T(8,128)(2,1)}, f32[512,2048]{1,0:T(8,128)}) custom-call(s32[8]{0:T(128)S(1)} %stack.125.order_ref, bf16[2048,128]{1,0:T(8,128)(2,1)S(1)} %get-tuple-element.43.ac_ref.bc_ref.refs_0_, bf16[2048,128]{1,0:T(8,128)(2,1)S(1)} %get-tuple-element.43.ac_ref.bc_ref.refs_0_, bf16[2048,384]{1,0:T(8,128)(2,1)S(1)} %copy-done, ...), custom_call_target="tpu_custom_call" | custom-call | flops 1 | bytes 1 | tf_op jit(solution)/shard_map/branch_near/pallas_call | solution.py:372
  199.3 8.8 %all-gather.4.cloned.1.call-done.refs_0_.refs_2_ = bf16[2048,2048]{1,0:T(8,128)(2,1)} async-done(((bf16[128,2048]{1,0:T(8,128)(2,1)}), bf16[2048,2048]{1,0:T(8,128)(2,1)}) %all-gather.4.cloned.1.call-update) | async-done | bytes 8388624 | tf_op jit(solution)/shard_map/all_gather | solution.py:636
  209.8 11.4 %gate_back.1 = (bf16[2048,768]{1,0:T(8,128)(2,1)}, bf16[2048,128]{1,0:T(8,128)(2,1)S(1)}) custom-call(bf16[2048,2048]{1,0:T(8,128)(2,1)} %all-gather.4.cloned.1.call-done.refs_0_.refs_2_, f32[2048,384]{1,0:T(8,128)} %get-tuple-element.40.refs_1_, f32[2048,384]{1,0:T(8,128)} %get-tuple-element.41.refs_2_, bf16[512,2048]{1,0:T(8,128)(2,1)S(1)} %copy-done.2, ...), custom_call_target="tpu_custom_call" | custom-call | flops 1 | bytes 1 | tf_op jit(solution)/shard_map/gate_back/pallas_call | solution.py:409
  222.0 11.2 %grads.2 = (f32[16,64,768]{2,1,0:T(8,128)}, bf16[16,64,768]{2,1,0:T(8,128)(2,1)}) custom-call(s32[1]{0:T(128)} %bitcast.12.part_ref.refs_0_, bf16[2048,2048]{1,0:T(8,128)(2,1)} %get-tuple-element.50.refs_1_, bf16[2048,768]{1,0:T(8,128)(2,1)} %get-tuple-element.46.refs_2_.refs_5_.refs_6_), custom_call_target="tpu_custom_call" | custom-call | flops 1 | bytes 1 | tf_op jit(solution)/shard_map/grads/pallas_call | solution.py:438
  235.3 8.2 %attend_back.1 = (bf16[2048,384]{1,0:T(8,128)(2,1)}, f32[1,384]{1,0:T(1,128)}) custom-call(bf16[2048,384]{1,0:T(8,128)(2,1)} %copy-done.13, f32[16,256,128]{2,1,0:T(8,128)} %copy-done.11, bf16[2048,128]{1,0:T(8,128)(2,1)} %copy-done.14, f32[2048,128]{1,0:T(8,128)} %get-tuple-element.88.refs_1_.own_ref.refs_3_, ...), custom_call_target="tpu_custom_call" | custom-call | flops 536870912 | bytes 12288000 | tf_op jit(solution)/shard_map/attend_back/pallas_call | solution.py:164
  243.5 2.4 collective-permute-done.3.refs_12_
  247.2 14.2 %dn_far.1 = (bf16[256,2048]{1,0:T(8,128)(2,1)}, bf16[256,2048]{1,0:T(8,128)(2,1)}, bf16[256,2048]{1,0:T(8,128)(2,1)}, bf16[256,2048]{1,0:T(8,128)(2,1)}, bf16[512,2048]{1,0:T(8,128)(2,1)}, /*index=5*/f32[8,2048]{1,0:T(8,128)}) custom-call(s32[8]{0:T(128)} %stack.116.refs_0_, bf16[16,136,2048]{2,1,0:T(8,128)(2,1)} %bitcast.79, ...), custom_call_target="tpu_custom_call" | custom-call | flops 1 | bytes 1 | tf_op jit(solution)/shard_map/dn_far/pallas_call | solution.py:532
  263.5 12.5 %dn_near.1 = (f32[1024,2048]{1,0:T(8,128)}, f32[8,2048]{1,0:T(8,128)}) custom-call(s32[8]{0:T(128)} %stack.143.refs_0_, bf16[16,136,2048]{2,1,0:T(8,128)(2,1)} %bitcast.81, bf16[16,136,2048]{2,1,0:T(8,128)(2,1)} %bitcast.82, f32[2048,128]{1,0:T(8,128)} %get-tuple-element.39.refs_3_.refs_4_, f32[2048,128]{1,0:T(8,128)} %get-tuple-element.39.refs_3_.refs_4_, ...), custom_call_target="tpu_custom_call" | custom-call | flops 1 | bytes 1 | tf_op jit(solution)/shard_map/dn_near/pallas_call | solution.py:532
  278.7 6.4 %combine.1 = (bf16[256,2048]{1,0:T(8,128)(2,1)}, bf16[256,2048]{1,0:T(8,128)(2,1)S(1)}, f32[512,2048]{1,0:T(8,128)}) custom-call(f32[1024,2048]{1,0:T(8,128)} %get-tuple-element.59.refs_0_, bf16[256,2048]{1,0:T(8,128)(2,1)S(1)} %collective-permute-done.4.refs_1_, bf16[256,2048]{1,0:T(8,128)(2,1)S(1)} %collective-permute-done.5.refs_2_, ...), custom_call_target="tpu_custom_call" | custom-call | flops 1 | bytes 1 | tf_op jit(solution)/shard_map/combine/pallas_call | solution.py:581
  287.6 1.9 copy-done.18
  289.5 3.4 add_convert_fusion.refs_3_
  292.9 4.7 %all-to-all-start.2 = ((bf16[16,64,768]{2,1,0:T(8,128)(2,1)}), bf16[16,64,768]{2,1,0:T(8,128)(2,1)}, u32[]{:S(2)}, u32[]{:S(2)}) async-start(bf16[16,64,768]{2,1,0:T(8,128)(2,1)} %add_convert_fusion.refs_3_), calls=%async_computation.3 | async-start | bytes 3145728 | tf_op jit(solution)/shard_map/all_to_all | solution.py:716
  297.6 8.8 %grads.3 = (f32[16,64,384]{2,1,0:T(8,128)}, bf16[16,64,384]{2,1,0:T(8,128)(2,1)}) custom-call(s32[1]{0:T(128)} %bitcast.12.part_ref.refs_0_, bf16[2048,2048]{1,0:T(8,128)(2,1)} %get-tuple-element.50.refs_1_, bf16[2048,384]{1,0:T(8,128)(2,1)} %get-tuple-element.52.refs_7_.refs_8_.refs_2_, bf16[16,64,768]{2,1,0:T(8,128)(2,1)} %add_convert_fusion.refs_3_), custom_call_target="tpu_custom_call" | custom-call | flops 1 | bytes 1 | tf_op jit(solution)/shard_map/grads/pallas_call | solution.py:438
  307.6 8.8 %rows.1.refs_3_ = bf16[480,2048]{1,0:T(8,128)(2,1)} custom-call(bf16[2048,128]{1,0:T(8,128)(2,1)} %copy-done.6, bf16[2048,384]{1,0:T(8,128)(2,1)} %get-tuple-element.44.ah_ref.bh_ref.refs_1_, bf16[2048,2048]{1,0:T(8,128)(2,1)} %all-gather.4.cloned.1.call-done.refs_0_.refs_2_, bf16[16,64,384]{2,1,0:T(8,128)(2,1)} %get-tuple-element.67.refs_3_), custom_call_target="tpu_custom_call" | custom-call | flops 1 | bytes 1 | tf_op jit(solution)/shard_map/rows/pallas_call | solution.py:467
  317.6 2.5 add_convert_fusion.3
  320.1 1.7 collective-permute-start.12
  322.3 4.6 %collective-permute-done.15 = bf16[16,64,384]{2,1,0:T(8,128)(2,1)S(1)} collective-permute-done((bf16[16,64,384]{2,1,0:T(8,128)(2,1)}, bf16[16,64,384]{2,1,0:T(8,128)(2,1)S(1)}, u32[]{:S(2)}, u32[]{:S(2)}) %collective-permute-start.15) | collective-permute-done | bytes 786464 | tf_op jit(solution)/shard_map/ppermute | solution.py:185
  328.0 3.7 collective-permute-start.10
  331.8 19.1 %collective-permute-done.12 = bf16[256,2048]{1,0:T(8,128)(2,1)} collective-permute-done((bf16[256,2048]{1,0:T(8,128)(2,1)}, bf16[256,2048]{1,0:T(8,128)(2,1)}, u32[]{:S(2)}, u32[]{:S(2)}) %collective-permute-start.12) | collective-permute-done | bytes 1048608 | tf_op jit(solution)/shard_map/ppermute | solution.py:185
  350.9 2.3 add_convert_fusion.2
  353.1 2.5 collective-permute-start.13
  357.1 10.3 %all-to-all-start.3 = ((bf16[16,64,384]{2,1,0:T(8,128)(2,1)}), bf16[16,64,384]{2,1,0:T(8,128)(2,1)S(1)}, u32[]{:S(2)}, u32[]{:S(2)}) async-start(bf16[16,64,384]{2,1,0:T(8,128)(2,1)} %after.7), calls=%async_computation.4 | async-start | bytes 1572864 | tf_op jit(solution)/shard_map/all_to_all | solution.py:745
  367.4 1.8 collective-permute-done.17
  369.1 2.9 convert_add_fusion
  372.0 1.9 slice.164
  375.0 18.4 %collective-permute-done.9 = bf16[128,2048]{1,0:T(8,128)(2,1)} collective-permute-done((bf16[128,2048]{1,0:T(8,128)(2,1)S(1)}, bf16[128,2048]{1,0:T(8,128)(2,1)}, u32[]{:S(2)}, u32[]{:S(2)}) %collective-permute-start.9) | collective-permute-done | bytes 524320 | tf_op jit(solution)/shard_map/ppermute | solution.py:185
  393.3 2.5 fusion.31
  402.2 1.9 convert_add_fusion.2
  404.1 6.1 %unpack.3 = f32[128,11264]{1,0:T(8,128)} custom-call(s32[1]{0:T(128)} %bitcast.12.part_ref.refs_0_, bf16[16,64,768]{2,1,0:T(8,128)(2,1)} %all-to-all-done.2.refs_1_.own_ref, bf16[16,64,768]{2,1,0:T(8,128)(2,1)S(1)} %collective-permute-done.14.other_ref), custom_call_target="tpu_custom_call" | custom-call | flops 1 | bytes 1 | tf_op jit(solution)/shard_map/unpack/pallas_call | solution.py:266
  413.2 5.8 %collective-permute-done.16.other_ref = bf16[16,64,384]{2,1,0:T(8,128)(2,1)S(1)} collective-permute-done((bf16[16,64,384]{2,1,0:T(8,128)(2,1)S(1)}, bf16[16,64,384]{2,1,0:T(8,128)(2,1)S(1)}, u32[]{:S(2)}, u32[]{:S(2)}) %collective-permute-start.16) | collective-permute-done | bytes 786464 | tf_op jit(solution)/shard_map/ppermute | solution.py:185
  419.0 3.4 unpack.2
  (164 shorter events, 54.0 us)
Async XLA Ops:
  7.2 125.0 %all-gather.6.cloned.1.call-start = ((), (), s32[]{:S(2)}) async-start(), calls=%async_computation.7 | async-start | bytes 9469952 | tf_op jit(solution)/shard_map/all_gather | solution.py:634
  10.5 197.6 %all-gather.4.cloned.1.call-start = ((), (), s32[]{:S(2)}) async-start(), calls=%async_computation.5 | async-start | bytes 8912896 | tf_op jit(solution)/shard_map/all_gather | solution.py:636
  11.3 1.8 copy-start.10
  15.1 7.6 %copy-start.12 = (bf16[128,6144]{1,0:T(8,128)(2,1)S(1)}, bf16[128,6144]{1,0:T(8,128)(2,1)}, u32[]{:S(2)}) copy-start(bf16[128,6144]{1,0:T(8,128)(2,1)} %own_ref.3) | copy-start | bytes 4718596
  15.1 57.0 %all-to-all-start = ((bf16[16,64,768]{2,1,0:T(8,128)(2,1)}), bf16[16,64,768]{2,1,0:T(8,128)(2,1)}, u32[]{:S(2)}, u32[]{:S(2)}) async-start(bf16[16,64,768]{2,1,0:T(8,128)(2,1)} %pack.2), calls=%async_computation | async-start | bytes 3145728 | tf_op jit(solution)/shard_map/all_to_all | solution.py:654
  22.7 63.2 %copy-start.24 = (bf16[352,2048]{1,0:T(8,128)(2,1)S(1)}, bf16[352,2048]{1,0:T(8,128)(2,1)}, u32[]{:S(2)}) copy-start(bf16[352,2048]{1,0:T(8,128)(2,1)} %param.18) | copy-start | bytes 4325380
  22.7 63.2 %copy-start.26 = (bf16[128,2048]{1,0:T(8,128)(2,1)S(1)}, bf16[128,2048]{1,0:T(8,128)(2,1)}, u32[]{:S(2)}) copy-start(bf16[128,2048]{1,0:T(8,128)(2,1)} %param.16) | copy-start | bytes 1572868
  72.1 41.8 %all-to-all-start.1 = ((bf16[16,64,384]{2,1,0:T(8,128)(2,1)}), bf16[16,64,384]{2,1,0:T(8,128)(2,1)}, u32[]{:S(2)}, u32[]{:S(2)}) async-start(bf16[16,64,384]{2,1,0:T(8,128)(2,1)} %pack.3), calls=%async_computation.1 | async-start | bytes 1572864 | tf_op jit(solution)/shard_map/all_to_all | solution.py:654
  82.2 274.8 %reduce-scatter.2.cloned.1.call-start = ((), (), s32[]{:S(2)}) async-start(), calls=%async_computation.6 | async-start | bytes 2621440 | tf_op jit(solution)/shard_map/reduce_scatter | solution.py:699
  82.3 38.7 %collective-permute-start = (bf16[16,64,768]{2,1,0:T(8,128)(2,1)}, bf16[16,64,768]{2,1,0:T(8,128)(2,1)}, u32[]{:S(2)}, u32[]{:S(2)}) collective-permute-start(bf16[16,64,768]{2,1,0:T(8,128)(2,1)} %all-to-all-done), channel_id=1, source_target_pairs={{0,16},{16,0},{1,17},{17,1},{2,18},{18,2},{3,19},{19,3},{4,20},{20... | collective-permute-start | bytes 4718600 | tf_op jit(solution)/shard_map/ppermute | solution.py:185
  113.9 29.0 %collective-permute-start.1 = (bf16[16,64,384]{2,1,0:T(8,128)(2,1)}, bf16[16,64,384]{2,1,0:T(8,128)(2,1)}, u32[]{:S(2)}, u32[]{:S(2)}) collective-permute-start(bf16[16,64,384]{2,1,0:T(8,128)(2,1)} %all-to-all-done.1), channel_id=1, source_target_pairs={{0,16},{16,0},{1,17},{17,1},{2,18},{18,2},{3,19},{19,3},{4,20},{20... | collective-permute-start | bytes 2359304 | tf_op jit(solution)/shard_map/ppermute | solution.py:185
  122.6 20.3 %copy-start.15 = (bf16[16,2,64,768]{3,2,1,0:T(8,128)(2,1)}, bf16[16,2,64,768]{3,2,1,0:T(8,128)(2,1)S(1)}, u32[]{:S(2)}) copy-start(bf16[16,2,64,768]{3,2,1,0:T(8,128)(2,1)S(1)} %bitcast_dynamic-update-slice_fusion) | copy-start | bytes 9437188
  122.6 14.3 %copy-start.28 = (pred[128]{0:T(512)(128)(4,1)S(1)}, pred[128]{0:T(512)(128)(4,1)}, u32[]{:S(2)}) copy-start(pred[128]{0:T(512)(128)(4,1)} %broadcast_compare_fusion.1) | copy-start | bytes 388
  122.6 14.3 %copy-start.29 = (f32[128]{0:T(128)S(1)}, f32[128]{0:T(128)}, u32[]{:S(2)}) copy-start(f32[128]{0:T(128)} %fusion.29) | copy-start | bytes 1540
  122.6 14.3 %copy-start.30 = (pred[128]{0:T(512)(128)(4,1)S(1)}, pred[128]{0:T(512)(128)(4,1)}, u32[]{:S(2)}) copy-start(pred[128]{0:T(512)(128)(4,1)} %get-tuple-element.91) | copy-start | bytes 388
  122.7 14.3 %copy-start.31 = (pred[128]{0:T(512)(128)(4,1)S(1)}, pred[128]{0:T(512)(128)(4,1)}, u32[]{:S(2)}) copy-start(pred[128]{0:T(512)(128)(4,1)} %get-tuple-element.92) | copy-start | bytes 388
  145.1 21.7 %copy-start.3 = (f32[2048,128]{1,0:T(8,128)S(1)}, f32[2048,128]{1,0:T(8,128)}, u32[]{:S(2)}) copy-start(f32[2048,128]{1,0:T(8,128)} %get-tuple-element.86.refs_3_.before_ref.refs_5_) | copy-start | bytes 3145732
  170.7 1.9 copy-start.9
  172.6 3.4 copy-start
  172.6 3.4 copy-start.1
  175.9 5.5 %copy-start.11 = (f32[16,256,128]{2,1,0:T(8,128)}, f32[16,256,128]{2,1,0:T(8,128)S(1)}, u32[]{:S(2)}) copy-start(f32[16,256,128]{2,1,0:T(8,128)S(1)} %get-tuple-element.48.refs_1_) | copy-start | bytes 6291460
  176.0 5.5 %copy-start.13 = (bf16[2048,384]{1,0:T(8,128)(2,1)}, bf16[2048,384]{1,0:T(8,128)(2,1)S(1)}, u32[]{:S(2)}) copy-start(bf16[2048,384]{1,0:T(8,128)(2,1)S(1)} %get-tuple-element.47.refs_0_) | copy-start | bytes 4718596
  176.0 13.0 %copy-start.6 = (bf16[2048,128]{1,0:T(8,128)(2,1)}, bf16[2048,128]{1,0:T(8,128)(2,1)S(1)}, u32[]{:S(2)}) copy-start(bf16[2048,128]{1,0:T(8,128)(2,1)S(1)} %get-tuple-element.43.ac_ref.bc_ref.refs_0_) | copy-start | bytes 1572868
  181.5 7.5 %collective-permute-start.2 = (bf16[1024,2048]{1,0:T(8,128)(2,1)}, bf16[1024,2048]{1,0:T(8,128)(2,1)}, u32[]{:S(2)}, u32[]{:S(2)}) collective-permute-start(bf16[1024,2048]{1,0:T(8,128)(2,1)} %branch_far.1), channel_id=1, source_target_pairs={{0,1},{1,0},{2,3},{3,2},{4,5},{5,4},{6,7},{7,6},{8,9},{9,8},{10,11... | collective-permute-start | bytes 12582920 | tf_op jit(solution)/shard_map/ppermute | solution.py:185
  197.9 48.0 %collective-permute-start.3 = (bf16[512,2048]{1,0:T(8,128)(2,1)}, bf16[512,2048]{1,0:T(8,128)(2,1)S(1)}, u32[]{:S(2)}, u32[]{:S(2)}) collective-permute-start(bf16[512,2048]{1,0:T(8,128)(2,1)} %get-tuple-element.45.refs_4_), channel_id=1, source_target_pairs={{0,2},{2,0},{1,3},{3,1},{4,6},{6,4},{5,7},{7,5},{8,10},{10,8},{9,1... | collective-permute-start | bytes 6291464 | tf_op jit(solution)/shard_map/ppermute | solution.py:185
  233.1 54.4 %collective-permute-start.11 = (bf16[16,64,768]{2,1,0:T(8,128)(2,1)}, bf16[16,64,768]{2,1,0:T(8,128)(2,1)}, u32[]{:S(2)}, u32[]{:S(2)}) collective-permute-start(bf16[16,64,768]{2,1,0:T(8,128)(2,1)} %get-tuple-element.51.refs_6_), channel_id=1, source_target_pairs={{0,16},{16,0},{1,17},{17,1},{2,18},{18,2},{3,19},{19,3},{4,20},{20... | collective-permute-start | bytes 4718600 | tf_op jit(solution)/shard_map/ppermute | solution.py:185
  261.4 1.9 copy-start.27
  261.5 17.2 %collective-permute-start.4 = (bf16[256,2048]{1,0:T(8,128)(2,1)}, bf16[256,2048]{1,0:T(8,128)(2,1)S(1)}, u32[]{:S(2)}, u32[]{:S(2)}) collective-permute-start(bf16[256,2048]{1,0:T(8,128)(2,1)} %get-tuple-element.55.refs_11_), channel_id=1, source_target_pairs={{0,1},{1,0},{2,3},{3,2},{4,5},{5,4},{6,7},{7,6},{8,9},{9,8},{10,11... | collective-permute-start | bytes 3145736 | tf_op jit(solution)/shard_map/ppermute | solution.py:185
  261.5 17.1 %collective-permute-start.5 = (bf16[256,2048]{1,0:T(8,128)(2,1)}, bf16[256,2048]{1,0:T(8,128)(2,1)S(1)}, u32[]{:S(2)}, u32[]{:S(2)}) collective-permute-start(bf16[256,2048]{1,0:T(8,128)(2,1)} %get-tuple-element.56.refs_12_), channel_id=1, source_target_pairs={{0,1},{1,0},{2,3},{3,2},{4,5},{5,4},{6,7},{7,6},{8,9},{9,8},{10,11... | collective-permute-start | bytes 3145736 | tf_op jit(solution)/shard_map/ppermute | solution.py:185
  262.0 16.6 %collective-permute-start.6 = (bf16[256,2048]{1,0:T(8,128)(2,1)}, bf16[256,2048]{1,0:T(8,128)(2,1)S(1)}, u32[]{:S(2)}, u32[]{:S(2)}) collective-permute-start(bf16[256,2048]{1,0:T(8,128)(2,1)} %get-tuple-element.57.refs_13_), channel_id=1, source_target_pairs={{0,1},{1,0},{2,3},{3,2},{4,5},{5,4},{6,7},{7,6},{8,9},{9,8},{10,11... | collective-permute-start | bytes 3145736 | tf_op jit(solution)/shard_map/ppermute | solution.py:185
  262.1 16.6 %collective-permute-start.7 = (bf16[256,2048]{1,0:T(8,128)(2,1)}, bf16[256,2048]{1,0:T(8,128)(2,1)}, u32[]{:S(2)}, u32[]{:S(2)}) collective-permute-start(bf16[256,2048]{1,0:T(8,128)(2,1)} %get-tuple-element.58.refs_14_), channel_id=1, source_target_pairs={{0,1},{1,0},{2,3},{3,2},{4,5},{5,4},{6,7},{7,6},{8,9},{9,8},{10,11... | collective-permute-start | bytes 3145736 | tf_op jit(solution)/shard_map/ppermute | solution.py:185
  286.1 31.5 %collective-permute-start.8 = (bf16[256,2048]{1,0:T(8,128)(2,1)}, bf16[256,2048]{1,0:T(8,128)(2,1)}, u32[]{:S(2)}, u32[]{:S(2)}) collective-permute-start(bf16[256,2048]{1,0:T(8,128)(2,1)} %get-tuple-element.61.refs_1_), channel_id=1, source_target_pairs={{0,2},{2,0},{1,3},{3,1},{4,6},{6,4},{5,7},{7,5},{8,10},{10,8},{9,1... | collective-permute-start | bytes 3145736 | tf_op jit(solution)/shard_map/ppermute | solution.py:185
  287.6 1.9 copy-start.18
  292.9 62.7 %all-to-all-start.2 = ((bf16[16,64,768]{2,1,0:T(8,128)(2,1)}), bf16[16,64,768]{2,1,0:T(8,128)(2,1)}, u32[]{:S(2)}, u32[]{:S(2)}) async-start(bf16[16,64,768]{2,1,0:T(8,128)(2,1)} %add_convert_fusion.refs_3_), calls=%async_computation.3 | async-start | bytes 3145728 | tf_op jit(solution)/shard_map/all_to_all | solution.py:716
  306.3 11.3 %copy-start.17 = (f32[512,2048]{1,0:T(8,128)S(1)}, f32[512,2048]{1,0:T(8,128)}, u32[]{:S(2)}) copy-start(f32[512,2048]{1,0:T(8,128)} %get-tuple-element.60) | copy-start | bytes 12582916
  306.3 20.6 %collective-permute-start.15 = (bf16[16,64,384]{2,1,0:T(8,128)(2,1)}, bf16[16,64,384]{2,1,0:T(8,128)(2,1)S(1)}, u32[]{:S(2)}, u32[]{:S(2)}) collective-permute-start(bf16[16,64,384]{2,1,0:T(8,128)(2,1)} %get-tuple-element.67.refs_3_), channel_id=1, source_target_pairs={{0,16},{16,0},{1,17},{17,1},{2,18},{18,2},{3,19},{19,3},{4,20},{20... | collective-permute-start | bytes 2359304 | tf_op jit(solution)/shard_map/ppermute | solution.py:185
  316.4 52.8 %collective-permute-start.17 = (bf16[480,2048]{1,0:T(8,128)(2,1)}, bf16[480,2048]{1,0:T(8,128)(2,1)}, u32[]{:S(2)}, u32[]{:S(2)}) collective-permute-start(bf16[480,2048]{1,0:T(8,128)(2,1)} %rows.1.refs_3_), channel_id=1, source_target_pairs={{0,16},{16,0},{1,17},{17,1},{2,18},{18,2},{3,19},{19,3},{4,20},{20... | collective-permute-start | bytes 5898248 | tf_op jit(solution)/shard_map/ppermute | solution.py:185
  320.1 6.8 %copy-start.23 = (f32[16,64,384]{2,1,0:T(8,128)S(1)}, f32[16,64,384]{2,1,0:T(8,128)}, u32[]{:S(2)}) copy-start(f32[16,64,384]{2,1,0:T(8,128)} %get-tuple-element.68) | copy-start | bytes 4718596
  320.1 30.8 %collective-permute-start.12 = (bf16[256,2048]{1,0:T(8,128)(2,1)}, bf16[256,2048]{1,0:T(8,128)(2,1)}, u32[]{:S(2)}, u32[]{:S(2)}) collective-permute-start(bf16[256,2048]{1,0:T(8,128)(2,1)} %after.6), channel_id=1, source_target_pairs={{0,2},{2,0},{1,3},{3,1},{4,6},{6,4},{5,7},{7,5},{8,10},{10,8},{9,1... | collective-permute-start | bytes 3145736 | tf_op jit(solution)/shard_map/ppermute | solution.py:185
  321.8 9.8 %copy-start.21 = (bf16[128,2048]{1,0:T(8,128)(2,1)S(1)}, bf16[128,2048]{1,0:T(8,128)(2,1)}, u32[]{:S(2)}) copy-start(bf16[128,2048]{1,0:T(8,128)(2,1)} %get-tuple-element.75.refs_1_) | copy-start | bytes 1572868
  328.0 47.0 %collective-permute-start.10 = (bf16[128,2048]{1,0:T(8,128)(2,1)}, bf16[128,2048]{1,0:T(8,128)(2,1)}, u32[]{:S(2)}, u32[]{:S(2)}) collective-permute-start(bf16[128,2048]{1,0:T(8,128)(2,1)} %get-tuple-element.74.refs_2_), channel_id=1, source_target_pairs={{0,12},{4,0},{8,4},{12,8},{1,13},{5,1},{9,5},{13,9},{2,14},{6,2},{... | collective-permute-start | bytes 1572872 | tf_op jit(solution)/shard_map/ppermute | solution.py:185
  331.6 61.7 %collective-permute-start.9 = (bf16[128,2048]{1,0:T(8,128)(2,1)S(1)}, bf16[128,2048]{1,0:T(8,128)(2,1)}, u32[]{:S(2)}, u32[]{:S(2)}) collective-permute-start(bf16[128,2048]{1,0:T(8,128)(2,1)S(1)} %copy-done.21), channel_id=1, source_target_pairs={{0,8},{4,12},{8,0},{12,4},{1,9},{5,13},{9,1},{13,5},{2,10},{6,14},... | collective-permute-start | bytes 1572872 | tf_op jit(solution)/shard_map/ppermute | solution.py:185
  353.1 40.2 %collective-permute-start.13 = (bf16[128,2048]{1,0:T(8,128)(2,1)}, bf16[128,2048]{1,0:T(8,128)(2,1)}, u32[]{:S(2)}, u32[]{:S(2)}) collective-permute-start(bf16[128,2048]{1,0:T(8,128)(2,1)} %add_convert_fusion.2), channel_id=1, source_target_pairs={{0,4},{4,8},{8,12},{12,0},{1,5},{5,9},{9,13},{13,1},{2,6},{6,10},{... | collective-permute-start | bytes 1572872 | tf_op jit(solution)/shard_map/ppermute | solution.py:185
  355.6 46.5 %collective-permute-start.14 = (bf16[16,64,768]{2,1,0:T(8,128)(2,1)}, bf16[16,64,768]{2,1,0:T(8,128)(2,1)S(1)}, u32[]{:S(2)}, u32[]{:S(2)}) collective-permute-start(bf16[16,64,768]{2,1,0:T(8,128)(2,1)} %all-to-all-done.2.refs_1_.own_ref), channel_id=1, source_target_pairs={{0,16},{16,0},{1,17},{17,1},{2,18},{18,2},{3,19},{19,3},{4,20},{20... | collective-permute-start | bytes 4718600 | tf_op jit(solution)/shard_map/ppermute | solution.py:185
  357.1 42.4 %all-to-all-start.3 = ((bf16[16,64,384]{2,1,0:T(8,128)(2,1)}), bf16[16,64,384]{2,1,0:T(8,128)(2,1)S(1)}, u32[]{:S(2)}, u32[]{:S(2)}) async-start(bf16[16,64,384]{2,1,0:T(8,128)(2,1)} %after.7), calls=%async_computation.4 | async-start | bytes 1572864 | tf_op jit(solution)/shard_map/all_to_all | solution.py:745
  393.3 3.7 copy-start.19
  393.3 3.7 copy-start.20
  399.4 19.6 %collective-permute-start.16 = (bf16[16,64,384]{2,1,0:T(8,128)(2,1)S(1)}, bf16[16,64,384]{2,1,0:T(8,128)(2,1)S(1)}, u32[]{:S(2)}, u32[]{:S(2)}) collective-permute-start(bf16[16,64,384]{2,1,0:T(8,128)(2,1)S(1)} %all-to-all-done.3.own_ref), channel_id=1, source_target_pairs={{0,16},{16,0},{1,17},{17,1},{2,18},{18,2},{3,19},{19,3},{4,20},{20... | collective-permute-start | bytes 2359304 | tf_op jit(solution)/shard_map/ppermute | solution.py:185
  (9 other events, 11.3 us)
Sparse Core Ops, SparseCore 0:
  10.9 121.2 all-gather.5
  134.3 73.7 all-gather.3
  262.7 50.3 reduce-scatter.1
